TPU v7x, 32 devices: a whole 2x2x4 slice. The times are simulated.
32 devices in a mesh: groups: 2 (over y), row: 4 (over z), col: 2 (over x), claim: 2 (over core).
Axes of the slice: x: 2, y: 2, z: 4, core: 2. Of those that a mesh axis runs over, the one named last changes fastest.
Arguments:
- claim_cell: int32 [32, 8, 192], P(('groups', 'row', 'col', 'claim')), parts along dimension 0, may hold values from 0 to 262143
- claim_weight: float32 [32, 8, 192], P(('groups', 'row', 'col', 'claim')), parts along dimension 0, may hold values from 0.1 to 10
- claim_count: int32 [32, 8], P(('groups', 'row', 'col', 'claim')), parts along dimension 0, may hold values from 0 to 192, as said below
- baseline: float32 [2048, 2048], P(('groups', 'row', 'claim'), 'col'), parts along dimension 0, may hold values from 0.05 to 0.3
- half_widths: int32 [16], replicated, may hold values from 0 to 64, as said below
Outputs:
- ratio_fields: float32 [16, 2048, 2048], P(None, ('groups', 'row', 'claim'), 'col'), parts along dimension 1
There are 2 independent parts, one for each index of `groups`. A program takes and returns all parts, laid end to end along the dimension named above; an argument that names none is the same for every part. Nothing has to cross between parts.
Inputs may be any that keep to these rules, and one draw needn't show every extreme that they name: `claim_count`: live slots of one sender to one tile come first; for one tile drawn from the seed every sender fills all 192 slots. `half_widths`: distinct values; one equals 64.
All inputs are finite; a program needn't handle non-finite values.
Results may differ from a plain program's by a relative error of at most 0.0003.
Values sent between devices are 32-bit elements; how exact they have to be, the bound alone decides.
No kernel may reach another device: no remote copies, remote signals or barrier semaphores. Data moves between devices by JAX's collectives and lax.ppermute only.
A program may use at most 64 MiB of HBM per device.

v0:
```python
import jax
import jax.numpy as jnp
from jax import lax
from jax.sharding import PartitionSpec as P

HALO = 64


sources_per_block = 4


def padded_2(cells, sides, width):
    for axis, dim in sides:
        count = lax.axis_size(axis)
        ends = count - 1
        head = lax.slice_in_dim(cells, 0, width, axis=dim)
        tail = lax.slice_in_dim(cells, cells.shape[dim] - width, cells.shape[dim], axis=dim)
        cells = jnp.concatenate(
            [
                lax.ppermute(tail, axis, [(i, (i + 1) % count) for i in range(ends)]),
                cells,
                lax.ppermute(head, axis, [((i + 1) % count, i) for i in range(ends)]),
            ],
            axis=dim,
        )
    return cells


def poisson_ratio(box_counts, box_base, side):
    positive = box_counts > 0
    safe_counts = jnp.where(positive, box_counts, 1.0)
    entropy = jnp.where(positive, box_counts * jnp.log(safe_counts / box_base), 0.0)
    return (entropy + box_base - box_counts) / side


def prefix_fields(padded, half_widths):
    block_rows = padded.shape[1] - 2 * HALO
    block_cols = padded.shape[2] - 2 * HALO
    zero_row = jnp.zeros_like(padded[:, :1, :])
    row_prefix = jnp.cumsum(jnp.concatenate([zero_row, padded], axis=1), axis=1)

    def one_size(half):
        upper = lax.dynamic_slice_in_dim(row_prefix, HALO + 1 + half, block_rows, 1)
        lower = lax.dynamic_slice_in_dim(row_prefix, HALO - half, block_rows, 1)
        row_boxes = upper - lower
        zero_col = jnp.zeros_like(row_boxes[:, :, :1])
        col_prefix = jnp.cumsum(jnp.concatenate([zero_col, row_boxes], axis=2), axis=2)
        right = lax.dynamic_slice_in_dim(col_prefix, HALO + 1 + half, block_cols, 2)
        left = lax.dynamic_slice_in_dim(col_prefix, HALO - half, block_cols, 2)
        boxed = right - left
        return poisson_ratio(boxed[0], boxed[1], (2 * half + 1).astype(jnp.float32))

    return lax.map(one_size, half_widths)


def bin_rows(grouped_cells, grouped_weights, first_row, row_count, block_cols):
    group_width = grouped_cells.shape[1]
    row_iota = lax.broadcasted_iota(jnp.int32, (row_count, group_width), 0)
    col_iota = lax.broadcasted_iota(jnp.int32, (group_width, block_cols), 1)

    def add_group(total, group):
        group_cells, group_weights = group
        local_row = group_cells // block_cols - first_row
        local_col = group_cells % block_cols
        row_onehot = jnp.where(
            local_row[None, :] == row_iota, group_weights[None, :], jnp.zeros((), jnp.float32)
        )
        col_onehot = (local_col[:, None] == col_iota).astype(jnp.float32)
        product = jnp.dot(
            row_onehot,
            col_onehot,
            precision=lax.Precision.HIGHEST,
            preferred_element_type=jnp.float32,
        )
        return (total + product, None)

    initial = jnp.zeros((row_count, block_cols), jnp.float32)
    total, _ = lax.scan(add_group, initial, (grouped_cells, grouped_weights))
    return total


def shards(claim_cell, claim_weight, claim_count, baseline, half_widths):
    block_rows, block_cols = baseline.shape
    slot_index = lax.broadcasted_iota(jnp.int32, claim_cell.shape, 2)
    live_weight = jnp.where(
        slot_index < claim_count[:, :, None], claim_weight, jnp.zeros((), jnp.float32)
    )
    got_cells, got_weights = (
        lax.all_to_all(claim_cell, ("row", "col"), split_axis=1, concat_axis=0, tiled=True),
        lax.all_to_all(live_weight, ("row", "col"), split_axis=1, concat_axis=0, tiled=True),
    )
    group_width = sources_per_block * got_cells.shape[2]
    grouped_cells = got_cells.reshape(-1, group_width)
    grouped_weights = got_weights.reshape(-1, group_width)
    binned = lax.psum_scatter(
        bin_rows(
            grouped_cells,
            grouped_weights,
            jnp.int32(0),
            block_rows * lax.axis_size("claim"),
            block_cols,
        ),
        "claim",
        scatter_dimension=0,
        tiled=True,
    )
    padded = padded_2(jnp.stack([binned, baseline]), ((("row", "claim"), 1), ("col", 2)), HALO)
    return prefix_fields(padded, half_widths)


def solution(mesh):
    in_specs = (
        P(("groups", "row", "col", "claim"), None, None),
        P(("groups", "row", "col", "claim"), None, None),
        P(("groups", "row", "col", "claim"), None),
        P(("groups", "row", "claim"), "col"),
        P(),
    )
    out_specs = P(None, ("groups", "row", "claim"), "col")
    return jax.shard_map(shards, mesh=mesh, in_specs=in_specs, out_specs=out_specs, check_vma=False)
```

profile of v0, /device:TPU:9, one launch (start us, length us, event | category | flops | bytes accessed | tf_op | source)
XLA Modules:
  0.0 297.5 jit_solution(10227519792455508682)
XLA Ops:
  6.5 1.3 copy.24
  7.8 5.7 %all-to-all-start = ((s32[1,8,192]{2,0,1:T(1,128)}), s32[1,8,192]{2,0,1:T(1,128)S(1)}, u32[]{:S(2)}, u32[]{:S(2)}) async-start(s32[1,8,192]{2,0,1:T(1,128)} %copy.24), calls=%async_computation | async-start | bytes 16384 | tf_op jit(solution)/shard_map/all_to_all | solution.py:89
  13.5 1.4 compare_select_fusion.5
  14.9 2.8 all-to-all-done
  17.7 4.5 %all-to-all-start.1 = ((f32[1,8,192]{2,0,1:T(1,128)}), f32[1,8,192]{2,0,1:T(1,128)S(1)}, u32[]{:S(2)}, u32[]{:S(2)}) async-start(f32[1,8,192]{2,0,1:T(1,128)} %compare_select_fusion.5), calls=%async_computation.1 | async-start | bytes 16384 | tf_op jit(solution)/shard_map/all_to_all | solution.py:90
  22.3 4.1 %all-to-all-done.1 = f32[1,8,192]{2,0,1:T(1,128)S(1)} async-done(((f32[1,8,192]{2,0,1:T(1,128)}), f32[1,8,192]{2,0,1:T(1,128)S(1)}, u32[]{:S(2)}, u32[]{:S(2)}) %all-to-all-start.1) | async-done | bytes 6176 | tf_op jit(solution)/shard_map/all_to_all | solution.py:90
  26.4 4.6 %while.26 = (s32[]{:T(128)}, f32[256,1024]{1,0:T(8,128)S(1)}, s32[2,768]{1,0:T(2,128)S(1)}, f32[2,768]{1,0:T(2,128)S(1)}, s32[]{:T(128)}, /*index=5*/s32[]{:T(128)}) while((s32[]{:T(128)}, f32[256,1024]{1,0:T(8,128)S(1)}, s32[2,768]{1,0:T(2,128)S(1)}, f32[2,768]{1,0:T(2,128)S(1)}, s32[]{:T(128)}, /*index=5*/s32[]{:T(128)}) %tuple.59), condition=%wide.region_1.2_spmd.clone, body=%wide.region_0.1_spmd.clone.sunk | while | flops 2417643008 | bytes 2127959 | solution.py:78
  26.5 2.2 fusion.37
  28.8 2.2 fusion.37
  32.0 10.3 %reduce-scatter.2.cloned.1.call-done = f32[128,1024]{1,0:T(8,128)} async-done(((f32[256,1024]{1,0:T(8,128)}), f32[128,1024]{1,0:T(8,128)}) %reduce-scatter.2.cloned.1.call-update) | async-done | bytes 524304 | tf_op jit(solution)/shard_map/reduce_scatter | solution.py:95
  43.5 3.2 %collective-permute-start = (f32[2,64,1024]{2,1,0:T(8,128)S(1)}, f32[2,64,1024]{2,1,0:T(8,128)S(1)}, u32[]{:S(2)}, u32[]{:S(2)}) collective-permute-start(f32[2,64,1024]{2,1,0:T(8,128)S(1)} %get-tuple-element.194), channel_id=1, source_target_pairs={{0,1},{1,4},{4,5},{5,8},{8,9},{9,12},{12,13},{2,3},{3,6},{6,7},{7,... | collective-permute-start | bytes 1572872 | tf_op jit(solution)/shard_map/ppermute | solution.py:20
  46.7 1.9 collective-permute-start.1
  48.6 4.2 %collective-permute-done = f32[2,64,1024]{2,1,0:T(8,128)S(1)} collective-permute-done((f32[2,64,1024]{2,1,0:T(8,128)S(1)}, f32[2,64,1024]{2,1,0:T(8,128)S(1)}, u32[]{:S(2)}, u32[]{:S(2)}) %collective-permute-start) | collective-permute-done | bytes 524320 | tf_op jit(solution)/shard_map/ppermute | solution.py:20
  52.8 4.4 %collective-permute-done.1 = f32[2,64,1024]{2,1,0:T(8,128)S(1)} collective-permute-done((f32[2,64,1024]{2,1,0:T(8,128)S(1)}, f32[2,64,1024]{2,1,0:T(8,128)S(1)}, u32[]{:S(2)}, u32[]{:S(2)}) %collective-permute-start.1) | collective-permute-done | bytes 524320 | tf_op jit(solution)/shard_map/ppermute | solution.py:22
  57.5 3.1 %collective-permute-start.2 = (f32[2,256,64]{2,1,0:T(8,128)S(1)}, f32[2,256,64]{2,1,0:T(8,128)S(1)}, u32[]{:S(2)}, u32[]{:S(2)}) collective-permute-start(f32[2,256,64]{2,1,0:T(8,128)S(1)} %get-tuple-element.193), channel_id=1, source_target_pairs={{0,2},{1,3},{4,6},{5,7},{8,10},{9,11},{12,14},{13,15},{16,18},{17,... | collective-permute-start | bytes 393224 | tf_op jit(solution)/shard_map/ppermute | solution.py:20
  60.6 1.3 collective-permute-start.3
  61.9 4.0 %collective-permute-done.2 = f32[2,256,64]{2,1,0:T(8,128)S(1)} collective-permute-done((f32[2,256,64]{2,1,0:T(8,128)S(1)}, f32[2,256,64]{2,1,0:T(8,128)S(1)}, u32[]{:S(2)}, u32[]{:S(2)}) %collective-permute-start.2) | collective-permute-done | bytes 131104 | tf_op jit(solution)/shard_map/ppermute | solution.py:20
  65.9 4.1 %collective-permute-done.3 = f32[2,256,64]{2,1,0:T(8,128)S(1)} collective-permute-done((f32[2,256,64]{2,1,0:T(8,128)S(1)}, f32[2,256,64]{2,1,0:T(8,128)S(1)}, u32[]{:S(2)}, u32[]{:S(2)}) %collective-permute-start.3) | collective-permute-done | bytes 131104 | tf_op jit(solution)/shard_map/ppermute | solution.py:22
  70.0 2.6 concatenate.13
  72.6 1.8 pad_bitcast_fusion
  74.7 2.4 fusion.22
  77.1 2.1 copy-done.2
  79.3 3.2 %broadcast_add_fusion.1 = f32[2,1152,3,128]{1,2,3,0:T(4,128)S(1)} fusion(f32[2,1152,3,128]{1,2,3,0:T(4,128)} %copy-done.2, f32[2,1152,3]{1,2,0:T(4,128)S(1)} %bitcast.55), kind=kLoop, calls=%fused_computation.41 | loop fusion | flops 884736 | bytes 7105536 | tf_op jit(solution)/shard_map/reduce_window_sum
  82.7 1.6 slice.69
  84.3 2.4 copy.28
  86.7 203.9 %while.25 = (s32[]{:T(128)}, f32[16,128,1024]{2,1,0:T(8,128)}, s32[16]{0:T(128)S(1)}, f32[2,257,1152]{1,2,0:T(8,128)S(1)}, s32[]{:T(128)}, /*index=5*/s32[1]{0:T...) while((s32[]{:T(128)}, f32[16,128,1024]{2,1,0:T(8,128)}, ...), condition=%wide.region_8.9_spmd, body=%wide.region_5.8_spmd.sunk | while | flops 43574024 | bytes 42071960 | solution.py:53
  90.5 1.3 fusion.33
  95.5 2.0 copy.46
  97.6 1.9 constant_dynamic-update-slice_fusion.2
  103.2 1.3 fusion.33
  108.3 2.0 copy.46
  110.3 1.9 constant_dynamic-update-slice_fusion.2
  116.0 1.3 fusion.33
  121.1 2.0 copy.46
  123.1 1.9 constant_dynamic-update-slice_fusion.2
  128.8 1.3 fusion.33
  133.8 2.0 copy.46
  135.9 1.9 constant_dynamic-update-slice_fusion.2
  146.6 2.0 copy.46
  148.6 1.9 constant_dynamic-update-slice_fusion.2
  159.3 2.0 copy.46
  161.3 1.9 constant_dynamic-update-slice_fusion.2
  167.0 1.3 fusion.33
  172.0 2.0 copy.46
  174.0 1.9 constant_dynamic-update-slice_fusion.2
  184.7 2.0 copy.46
  186.8 1.9 constant_dynamic-update-slice_fusion.2
  192.4 1.3 fusion.33
  197.5 2.0 copy.46
  199.5 1.9 constant_dynamic-update-slice_fusion.2
  210.2 2.0 copy.46
  212.3 1.9 constant_dynamic-update-slice_fusion.2
  223.0 2.0 copy.46
  225.0 1.9 constant_dynamic-update-slice_fusion.2
  235.7 2.0 copy.46
  237.8 1.9 constant_dynamic-update-slice_fusion.2
  248.4 2.0 copy.46
  250.5 1.9 constant_dynamic-update-slice_fusion.2
  261.2 2.0 copy.46
  263.2 1.9 constant_dynamic-update-slice_fusion.2
  273.9 2.0 copy.46
  276.0 1.9 constant_dynamic-update-slice_fusion.2
  286.7 2.0 copy.46
  288.7 1.9 constant_dynamic-update-slice_fusion.2
  (264 shorter events, 69.2 us)
Async XLA Ops:
  7.8 9.8 %all-to-all-start = ((s32[1,8,192]{2,0,1:T(1,128)}), s32[1,8,192]{2,0,1:T(1,128)S(1)}, u32[]{:S(2)}, u32[]{:S(2)}) async-start(s32[1,8,192]{2,0,1:T(1,128)} %copy.24), calls=%async_computation | async-start | bytes 16384 | tf_op jit(solution)/shard_map/all_to_all | solution.py:89
  17.7 8.6 %all-to-all-start.1 = ((f32[1,8,192]{2,0,1:T(1,128)}), f32[1,8,192]{2,0,1:T(1,128)S(1)}, u32[]{:S(2)}, u32[]{:S(2)}) async-start(f32[1,8,192]{2,0,1:T(1,128)} %compare_select_fusion.5), calls=%async_computation.1 | async-start | bytes 16384 | tf_op jit(solution)/shard_map/all_to_all | solution.py:90
  22.1 20.1 %reduce-scatter.2.cloned.1.call-start = ((), (), s32[]{:S(2)}) async-start(), calls=%async_computation.3 | async-start | bytes 1572864 | tf_op jit(solution)/shard_map/reduce_scatter | solution.py:95
  26.4 15.9 %copy-start.3 = (f32[128,1024]{1,0:T(8,128)S(1)}, f32[128,1024]{1,0:T(8,128)}, u32[]{:S(2)}) copy-start(f32[128,1024]{1,0:T(8,128)} %param.12) | copy-start | bytes 1572868
  31.0 1.0 copy-start.5
  42.3 14.9 %copy-start.4 = (f32[128,1024]{1,0:T(8,128)S(1)}, f32[128,1024]{1,0:T(8,128)}, u32[]{:S(2)}) copy-start(f32[128,1024]{1,0:T(8,128)} %reduce-scatter.2.cloned.1.call-done) | copy-start | bytes 1572868
  43.5 9.3 %collective-permute-start = (f32[2,64,1024]{2,1,0:T(8,128)S(1)}, f32[2,64,1024]{2,1,0:T(8,128)S(1)}, u32[]{:S(2)}, u32[]{:S(2)}) collective-permute-start(f32[2,64,1024]{2,1,0:T(8,128)S(1)} %get-tuple-element.194), channel_id=1, source_target_pairs={{0,1},{1,4},{4,5},{5,8},{8,9},{9,12},{12,13},{2,3},{3,6},{6,7},{7,... | collective-permute-start | bytes 1572872 | tf_op jit(solution)/shard_map/ppermute | solution.py:20
  46.7 10.5 %collective-permute-start.1 = (f32[2,64,1024]{2,1,0:T(8,128)S(1)}, f32[2,64,1024]{2,1,0:T(8,128)S(1)}, u32[]{:S(2)}, u32[]{:S(2)}) collective-permute-start(f32[2,64,1024]{2,1,0:T(8,128)S(1)} %get-tuple-element.195), channel_id=1, source_target_pairs={{1,0},{4,1},{5,4},{8,5},{9,8},{12,9},{13,12},{3,2},{6,3},{7,6},{10... | collective-permute-start | bytes 1572872 | tf_op jit(solution)/shard_map/ppermute | solution.py:22
  57.5 8.4 %collective-permute-start.2 = (f32[2,256,64]{2,1,0:T(8,128)S(1)}, f32[2,256,64]{2,1,0:T(8,128)S(1)}, u32[]{:S(2)}, u32[]{:S(2)}) collective-permute-start(f32[2,256,64]{2,1,0:T(8,128)S(1)} %get-tuple-element.193), channel_id=1, source_target_pairs={{0,2},{1,3},{4,6},{5,7},{8,10},{9,11},{12,14},{13,15},{16,18},{17,... | collective-permute-start | bytes 393224 | tf_op jit(solution)/shard_map/ppermute | solution.py:20
  60.6 9.4 %collective-permute-start.3 = (f32[2,256,64]{2,1,0:T(8,128)S(1)}, f32[2,256,64]{2,1,0:T(8,128)S(1)}, u32[]{:S(2)}, u32[]{:S(2)}) collective-permute-start(f32[2,256,64]{2,1,0:T(8,128)S(1)} %get-tuple-element.192), channel_id=1, source_target_pairs={{2,0},{3,1},{6,4},{7,5},{10,8},{11,9},{14,12},{15,13},{18,16},{19,... | collective-permute-start | bytes 393224 | tf_op jit(solution)/shard_map/ppermute | solution.py:22
  77.1 2.1 copy-start.2
  84.3 2.4 copy-start.6
  86.7 3.8 %copy-start = (f32[2,257,1152]{1,2,0:T(8,128)}, f32[2,257,1152]{1,2,0:T(8,128)S(1)}, u32[]{:S(2)}) copy-start(f32[2,257,1152]{1,2,0:T(8,128)S(1)} %get-tuple-element.301) | copy-start | bytes 7105540 | tf_op jit(solution)/shard_map/while
  93.8 5.6 %copy-start.1 = (f32[2,257,1152]{1,2,0:T(8,128)S(1)}, f32[2,257,1152]{1,2,0:T(8,128)}, u32[]{:S(2)}) copy-start(f32[2,257,1152]{1,2,0:T(8,128)} %copy-done) | copy-start | bytes 7105540 | tf_op jit(solution)/shard_map/while
  99.4 3.8 %copy-start = (f32[2,257,1152]{1,2,0:T(8,128)}, f32[2,257,1152]{1,2,0:T(8,128)S(1)}, u32[]{:S(2)}) copy-start(f32[2,257,1152]{1,2,0:T(8,128)S(1)} %get-tuple-element.301) | copy-start | bytes 7105540 | tf_op jit(solution)/shard_map/while
  106.6 5.6 %copy-start.1 = (f32[2,257,1152]{1,2,0:T(8,128)S(1)}, f32[2,257,1152]{1,2,0:T(8,128)}, u32[]{:S(2)}) copy-start(f32[2,257,1152]{1,2,0:T(8,128)} %copy-done) | copy-start | bytes 7105540 | tf_op jit(solution)/shard_map/while
  112.2 3.8 %copy-start = (f32[2,257,1152]{1,2,0:T(8,128)}, f32[2,257,1152]{1,2,0:T(8,128)S(1)}, u32[]{:S(2)}) copy-start(f32[2,257,1152]{1,2,0:T(8,128)S(1)} %get-tuple-element.301) | copy-start | bytes 7105540 | tf_op jit(solution)/shard_map/while
  119.3 5.6 %copy-start.1 = (f32[2,257,1152]{1,2,0:T(8,128)S(1)}, f32[2,257,1152]{1,2,0:T(8,128)}, u32[]{:S(2)}) copy-start(f32[2,257,1152]{1,2,0:T(8,128)} %copy-done) | copy-start | bytes 7105540 | tf_op jit(solution)/shard_map/while
  125.0 3.8 %copy-start = (f32[2,257,1152]{1,2,0:T(8,128)}, f32[2,257,1152]{1,2,0:T(8,128)S(1)}, u32[]{:S(2)}) copy-start(f32[2,257,1152]{1,2,0:T(8,128)S(1)} %get-tuple-element.301) | copy-start | bytes 7105540 | tf_op jit(solution)/shard_map/while
  132.1 5.6 %copy-start.1 = (f32[2,257,1152]{1,2,0:T(8,128)S(1)}, f32[2,257,1152]{1,2,0:T(8,128)}, u32[]{:S(2)}) copy-start(f32[2,257,1152]{1,2,0:T(8,128)} %copy-done) | copy-start | bytes 7105540 | tf_op jit(solution)/shard_map/while
  137.7 3.8 %copy-start = (f32[2,257,1152]{1,2,0:T(8,128)}, f32[2,257,1152]{1,2,0:T(8,128)S(1)}, u32[]{:S(2)}) copy-start(f32[2,257,1152]{1,2,0:T(8,128)S(1)} %get-tuple-element.301) | copy-start | bytes 7105540 | tf_op jit(solution)/shard_map/while
  144.8 5.6 %copy-start.1 = (f32[2,257,1152]{1,2,0:T(8,128)S(1)}, f32[2,257,1152]{1,2,0:T(8,128)}, u32[]{:S(2)}) copy-start(f32[2,257,1152]{1,2,0:T(8,128)} %copy-done) | copy-start | bytes 7105540 | tf_op jit(solution)/shard_map/while
  150.5 3.8 %copy-start = (f32[2,257,1152]{1,2,0:T(8,128)}, f32[2,257,1152]{1,2,0:T(8,128)S(1)}, u32[]{:S(2)}) copy-start(f32[2,257,1152]{1,2,0:T(8,128)S(1)} %get-tuple-element.301) | copy-start | bytes 7105540 | tf_op jit(solution)/shard_map/while
  157.6 5.6 %copy-start.1 = (f32[2,257,1152]{1,2,0:T(8,128)S(1)}, f32[2,257,1152]{1,2,0:T(8,128)}, u32[]{:S(2)}) copy-start(f32[2,257,1152]{1,2,0:T(8,128)} %copy-done) | copy-start | bytes 7105540 | tf_op jit(solution)/shard_map/while
  163.2 3.8 %copy-start = (f32[2,257,1152]{1,2,0:T(8,128)}, f32[2,257,1152]{1,2,0:T(8,128)S(1)}, u32[]{:S(2)}) copy-start(f32[2,257,1152]{1,2,0:T(8,128)S(1)} %get-tuple-element.301) | copy-start | bytes 7105540 | tf_op jit(solution)/shard_map/while
  170.3 5.6 %copy-start.1 = (f32[2,257,1152]{1,2,0:T(8,128)S(1)}, f32[2,257,1152]{1,2,0:T(8,128)}, u32[]{:S(2)}) copy-start(f32[2,257,1152]{1,2,0:T(8,128)} %copy-done) | copy-start | bytes 7105540 | tf_op jit(solution)/shard_map/while
  175.9 3.8 %copy-start = (f32[2,257,1152]{1,2,0:T(8,128)}, f32[2,257,1152]{1,2,0:T(8,128)S(1)}, u32[]{:S(2)}) copy-start(f32[2,257,1152]{1,2,0:T(8,128)S(1)} %get-tuple-element.301) | copy-start | bytes 7105540 | tf_op jit(solution)/shard_map/while
  183.0 5.6 %copy-start.1 = (f32[2,257,1152]{1,2,0:T(8,128)S(1)}, f32[2,257,1152]{1,2,0:T(8,128)}, u32[]{:S(2)}) copy-start(f32[2,257,1152]{1,2,0:T(8,128)} %copy-done) | copy-start | bytes 7105540 | tf_op jit(solution)/shard_map/while
  188.7 3.8 %copy-start = (f32[2,257,1152]{1,2,0:T(8,128)}, f32[2,257,1152]{1,2,0:T(8,128)S(1)}, u32[]{:S(2)}) copy-start(f32[2,257,1152]{1,2,0:T(8,128)S(1)} %get-tuple-element.301) | copy-start | bytes 7105540 | tf_op jit(solution)/shard_map/while
  195.8 5.6 %copy-start.1 = (f32[2,257,1152]{1,2,0:T(8,128)S(1)}, f32[2,257,1152]{1,2,0:T(8,128)}, u32[]{:S(2)}) copy-start(f32[2,257,1152]{1,2,0:T(8,128)} %copy-done) | copy-start | bytes 7105540 | tf_op jit(solution)/shard_map/while
  201.4 3.8 %copy-start = (f32[2,257,1152]{1,2,0:T(8,128)}, f32[2,257,1152]{1,2,0:T(8,128)S(1)}, u32[]{:S(2)}) copy-start(f32[2,257,1152]{1,2,0:T(8,128)S(1)} %get-tuple-element.301) | copy-start | bytes 7105540 | tf_op jit(solution)/shard_map/while
  208.5 5.6 %copy-start.1 = (f32[2,257,1152]{1,2,0:T(8,128)S(1)}, f32[2,257,1152]{1,2,0:T(8,128)}, u32[]{:S(2)}) copy-start(f32[2,257,1152]{1,2,0:T(8,128)} %copy-done) | copy-start | bytes 7105540 | tf_op jit(solution)/shard_map/while
  214.1 3.8 %copy-start = (f32[2,257,1152]{1,2,0:T(8,128)}, f32[2,257,1152]{1,2,0:T(8,128)S(1)}, u32[]{:S(2)}) copy-start(f32[2,257,1152]{1,2,0:T(8,128)S(1)} %get-tuple-element.301) | copy-start | bytes 7105540 | tf_op jit(solution)/shard_map/while
  221.2 5.6 %copy-start.1 = (f32[2,257,1152]{1,2,0:T(8,128)S(1)}, f32[2,257,1152]{1,2,0:T(8,128)}, u32[]{:S(2)}) copy-start(f32[2,257,1152]{1,2,0:T(8,128)} %copy-done) | copy-start | bytes 7105540 | tf_op jit(solution)/shard_map/while
  226.9 3.8 %copy-start = (f32[2,257,1152]{1,2,0:T(8,128)}, f32[2,257,1152]{1,2,0:T(8,128)S(1)}, u32[]{:S(2)}) copy-start(f32[2,257,1152]{1,2,0:T(8,128)S(1)} %get-tuple-element.301) | copy-start | bytes 7105540 | tf_op jit(solution)/shard_map/while
  234.0 5.6 %copy-start.1 = (f32[2,257,1152]{1,2,0:T(8,128)S(1)}, f32[2,257,1152]{1,2,0:T(8,128)}, u32[]{:S(2)}) copy-start(f32[2,257,1152]{1,2,0:T(8,128)} %copy-done) | copy-start | bytes 7105540 | tf_op jit(solution)/shard_map/while
  239.6 3.8 %copy-start = (f32[2,257,1152]{1,2,0:T(8,128)}, f32[2,257,1152]{1,2,0:T(8,128)S(1)}, u32[]{:S(2)}) copy-start(f32[2,257,1152]{1,2,0:T(8,128)S(1)} %get-tuple-element.301) | copy-start | bytes 7105540 | tf_op jit(solution)/shard_map/while
  246.7 5.6 %copy-start.1 = (f32[2,257,1152]{1,2,0:T(8,128)S(1)}, f32[2,257,1152]{1,2,0:T(8,128)}, u32[]{:S(2)}) copy-start(f32[2,257,1152]{1,2,0:T(8,128)} %copy-done) | copy-start | bytes 7105540 | tf_op jit(solution)/shard_map/while
  252.4 3.8 %copy-start = (f32[2,257,1152]{1,2,0:T(8,128)}, f32[2,257,1152]{1,2,0:T(8,128)S(1)}, u32[]{:S(2)}) copy-start(f32[2,257,1152]{1,2,0:T(8,128)S(1)} %get-tuple-element.301) | copy-start | bytes 7105540 | tf_op jit(solution)/shard_map/while
  259.5 5.6 %copy-start.1 = (f32[2,257,1152]{1,2,0:T(8,128)S(1)}, f32[2,257,1152]{1,2,0:T(8,128)}, u32[]{:S(2)}) copy-start(f32[2,257,1152]{1,2,0:T(8,128)} %copy-done) | copy-start | bytes 7105540 | tf_op jit(solution)/shard_map/while
  265.1 3.8 %copy-start = (f32[2,257,1152]{1,2,0:T(8,128)}, f32[2,257,1152]{1,2,0:T(8,128)S(1)}, u32[]{:S(2)}) copy-start(f32[2,257,1152]{1,2,0:T(8,128)S(1)} %get-tuple-element.301) | copy-start | bytes 7105540 | tf_op jit(solution)/shard_map/while
  272.2 5.6 %copy-start.1 = (f32[2,257,1152]{1,2,0:T(8,128)S(1)}, f32[2,257,1152]{1,2,0:T(8,128)}, u32[]{:S(2)}) copy-start(f32[2,257,1152]{1,2,0:T(8,128)} %copy-done) | copy-start | bytes 7105540 | tf_op jit(solution)/shard_map/while
  277.9 3.8 %copy-start = (f32[2,257,1152]{1,2,0:T(8,128)}, f32[2,257,1152]{1,2,0:T(8,128)S(1)}, u32[]{:S(2)}) copy-start(f32[2,257,1152]{1,2,0:T(8,128)S(1)} %get-tuple-element.301) | copy-start | bytes 7105540 | tf_op jit(solution)/shard_map/while
  285.0 5.6 %copy-start.1 = (f32[2,257,1152]{1,2,0:T(8,128)S(1)}, f32[2,257,1152]{1,2,0:T(8,128)}, u32[]{:S(2)}) copy-start(f32[2,257,1152]{1,2,0:T(8,128)} %copy-done) | copy-start | bytes 7105540 | tf_op jit(solution)/shard_map/while
Sparse Core Ops, SparseCore 0:
  32.1 10.0 reduce-scatter.1
where the time goes:
time: 300 us; the launch traced here: 297 us
  local copies, waits for them, and re-layouts  96.6 us (32%)
  loops' own time  67.8 us (23%)
  other arithmetic  61.7 us (21%)
  waiting for transfers between devices  33.8 us (11%)
  starting transfers between devices  19.7 us (7%)
  between operations  13.5 us (4%)
  matrix products  4.39 us (1%)
    another operation x1, loops' own time, prefix_fields(): return lax.map(one_size, half_widths)  67.7 us
    dynamic_update_slice x32, local copies, waits for them, and re-layouts, prefix_fields(): return lax.map(one_size, half_widths)  62.7 us
    another operation x51, other arithmetic  28.7 us
    div x16, other arithmetic, poisson_ratio(): return (entropy + box_base - box_counts) / side  15.9 us
    dynamic_slice x16, local copies, waits for them, and re-layouts, prefix_fields(): return lax.map(one_size, half_widths)  11.2 us
    another operation x68, local copies, waits for them, and re-layouts  11.1 us
    sub x16, other arithmetic, one_size(): row_boxes = upper - lower  10.9 us
    reduce_scatter x1, waiting for transfers between devices, shards(): lax.psum_scatter(bin_rows(grouped_cells, grouped_weights, jnp.int32(0), b...  10.3 us
  transfers between devices with their start and end apart: 7, of which 7 were waited for; matrix products, arithmetic and copies ran while one was open for 0% of the time, Pallas kernels for 0%

commit v1 on v0

v1 whole, which is shorter than its diff:
```python
import functools

import jax
import jax.numpy as jnp
from jax import lax
from jax.experimental import pallas as pl
from jax.experimental.pallas import tpu as pltpu
from jax.sharding import PartitionSpec as P

HALO = 64
LANES = 128
CODE = 4096
ROW_BIAS = 256
COL_BIAS = 1024
TINY = 1e-30
F32 = jnp.float32
BF16 = jnp.bfloat16


def side_tiles(cols):
    return min(cols - 1, 2)


def pieces_of(dest, rows, cols):
    row, col, claim = dest
    other = row - 1 if claim == 0 else row + 1
    sides = [(col, 0)]
    if cols == 2:
        sides.append((1 - col, -1 if col == 1 else 1))
    elif cols > 2:
        sides += [(col - 1, -1), (col + 1, 1)]
    found = []
    for tile_row, vertical in ((row, 0), (other, 1)):
        for tile_col, side in sides:
            there = 0 <= tile_row < rows and 0 <= tile_col < cols
            found.append((tile_row * cols + tile_col if there else None, vertical, side))
    return found


def pack_kernel(rows, cols, block_rows, block_cols, cell_ref, weight_ref, count_ref, out_ref):
    cell = cell_ref[0]
    slot = lax.broadcasted_iota(jnp.int32, cell.shape, 1)
    weight = jnp.where(slot < count_ref[...], weight_ref[0], 0.0)
    tile_row = lax.div(cell, block_cols)
    tile_col = lax.rem(cell, block_cols)
    codes = {}
    for claim in (0, 1):
        for vertical in (0, 1):
            if vertical:
                first = 2 * block_rows - HALO if claim == 0 else 0
            else:
                first = 0 if claim == 0 else block_rows - HALO
            for side in (-1, 0, 1):
                shift = {-1: HALO - block_cols, 0: 0, 1: HALO}[side]
                row_code = (tile_row + (ROW_BIAS - first)) * CODE
                codes[claim, vertical, side] = (row_code + tile_col + (shift + COL_BIAS)).astype(F32)
    zero = jnp.zeros((1, cell.shape[1]), F32)
    index = 0
    for row in range(rows):
        for col in range(cols):
            for claim in (0, 1):
                for place, (tile, vertical, side) in enumerate(pieces_of((row, col, claim), rows, cols)):
                    if tile is None:
                        out_ref[index, 2 * place : 2 * place + 1, :] = zero
                        out_ref[index, 2 * place + 1 : 2 * place + 2, :] = zero
                    else:
                        out_ref[index, 2 * place : 2 * place + 1, :] = codes[claim, vertical, side][tile : tile + 1]
                        out_ref[index, 2 * place + 1 : 2 * place + 2, :] = weight[tile : tile + 1]
                index += 1


def halves(value):
    high = value.astype(BF16)
    return high, (value - high.astype(F32)).astype(BF16)


def onehot(index, size):
    return index == lax.broadcasted_iota(jnp.int32, (size, index.shape[1]), 0)


def scan_kernel(
    sides, params_ref, got_ref, base_ref, above_ref, below_ref, beside_ref, out_ref, prefix, window, code_s, weight_s, own_acc, far_acc, side_acc, corner_acc
):
    block_rows, block_cols = base_ref.shape
    blocks = block_cols // LANES
    step = pl.program_id(0)
    senders, _, slots = got_ref.shape
    chunks = senders * slots // LANES
    own_rows = block_rows + HALO

    def prefix_of(field):
        lane = lax.broadcasted_iota(jnp.int32, (2 * block_rows, LANES), 1)
        sub = lax.broadcasted_iota(jnp.int32, (2 * block_rows // 8, 8, LANES), 1)
        for block in range(blocks + 1):
            left = window[blocks] if block == 0 else pltpu.roll(window[block - 1], HALO, axis=1)
            right = window[blocks] if block == blocks else pltpu.roll(window[block], HALO, axis=1)
            cells = jnp.where(lane < HALO, left, right).reshape(-1, 8, LANES)
            for hop in (1, 2, 4):
                cells = cells + jnp.where(sub >= hop, pltpu.roll(cells, hop, axis=1), 0.0)
            carry = jnp.zeros((8, LANES), F32)
            prefix[field, block, 0:8, :] = carry
            for tile in range(2 * block_rows // 8):
                total = cells[tile] + carry
                prefix[field, block, 8 * tile + 8 : 8 * tile + 16, :] = total
                carry = jnp.broadcast_to(total[7:8], (8, LANES))

    @pl.when(step == 0)
    def _():
        claim = params_ref[0]
        for place in range(2 * sides + 2):
            code = got_ref[:, 2 * place, :].astype(jnp.int32)
            weight = got_ref[:, 2 * place + 1, :]
            half = senders // 2
            for ref, value in ((code_s, code), (weight_s, weight)):
                ref[place, 0:senders, :] = value[:, :LANES]
                ref[place, senders : senders + half, 0 : slots - LANES] = value[:half, LANES:]
                ref[place, senders : senders + half, slots - LANES : LANES] = value[half:, LANES:]
        for acc in (own_acc, far_acc, side_acc, corner_acc):
            acc[...] = jnp.zeros_like(acc)

        def add_pair(pair, _):
            for place in range(2 * sides + 2):
                vertical, side = divmod(place, sides + 1)
                rows = HALO if vertical else own_rows
                cols = LANES if side else block_cols
                row_parts, col_parts = [], []
                for one in (0, 1):
                    code = code_s[place, pl.ds(2 * pair + one, 1), :]
                    weight = weight_s[place, pl.ds(2 * pair + one, 1), :]
                    high = weight.astype(BF16).astype(F32)
                    low = weight - high
                    hit = onehot(lax.div(code, CODE) - ROW_BIAS, rows)
                    row_parts.append(
                        jnp.concatenate([jnp.where(hit, high, 0.0), jnp.where(hit, low, 0.0)], axis=0).astype(BF16)
                    )
                    col_parts.append(
                        jnp.where(onehot(lax.rem(code, CODE) - COL_BIAS, cols), 1.0, 0.0).astype(BF16)
                    )
                product = lax.dot_general(
                    jnp.concatenate(row_parts, axis=1),
                    jnp.concatenate(col_parts, axis=1),
                    (((1,), (1,)), ((), ())),
                    preferred_element_type=F32,
                )
                acc = {(0, False): own_acc, (1, False): far_acc, (0, True): side_acc, (1, True): corner_acc}[
                    vertical, side > 0
                ]
                acc[...] += product
            return 0

        lax.fori_loop(0, chunks // 2, add_pair, 0)
        own_at = pl.multiple_of((1 - claim) * HALO, HALO)
        far_at = pl.multiple_of(claim * own_rows, HALO)
        for block in range(blocks):
            here = slice(block * LANES, (block + 1) * LANES)
            window[block, pl.ds(own_at, own_rows), :] = own_acc[:own_rows, here] + own_acc[own_rows:, here]
            window[block, pl.ds(far_at, HALO), :] = far_acc[:HALO, here] + far_acc[HALO:, here]
        window[blocks, pl.ds(own_at, own_rows), :] = side_acc[:own_rows] + side_acc[own_rows:]
        window[blocks, pl.ds(far_at, HALO), :] = corner_acc[:HALO] + corner_acc[HALO:]
        prefix_of(0)
        for block in range(blocks):
            here = slice(block * LANES, (block + 1) * LANES)
            window[block, 0:HALO, :] = above_ref[:, here]
            window[block, HALO : HALO + block_rows, :] = base_ref[:, here]
            window[block, HALO + block_rows :, :] = below_ref[:, here]
        window[blocks] = beside_ref[...]
        prefix_of(1)

    half = params_ref[1 + step]
    inverse = 1.0 / (2 * half + 1).astype(F32)
    from_col = lax.broadcasted_iota(jnp.int32, (2 * LANES, LANES), 0)
    to_col = lax.broadcasted_iota(jnp.int32, (2 * LANES, LANES), 1) + HALO
    band = jnp.where(jnp.abs(from_col - to_col) <= half, 1.0, 0.0).astype(BF16)

    def boxes(field):
        parts = []
        for block in range(blocks + 1):
            strip = prefix[field, block, pl.ds(HALO + 8 + half, block_rows), :] - prefix[
                field, block, pl.ds(HALO + 7 - half, block_rows), :
            ]
            parts.append(halves(strip))
        total = None
        for part in (0, 1):
            left = jnp.concatenate(
                [jnp.concatenate([parts[b][part], parts[b + 1][part]], axis=1) for b in range(blocks)], axis=0
            )
            product = jnp.dot(left, band, preferred_element_type=F32)
            total = product if total is None else total + product
        return total

    counts = boxes(0)
    base = boxes(1)
    result = (counts * (jnp.log(jnp.maximum(counts, TINY)) - jnp.log(base) - 1.0) + base) * inverse
    for block in range(blocks):
        out_ref[0, :, block * LANES : (block + 1) * LANES] = result[block * block_rows : (block + 1) * block_rows]


def shards(rows, cols, claim_cell, claim_weight, claim_count, baseline, half_widths):
    block_rows, block_cols = baseline.shape
    slots = claim_cell.shape[2]
    sides = side_tiles(cols)
    devices = rows * cols * 2
    sent = pl.pallas_call(
        functools.partial(pack_kernel, rows, cols, block_rows, block_cols),
        out_shape=jax.ShapeDtypeStruct((devices, 4 * (sides + 1), slots), F32),
    )(claim_cell, claim_weight, claim_count.reshape(-1, 1))
    got = lax.all_to_all(sent, ("row", "col", "claim"), split_axis=0, concat_axis=0, tiled=True)

    strips = rows * 2
    down = [(i, i + 1) for i in range(strips - 1)]
    up = [(i + 1, i) for i in range(strips - 1)]
    above = lax.ppermute(baseline[block_rows - HALO :], ("row", "claim"), down)
    below = lax.ppermute(baseline[:HALO], ("row", "claim"), up)
    tall = jnp.concatenate([above, baseline, below], axis=0)
    first, last = tall[:, :HALO], tall[:, block_cols - HALO :]
    if cols == 2:
        col = lax.axis_index("col")
        beside = lax.ppermute(
            jnp.concatenate([jnp.where(col == 0, last, 0.0), jnp.where(col == 1, first, 0.0)], axis=1),
            "col",
            [(0, 1), (1, 0)],
        )
    else:
        beside = jnp.concatenate(
            [
                lax.ppermute(last, "col", [(i, i + 1) for i in range(cols - 1)]),
                lax.ppermute(first, "col", [(i + 1, i) for i in range(cols - 1)]),
            ],
            axis=1,
        )
    params = jnp.concatenate([lax.axis_index("claim").astype(jnp.int32)[None], half_widths])
    sizes = half_widths.shape[0]
    blocks = block_cols // LANES
    places = 2 * (sides + 1)
    chunk_rows = devices * slots // LANES
    whole = pl.BlockSpec(memory_space=pltpu.VMEM)
    return pl.pallas_call(
        functools.partial(scan_kernel, sides),
        grid_spec=pltpu.PrefetchScalarGridSpec(
            num_scalar_prefetch=1,
            grid=(sizes,),
            in_specs=[whole] * 5,
            out_specs=pl.BlockSpec((1, block_rows, block_cols), lambda k, params: (k, 0, 0)),
            scratch_shapes=[
                pltpu.VMEM((2, blocks + 1, 2 * block_rows + 8, LANES), F32),
                pltpu.VMEM((blocks + 1, 2 * block_rows, LANES), F32),
                pltpu.VMEM((places, chunk_rows, LANES), jnp.int32),
                pltpu.VMEM((places, chunk_rows, LANES), F32),
                pltpu.VMEM((2 * (block_rows + HALO), block_cols), F32),
                pltpu.VMEM((2 * HALO, block_cols), F32),
                pltpu.VMEM((2 * (block_rows + HALO), LANES), F32),
                pltpu.VMEM((2 * HALO, LANES), F32),
            ],
        ),
        out_shape=jax.ShapeDtypeStruct((sizes, block_rows, block_cols), F32),
        compiler_params=pltpu.CompilerParams(vmem_limit_bytes=48 * 1024 * 1024),
    )(params, got, baseline, above, below, beside)


def solution(mesh):
    in_specs = (
        P(("groups", "row", "col", "claim"), None, None),
        P(("groups", "row", "col", "claim"), None, None),
        P(("groups", "row", "col", "claim"), None),
        P(("groups", "row", "claim"), "col"),
        P(),
    )
    out_specs = P(None, ("groups", "row", "claim"), "col")
    body = functools.partial(shards, mesh.shape["row"], mesh.shape["col"])
    return jax.shard_map(body, mesh=mesh, in_specs=in_specs, out_specs=out_specs, check_vma=False)
```

time: 300 us -> 49.4 us (0.16)
  the two profiles are of different devices: /device:TPU:9 before, /device:TPU:0 now
where the time goes in v1:
time: 49.4 us; the launch traced here: 49 us
  Pallas kernels  24.5 us (50%)
  starting transfers between devices  14.9 us (30%)
  local copies, waits for them, and re-layouts  4.54 us (9%)
  waiting for transfers between devices  4.07 us (8%)
  other arithmetic  0.93 us (2%)
    pallas_call x1, Pallas kernels, shards(): pl.pallas_call(functools.partial(scan_kernel, sides), grid_spec=pltpu.Pre...  23 us
    all_to_all x1, starting transfers between devices, shards(): lax.all_to_all(sent, ('row', 'col', 'claim'), split_axis=0, concat_axis=0...  9.25 us
    all_to_all x1, waiting for transfers between devices, shards(): lax.all_to_all(sent, ('row', 'col', 'claim'), split_axis=0, concat_axis=0...  3.86 us
    ppermute x1, starting transfers between devices, shards(): above = lax.ppermute(baseline[block_rows - HALO:], ('row', 'claim'), down)  2.37 us
    unnamed x4, local copies, waits for them, and re-layouts  2.14 us
    ppermute x1, starting transfers between devices, shards(): lax.ppermute(jnp.concatenate([jnp.where(col == 0, last, 0.0), jnp.where(c...  1.98 us
    pallas_call x1, Pallas kernels, shards(): pl.pallas_call(functools.partial(pack_kernel, rows, cols, block_rows, blo...  1.46 us
    reshape x1, local copies, waits for them, and re-layouts, shards(): claim_count.reshape(-1, 1)  1.32 us
  transfers between devices with their start and end apart: 4, of which 2 were waited for; matrix products, arithmetic and copies ran while one was open for 7% of the time, Pallas kernels for 3%

profile of v1, /device:TPU:0, one launch (start us, length us, event | category | flops | bytes accessed | tf_op | source)
XLA Modules:
  0.0 49.0 jit_solution(2698938926026729342)
XLA Ops:
  0.0 1.1 %fusion = (f32[64,1024]{1,0:T(8,128)S(1)}, f32[64,1024]{1,0:T(8,128)S(1)}) fusion(f32[128,1024]{1,0:T(8,128)} %base_ref.1), kind=kLoop, calls=%fused_computation.7 | loop fusion | bytes 1048576 | tf_op jit(solution)/shard_map/slice | solution.py:213
  1.1 2.4 %collective-permute-start = (f32[64,1024]{1,0:T(8,128)S(1)}, f32[64,1024]{1,0:T(8,128)S(1)}, u32[]{:S(2)}, u32[]{:S(2)}) collective-permute-start(f32[64,1024]{1,0:T(8,128)S(1)} %get-tuple-element.8), channel_id=1, source_target_pairs={{0,1},{1,4},{4,5},{5,8},{8,9},{9,12},{12,13},{2,3},{3,6},{6,7},{7,... | collective-permute-start | bytes 786440 | tf_op jit(solution)/shard_map/ppermute | solution.py:212
  3.5 1.3 %collective-permute-start.1 = (f32[64,1024]{1,0:T(8,128)S(1)}, f32[64,1024]{1,0:T(8,128)S(1)}, u32[]{:S(2)}, u32[]{:S(2)}) collective-permute-start(f32[64,1024]{1,0:T(8,128)S(1)} %get-tuple-element.7), channel_id=1, source_target_pairs={{1,0},{4,1},{5,4},{8,5},{9,8},{12,9},{13,12},{3,2},{6,3},{7,6},{10... | collective-permute-start | bytes 786440 | tf_op jit(solution)/shard_map/ppermute | solution.py:213
  4.8 1.3 %copy.6.count_ref = s32[8,1]{1,0:T(8,128)} copy(s32[8,1]{0,1:T(1,128)} %bitcast.2) | data formatting | bytes 64 | tf_op jit(solution)/shard_map/reshape | solution.py:206
  6.1 1.5 %shard_map.55 = f32[16,8,192]{2,1,0:T(8,128)} custom-call(s32[1,8,192]{2,1,0:T(8,128)} %cell_ref.1, f32[1,8,192]{2,1,0:T(8,128)} %weight_ref.1, s32[8,1]{1,0:T(8,128)} %copy.6.count_ref), custom_call_target="tpu_custom_call" | custom-call | tf_op jit(solution)/shard_map/pallas_call | solution.py:203
  7.5 9.3 %all-to-all-start = ((f32[16,8,192]{2,1,0:T(8,128)}), f32[16,8,192]{2,1,0:T(8,128)S(1)}, u32[]{:S(2)}, u32[]{:S(2)}) async-start(f32[16,8,192]{2,1,0:T(8,128)} %shard_map.55), calls=%async_computation | async-start | bytes 262144 | tf_op jit(solution)/shard_map/all_to_all | solution.py:207
  16.8 0.0 collective-permute-done.above_ref
  16.8 1.1 %constant_dynamic-update-slice_fusion.1 = f32[256,1024]{1,0:T(8,128)S(1)} fusion(f32[256,1024]{1,0:T(8,128)S(1)} %constant_dynamic-update-slice_fusion.2, f32[128,1024]{1,0:T(8,128)} %base_ref.1), kind=kLoop, calls=%fused_computation.4 | loop fusion | bytes 1048576
  17.9 0.0 collective-permute-done.1.below_ref
  18.0 0.1 slice_select_fusion.1
  18.1 0.1 pad_maximum_fusion
  18.2 2.0 %collective-permute-start.2 = (f32[256,128]{1,0:T(8,128)S(1)}, f32[256,128]{1,0:T(8,128)S(1)}, u32[]{:S(2)}, u32[]{:S(2)}) collective-permute-start(f32[256,128]{1,0:T(8,128)S(1)} %pad_maximum_fusion), channel_id=1, source_target_pairs={{0,2},{2,0},{1,3},{3,1},{4,6},{6,4},{5,7},{7,5},{8,10},{10,8},{9,1... | collective-permute-start | bytes 393224 | tf_op jit(solution)/shard_map/ppermute | solution.py:218
  20.1 0.7 %pad_add_fusion.params_ref = s32[17]{0:T(128)S(1)} fusion(s32[16]{0:T(128)} %param.9, s32[1]{0:T(128)} %bitcast), kind=kLoop, calls=%fused_computation.6 | loop fusion | flops 17 | bytes 136 | tf_op jit(solution)/shard_map/concatenate | solution.py:231
  20.9 3.9 %all-to-all-done.got_ref = f32[16,8,192]{2,1,0:T(8,128)S(1)} async-done(((f32[16,8,192]{2,1,0:T(8,128)}), f32[16,8,192]{2,1,0:T(8,128)S(1)}, u32[]{:S(2)}, u32[]{:S(2)}) %all-to-all-start) | async-done | bytes 98336 | tf_op jit(solution)/shard_map/all_to_all | solution.py:207
  24.7 0.2 collective-permute-done.2.beside_ref
  24.9 0.0 copy-start
  24.9 1.0 %copy-done = f32[128,1024]{1,0:T(8,128)S(1)} copy-done((f32[128,1024]{1,0:T(8,128)S(1)}, f32[128,1024]{1,0:T(8,128)}, u32[]{:S(2)}) %copy-start) | copy-done | bytes 524312
  26.0 23.0 %shard_map.56 = f32[16,128,1024]{2,1,0:T(8,128)} custom-call(s32[17]{0:T(128)S(1)} %pad_add_fusion.params_ref, f32[16,8,192]{2,1,0:T(8,128)S(1)} %all-to-all-done.got_ref, f32[128,1024]{1,0:T(8,128)S(1)} %copy-done, f32[64,1024]{1,0:T(8,128)S(1)} %collective-permute-done.above_ref, f32[64,1024]{1,0:T(8,128)S(1)} %collective-permute-done.1.below_ref, ...), custom_call_target="tpu_custom_call" | custom-call | tf_op jit(solution)/shard_map/pallas_call | solution.py:237
  (2 shorter events, 0.0 us)
Async XLA Ops:
  1.1 15.7 %collective-permute-start = (f32[64,1024]{1,0:T(8,128)S(1)}, f32[64,1024]{1,0:T(8,128)S(1)}, u32[]{:S(2)}, u32[]{:S(2)}) collective-permute-start(f32[64,1024]{1,0:T(8,128)S(1)} %get-tuple-element.8), channel_id=1, source_target_pairs={{0,1},{1,4},{4,5},{5,8},{8,9},{9,12},{12,13},{2,3},{3,6},{6,7},{7,... | collective-permute-start | bytes 786440 | tf_op jit(solution)/shard_map/ppermute | solution.py:212
  3.5 14.5 %collective-permute-start.1 = (f32[64,1024]{1,0:T(8,128)S(1)}, f32[64,1024]{1,0:T(8,128)S(1)}, u32[]{:S(2)}, u32[]{:S(2)}) collective-permute-start(f32[64,1024]{1,0:T(8,128)S(1)} %get-tuple-element.7), channel_id=1, source_target_pairs={{1,0},{4,1},{5,4},{8,5},{9,8},{12,9},{13,12},{3,2},{6,3},{7,6},{10... | collective-permute-start | bytes 786440 | tf_op jit(solution)/shard_map/ppermute | solution.py:213
  7.5 17.2 %all-to-all-start = ((f32[16,8,192]{2,1,0:T(8,128)}), f32[16,8,192]{2,1,0:T(8,128)S(1)}, u32[]{:S(2)}, u32[]{:S(2)}) async-start(f32[16,8,192]{2,1,0:T(8,128)} %shard_map.55), calls=%async_computation | async-start | bytes 262144 | tf_op jit(solution)/shard_map/all_to_all | solution.py:207
  18.2 6.8 %collective-permute-start.2 = (f32[256,128]{1,0:T(8,128)S(1)}, f32[256,128]{1,0:T(8,128)S(1)}, u32[]{:S(2)}, u32[]{:S(2)}) collective-permute-start(f32[256,128]{1,0:T(8,128)S(1)} %pad_maximum_fusion), channel_id=1, source_target_pairs={{0,2},{2,0},{1,3},{3,1},{4,6},{6,4},{5,7},{7,5},{8,10},{10,8},{9,1... | collective-permute-start | bytes 393224 | tf_op jit(solution)/shard_map/ppermute | solution.py:218
  24.9 1.0 %copy-start = (f32[128,1024]{1,0:T(8,128)S(1)}, f32[128,1024]{1,0:T(8,128)}, u32[]{:S(2)}) copy-start(f32[128,1024]{1,0:T(8,128)} %base_ref.1) | copy-start | bytes 1572868

commit v2 on v1

v2 whole, which is shorter than its diff:
```python
import functools

import jax
import jax.numpy as jnp
from jax import lax
from jax.experimental import pallas as pl
from jax.experimental.pallas import tpu as pltpu
from jax.sharding import PartitionSpec as P

HALO = 64
LANES = 128
CODE = 4096
ROW_BIAS = 256
COL_BIAS = 1024
TINY = 1e-30
VMEM_LIMIT = 52 * 1024 * 1024
F32 = jnp.float32
BF16 = jnp.bfloat16


def side_tiles(cols):
    return min(cols - 1, 2)


def pieces_of(dest, rows, cols):
    row, col, claim = dest
    other = row - 1 if claim == 0 else row + 1
    sides = [(col, 0)]
    if cols == 2:
        sides.append((1 - col, -1 if col == 1 else 1))
    elif cols > 2:
        sides += [(col - 1, -1), (col + 1, 1)]
    found = []
    for tile_row, vertical in ((row, 0), (other, 1)):
        for tile_col, side in sides:
            there = 0 <= tile_row < rows and 0 <= tile_col < cols
            found.append((tile_row * cols + tile_col if there else None, vertical, side))
    return found


def pack_kernel(rows, cols, block_rows, block_cols, cell_ref, weight_ref, count_ref, out_ref):
    cell = cell_ref[0]
    tiles, slots = cell.shape
    slot = lax.broadcasted_iota(jnp.int32, (1, slots), 1)
    weights = [jnp.where(slot < count_ref[0, tile], weight_ref[0, tile : tile + 1, :], 0.0) for tile in range(tiles)]
    tile_row = lax.div(cell, block_cols)
    tile_col = lax.rem(cell, block_cols)
    codes = {}
    for claim in (0, 1):
        for vertical in (0, 1):
            if vertical:
                first = 2 * block_rows - HALO if claim == 0 else 0
            else:
                first = 0 if claim == 0 else block_rows - HALO
            for side in (-1, 0, 1):
                shift = {-1: HALO - block_cols, 0: 0, 1: HALO}[side]
                row_code = (tile_row + (ROW_BIAS - first)) * CODE
                codes[claim, vertical, side] = (row_code + tile_col + (shift + COL_BIAS)).astype(F32)
    zero = jnp.zeros((1, slots), F32)
    index = 0
    for row in range(rows):
        for col in range(cols):
            for claim in (0, 1):
                for place, (tile, vertical, side) in enumerate(pieces_of((row, col, claim), rows, cols)):
                    there = tile is not None
                    code = codes[claim, vertical, side][tile : tile + 1] if there else zero
                    out_ref[index, 2 * place : 2 * place + 1, :] = code
                    out_ref[index, 2 * place + 1 : 2 * place + 2, :] = weights[tile] if there else zero
                index += 1


def halves(value):
    high = value.astype(BF16)
    return high, (value - high.astype(F32)).astype(BF16)


def row_prefix(window, prefix):
    side, rows, _ = window.shape
    side -= 1
    lane = lax.broadcasted_iota(jnp.int32, (rows, LANES), 1)
    sub = lax.broadcasted_iota(jnp.int32, (rows // 8, 8, LANES), 1)
    before = window[side]
    for block in range(side + 1):
        after = window[side] if block == side else pltpu.roll(window[block], HALO, axis=1)
        cells = jnp.where(lane < HALO, before, after).reshape(-1, 8, LANES)
        before = after
        for hop in (1, 2, 4):
            cells = cells + jnp.where(sub >= hop, pltpu.roll(cells, hop, axis=1), 0.0)
        carry = jnp.zeros((8, LANES), F32)
        prefix[block, 0:8, :] = carry
        for tile in range(rows // 8):
            total = cells[tile] + carry
            prefix[block, 8 * tile + 8 : 8 * tile + 16, :] = total
            carry = jnp.broadcast_to(total[7:8], (8, LANES))


def band_of(half):
    here = lax.broadcasted_iota(jnp.int32, (LANES, LANES), 0)
    there = lax.broadcasted_iota(jnp.int32, (LANES, LANES), 1)
    gap = here - there
    both = [jnp.where(jnp.abs(gap + shift) <= half, 1.0, 0.0) for shift in (-HALO, LANES - HALO)]
    band = jnp.concatenate(both, axis=1).astype(BF16)
    return jnp.concatenate([band, band], axis=0)


def column_boxes(prefix, half, block_rows, use):
    band = band_of(half)
    before = None
    for block in range(prefix.shape[0]):
        lower = prefix[block, pl.ds(HALO + 8 + half, block_rows), :]
        upper = prefix[block, pl.ds(HALO + 7 - half, block_rows), :]
        product = jnp.dot(
            jnp.concatenate(halves(lower - upper), axis=1), band, preferred_element_type=F32
        )
        if block > 0:
            use(block - 1, before + product[:, LANES:])
        before = product[:, :LANES]


def lanes_of(block):
    return slice(block * LANES, (block + 1) * LANES)


def base_kernel(halves_ref, base_ref, above_ref, below_ref, beside_ref, out_ref, buffer, sems, window, prefix):
    block_rows, block_cols = base_ref.shape
    blocks = block_cols // LANES
    for block in range(blocks):
        window[block, 0:HALO, :] = above_ref[:, lanes_of(block)]
        window[block, HALO : HALO + block_rows, :] = base_ref[:, lanes_of(block)]
        window[block, HALO + block_rows :, :] = below_ref[:, lanes_of(block)]
    window[blocks] = beside_ref[...]
    row_prefix(window, prefix)
    sizes = buffer.shape[0]

    def one_size(step, _):
        def use(block, boxes):
            buffer[step, :, lanes_of(block)] = boxes

        column_boxes(prefix, halves_ref[step], block_rows, use)
        pltpu.make_async_copy(buffer.at[step], out_ref.at[step], sems.at[step]).start()
        return 0

    lax.fori_loop(0, sizes, one_size, 0, unroll=2)

    def finish(step, _):
        pltpu.make_async_copy(buffer.at[step], out_ref.at[step], sems.at[step]).wait()
        return 0

    lax.fori_loop(0, sizes, finish, 0)


def pack16(row):
    return jnp.broadcast_to(row.astype(F32), (16, row.shape[1])).astype(BF16)


def tall(packed, size):
    return jnp.concatenate([packed] * (size // 16), axis=0)


def scan_kernel(
    sides, halves_ref, got_ref, boxes_ref, out_ref, buffer, read_sems, write_sems,
    prefix, window, code_s, weight_s, row_hot, col_hot, own_acc, far_acc, side_acc, corner_acc,
):
    sizes, block_rows, block_cols = buffer.shape
    blocks = block_cols // LANES
    senders, _, slots = got_ref.shape
    chunks = senders * slots // LANES
    depth = row_hot.shape[1] // LANES
    own_rows = block_rows + HALO
    claim = lax.axis_index("claim")

    def read_of(step):
        return pltpu.make_async_copy(boxes_ref.at[step], buffer.at[step], read_sems.at[step])

    def write_of(step):
        return pltpu.make_async_copy(buffer.at[step], out_ref.at[step], write_sems.at[step])

    def begin(step, _):
        read_of(step).start()
        return 0

    lax.fori_loop(0, sizes, begin, 0)
    for place in range(2 * sides + 2):
        code = got_ref[:, 2 * place, :].astype(jnp.int32)
        weight = got_ref[:, 2 * place + 1, :]
        split = senders // 2
        for ref, value in ((code_s, code), (weight_s, weight)):
            ref[place, 0:senders, :] = value[:, :LANES]
            ref[place, senders : senders + split, 0 : slots - LANES] = value[:split, LANES:]
            ref[place, senders : senders + split, slots - LANES : LANES] = value[split:, LANES:]
    for acc in (own_acc, far_acc, side_acc, corner_acc):
        acc[...] = jnp.zeros_like(acc)
    target = {(0, False): own_acc, (1, False): far_acc, (0, True): side_acc, (1, True): corner_acc}
    one, none = jnp.ones((), BF16), jnp.zeros((), BF16)

    def add_chunk(chunk, _):
        for place in range(2 * sides + 2):
            vertical, side = divmod(place, sides + 1)
            rows = HALO if vertical else own_rows
            cols = LANES if side else block_cols
            code8 = code_s[place, pl.ds(pl.multiple_of(chunk * depth, depth), depth), :]
            weight8 = weight_s[place, pl.ds(pl.multiple_of(chunk * depth, depth), depth), :]
            row8 = lax.shift_right_logical(code8, 12) - ROW_BIAS
            col8 = (code8 & (CODE - 1)) - COL_BIAS
            high8 = weight8.astype(BF16).astype(F32)
            low8 = weight8 - high8
            row_iota = lax.broadcasted_iota(jnp.int32, (rows, LANES), 0).astype(F32).astype(BF16)
            col_iota = lax.broadcasted_iota(jnp.int32, (LANES, LANES), 0).astype(F32).astype(BF16)
            for part in range(depth):
                at = lanes_of(part)
                hit = tall(pack16(row8[part : part + 1]), rows) == row_iota
                row_hot[0:rows, at] = jnp.where(hit, tall(pack16(high8[part : part + 1]), rows), none)
                row_hot[rows : 2 * rows, at] = jnp.where(hit, tall(pack16(low8[part : part + 1]), rows), none)
                col = col8[part : part + 1]
                for block in range(cols // LANES):
                    inside = jnp.where(lax.shift_right_arithmetic(col, 7) == block, col & (LANES - 1), -1)
                    col_hot[lanes_of(block), at] = jnp.where(
                        tall(pack16(inside), LANES) == col_iota, one, none
                    )
            acc = target[vertical, side > 0]
            acc[...] += lax.dot_general(
                row_hot[0 : 2 * rows, :],
                col_hot[0:cols, :],
                (((1,), (1,)), ((), ())),
                preferred_element_type=F32,
            )
        return 0

    lax.fori_loop(0, chunks // depth, add_chunk, 0)
    own_at = pl.multiple_of((1 - claim) * HALO, HALO)
    far_at = pl.multiple_of(claim * own_rows, HALO)
    for block in range(blocks):
        here = lanes_of(block)
        window[block, pl.ds(own_at, own_rows), :] = own_acc[:own_rows, here] + own_acc[own_rows:, here]
        window[block, pl.ds(far_at, HALO), :] = far_acc[:HALO, here] + far_acc[HALO:, here]
    window[blocks, pl.ds(own_at, own_rows), :] = side_acc[:own_rows] + side_acc[own_rows:]
    window[blocks, pl.ds(far_at, HALO), :] = corner_acc[:HALO] + corner_acc[HALO:]
    row_prefix(window, prefix)

    def one_size(step, _):
        half = halves_ref[step]
        inverse = 1.0 / (2 * half + 1).astype(F32)
        read_of(step).wait()

        def use(block, counts):
            here = lanes_of(block)
            base = buffer[step, :, here]
            gain = jnp.log(jnp.maximum(counts, TINY)) - jnp.log(base) - 1.0
            buffer[step, :, here] = (counts * gain + base) * inverse

        column_boxes(prefix, half, block_rows, use)
        write_of(step).start()
        return 0

    lax.fori_loop(0, sizes, one_size, 0, unroll=2)

    def finish(step, _):
        write_of(step).wait()
        return 0

    lax.fori_loop(0, sizes, finish, 0)


def shards(rows, cols, claim_cell, claim_weight, claim_count, baseline, half_widths):
    block_rows, block_cols = baseline.shape
    slots = claim_cell.shape[2]
    sides = side_tiles(cols)
    devices = rows * cols * 2
    whole = pl.BlockSpec(memory_space=pltpu.VMEM)
    scalars = pl.BlockSpec(memory_space=pltpu.SMEM)
    sent = pl.pallas_call(
        functools.partial(pack_kernel, rows, cols, block_rows, block_cols),
        in_specs=[whole, whole, scalars],
        out_shape=jax.ShapeDtypeStruct((devices, 4 * (sides + 1), slots), F32),
    )(claim_cell, claim_weight, claim_count)
    got = lax.all_to_all(sent, ("row", "col", "claim"), split_axis=0, concat_axis=0, tiled=True)

    strips = rows * 2
    down = [(i, i + 1) for i in range(strips - 1)]
    up = [(i + 1, i) for i in range(strips - 1)]
    above = lax.ppermute(baseline[block_rows - HALO :], ("row", "claim"), down)
    below = lax.ppermute(baseline[:HALO], ("row", "claim"), up)
    pieces = (above, baseline, below)
    first = jnp.concatenate([piece[:, :HALO] for piece in pieces], axis=0)
    last = jnp.concatenate([piece[:, block_cols - HALO :] for piece in pieces], axis=0)
    if cols == 2:
        col = lax.axis_index("col")
        beside = lax.ppermute(
            jnp.concatenate([jnp.where(col == 0, last, 0.0), jnp.where(col == 1, first, 0.0)], axis=1),
            "col",
            [(0, 1), (1, 0)],
        )
    else:
        beside = jnp.concatenate(
            [
                lax.ppermute(last, "col", [(i, i + 1) for i in range(cols - 1)]),
                lax.ppermute(first, "col", [(i + 1, i) for i in range(cols - 1)]),
            ],
            axis=1,
        )
    sizes = half_widths.shape[0]
    blocks = block_cols // LANES
    places = 2 * (sides + 1)
    chunk_rows = devices * slots // LANES
    window = pltpu.VMEM((blocks + 1, 2 * block_rows, LANES), F32)
    prefix = pltpu.VMEM((blocks + 1, 2 * block_rows + 8, LANES), F32)
    field = (sizes, block_rows, block_cols)
    work = 2 * sizes * block_rows * (blocks + 1) * (2 * LANES) ** 2
    boxes = pl.pallas_call(
        base_kernel,
        in_specs=[scalars] + [whole] * 4,
        out_specs=pl.BlockSpec(memory_space=pltpu.HBM),
        out_shape=jax.ShapeDtypeStruct(field, F32),
        scratch_shapes=[pltpu.VMEM(field, F32), pltpu.SemaphoreType.DMA((sizes,)), window, prefix],
        cost_estimate=pl.CostEstimate(flops=work, bytes_accessed=4 * sizes * block_rows * block_cols, transcendentals=0),
        compiler_params=pltpu.CompilerParams(vmem_limit_bytes=VMEM_LIMIT),
    )(half_widths, baseline, above, below, beside)
    depth = 8 * LANES
    own_rows = block_rows + HALO
    return pl.pallas_call(
        functools.partial(scan_kernel, sides),
        in_specs=[scalars, whole, pl.BlockSpec(memory_space=pltpu.HBM)],
        out_specs=pl.BlockSpec(memory_space=pltpu.HBM),
        scratch_shapes=[
            pltpu.VMEM(field, F32),
            pltpu.SemaphoreType.DMA((sizes,)),
            pltpu.SemaphoreType.DMA((sizes,)),
            prefix,
            window,
            pltpu.VMEM((places, chunk_rows, LANES), jnp.int32),
            pltpu.VMEM((places, chunk_rows, LANES), F32),
            pltpu.VMEM((2 * own_rows, depth), BF16),
            pltpu.VMEM((block_cols, depth), BF16),
            pltpu.VMEM((2 * own_rows, block_cols), F32),
            pltpu.VMEM((2 * HALO, block_cols), F32),
            pltpu.VMEM((2 * own_rows, LANES), F32),
            pltpu.VMEM((2 * HALO, LANES), F32),
        ],
        out_shape=jax.ShapeDtypeStruct(field, F32),
        compiler_params=pltpu.CompilerParams(vmem_limit_bytes=VMEM_LIMIT),
    )(half_widths, got, boxes)


def solution(mesh):
    in_specs = (
        P(("groups", "row", "col", "claim"), None, None),
        P(("groups", "row", "col", "claim"), None, None),
        P(("groups", "row", "col", "claim"), None),
        P(("groups", "row", "claim"), "col"),
        P(),
    )
    out_specs = P(None, ("groups", "row", "claim"), "col")
    body = functools.partial(shards, mesh.shape["row"], mesh.shape["col"])
    return jax.shard_map(body, mesh=mesh, in_specs=in_specs, out_specs=out_specs, check_vma=False)
```

time: 49.4 us -> 46.9 us (0.949)
  waiting for transfers between devices: 4.07 us -> 0.1 us
  starting transfers between devices: 14.9 us -> 16.5 us
  Pallas kernels: 24.5 us -> 25.8 us
  other arithmetic: 0.93 us -> 0.13 us
  local copies, waits for them, and re-layouts: 4.54 us -> 3.88 us
    all_to_all x1, waiting for transfers between devices: 3.86 us -> 0.01 us  [shards(): lax.all_to_all(sent, ('row', 'col', 'claim'), split_axis=0, concat_axis=0...]
    reshape x1 -> x0, local copies, waits for them, and re-layouts: 1.32 us -> none  [shards(): claim_count.reshape(-1, 1)]
    pallas_call x1 -> x2, Pallas kernels: 23 us -> 24.3 us  [the longest x1 17.9 us: shards(): pl.pallas_call(functools.partial(scan_kernel, sides), in_specs=[scalars,...]
    slice x0 -> x3, local copies, waits for them, and re-layouts: none -> 1.11 us  [shards(): piece[:, block_cols - HALO:]]
    ppermute x1, starting transfers between devices: 1.98 us -> 3 us  [shards(): lax.ppermute(jnp.concatenate([jnp.where(col == 0, last, 0.0), jnp.where(c...]
    concatenate x1 -> x0, other arithmetic: 0.73 us -> none  [shards(): jnp.concatenate([lax.axis_index('claim').astype(jnp.int32)[None], half_wi...]
    ppermute x1, starting transfers between devices: 2.37 us -> 3.05 us  [shards(): above = lax.ppermute(baseline[block_rows - HALO:], ('row', 'claim'), down)]
    unnamed x4 -> x6, local copies, waits for them, and re-layouts: 2.14 us -> 1.7 us
  transfers between devices with their start and end apart: 4 -> 4, of which waited for: 2 -> 1; matrix products, arithmetic and copies ran while one was open for 7% -> 2% of each run, Pallas kernels for 3% -> 17%
where the time goes in v2:
time: 46.9 us; the launch traced here: 46.5 us
  Pallas kernels  25.8 us (55%)
  starting transfers between devices  16.5 us (35%)
  local copies, waits for them, and re-layouts  3.88 us (8%)
    pallas_call x1, Pallas kernels, shards(): pl.pallas_call(functools.partial(scan_kernel, sides), in_specs=[scalars,...  17.9 us
    all_to_all x1, starting transfers between devices, shards(): lax.all_to_all(sent, ('row', 'col', 'claim'), split_axis=0, concat_axis=0...  9.12 us
    pallas_call x1, Pallas kernels, shards(): pl.pallas_call(base_kernel, in_specs=[scalars] + [whole] * 4, out_specs=p...  6.45 us
    ppermute x1, starting transfers between devices, shards(): above = lax.ppermute(baseline[block_rows - HALO:], ('row', 'claim'), down)  3.05 us
    ppermute x1, starting transfers between devices, shards(): lax.ppermute(jnp.concatenate([jnp.where(col == 0, last, 0.0), jnp.where(c...  3 us
    unnamed x6, local copies, waits for them, and re-layouts  1.7 us
    pallas_call x1, Pallas kernels, shards(): pl.pallas_call(functools.partial(pack_kernel, rows, cols, block_rows, blo...  1.5 us
    ppermute x1, starting transfers between devices, shards(): below = lax.ppermute(baseline[:HALO], ('row', 'claim'), up)  1.29 us
  transfers between devices with their start and end apart: 4, of which 1 were waited for; matrix products, arithmetic and copies ran while one was open for 2% of the time, Pallas kernels for 17%

profile of v2, /device:TPU:0, one launch (start us, length us, event | category | flops | bytes accessed | tf_op | source)
XLA Modules:
  0.0 46.5 jit_solution(6426070337627738150)
XLA Ops:
  0.0 0.0 copy-start.2
  0.0 1.1 %fusion.1 = (f32[64,1024]{1,0:T(8,128)S(1)}, f32[64,1024]{1,0:T(8,128)S(1)}) fusion(f32[128,1024]{1,0:T(8,128)} %base_ref.1), kind=kLoop, calls=%fused_computation.4 | loop fusion | bytes 1048576 | tf_op jit(solution)/shard_map/slice | solution.py:282
  1.1 1.3 %collective-permute-start.1 = (f32[64,1024]{1,0:T(8,128)S(1)}, f32[64,1024]{1,0:T(8,128)S(1)}, u32[]{:S(2)}, u32[]{:S(2)}) collective-permute-start(f32[64,1024]{1,0:T(8,128)S(1)} %get-tuple-element.7), channel_id=1, source_target_pairs={{1,0},{4,1},{5,4},{8,5},{9,8},{12,9},{13,12},{3,2},{6,3},{7,6},{10... | collective-permute-start | bytes 786440 | tf_op jit(solution)/shard_map/ppermute | solution.py:282
  2.4 3.0 %collective-permute-start = (f32[64,1024]{1,0:T(8,128)S(1)}, f32[64,1024]{1,0:T(8,128)S(1)}, u32[]{:S(2)}, u32[]{:S(2)}) collective-permute-start(f32[64,1024]{1,0:T(8,128)S(1)} %get-tuple-element.8), channel_id=1, source_target_pairs={{0,1},{1,4},{4,5},{5,8},{8,9},{9,12},{12,13},{2,3},{3,6},{6,7},{7,... | collective-permute-start | bytes 786440 | tf_op jit(solution)/shard_map/ppermute | solution.py:281
  5.4 1.0 %fusion = (f32[128,64]{1,0:T(8,128)S(1)}, f32[128,64]{1,0:T(8,128)S(1)}) fusion(f32[128,1024]{1,0:T(8,128)} %base_ref.1), kind=kLoop, calls=%fused_computation.3 | loop fusion | bytes 131072 | tf_op jit(solution)/shard_map/slice | solution.py:285
  6.4 0.0 collective-permute-done.1.below_ref
  6.4 0.1 fusion.3
  6.5 0.1 collective-permute-done.above_ref
  6.6 0.1 fusion.2
  6.7 0.1 pad_maximum_fusion
  6.8 3.0 %collective-permute-start.2 = (f32[256,128]{1,0:T(8,128)S(1)}, f32[256,128]{1,0:T(8,128)S(1)}, u32[]{:S(2)}, u32[]{:S(2)}) collective-permute-start(f32[256,128]{1,0:T(8,128)S(1)} %pad_maximum_fusion), channel_id=1, source_target_pairs={{0,2},{2,0},{1,3},{3,1},{4,6},{6,4},{5,7},{7,5},{8,10},{10,8},{9,1... | collective-permute-start | bytes 393224 | tf_op jit(solution)/shard_map/ppermute | solution.py:288
  9.8 1.5 %shard_map.55 = f32[16,8,192]{2,1,0:T(8,128)} custom-call(s32[1,8,192]{2,1,0:T(8,128)} %cell_ref.1, f32[1,8,192]{2,1,0:T(8,128)} %weight_ref.1, s32[1,8]{1,0:T(1,128)} %count_ref.1), custom_call_target="tpu_custom_call" | custom-call | tf_op jit(solution)/shard_map/pallas_call | solution.py:271
  11.3 9.1 %all-to-all-start = ((f32[16,8,192]{2,1,0:T(8,128)}), f32[16,8,192]{2,1,0:T(8,128)S(1)}, u32[]{:S(2)}, u32[]{:S(2)}) async-start(f32[16,8,192]{2,1,0:T(8,128)} %shard_map.55), calls=%async_computation | async-start | bytes 262144 | tf_op jit(solution)/shard_map/all_to_all | solution.py:276
  20.4 0.0 collective-permute-done.2.beside_ref
  20.4 0.0 copy-start
  20.4 1.0 %copy-done = f32[128,1024]{1,0:T(8,128)S(1)} copy-done((f32[128,1024]{1,0:T(8,128)S(1)}, f32[128,1024]{1,0:T(8,128)}, u32[]{:S(2)}) %copy-start) | copy-done | bytes 524312
  21.5 0.0 copy-start.1
  21.5 0.7 %copy-done.1 = s32[16]{0:T(128)S(1)} copy-done((s32[16]{0:T(128)S(1)}, s32[16]{0:T(128)}, u32[]{:S(2)}) %copy-start.1) | copy-done | bytes 88
  22.1 6.5 %shard_map.56.boxes_ref = f32[16,128,1024]{2,1,0:T(8,128)} custom-call(s32[16]{0:T(128)S(1)} %copy-done.1, f32[128,1024]{1,0:T(8,128)S(1)} %copy-done, f32[64,1024]{1,0:T(8,128)S(1)} %collective-permute-done.above_ref, f32[64,1024]{1,0:T(8,128)S(1)} %collective-permute-done.1.below_ref, f32[256,128]{1,0:T(8,128)S(1)} %collective-permute-done.2.beside_ref), custom_call_target="tpu_custom_call" | custom-call | flops 2415919104 | bytes 8388608 | tf_op jit(solution)/shard_map/pallas_call | solution.py:309
  28.6 0.0 all-to-all-done.got_ref
  28.6 0.0 copy-done.2
  28.6 17.9 %shard_map.57 = f32[16,128,1024]{2,1,0:T(8,128)} custom-call(s32[16]{0:T(128)S(1)} %copy-done.2, f32[16,8,192]{2,1,0:T(8,128)S(1)} %all-to-all-done.got_ref, f32[16,128,1024]{2,1,0:T(8,128)} %shard_map.56.boxes_ref), custom_call_target="tpu_custom_call" | custom-call | tf_op jit(solution)/shard_map/pallas_call | solution.py:320
  (1 shorter events, 0.0 us)
Async XLA Ops:
  0.0 28.6 %copy-start.2 = (s32[16]{0:T(128)S(1)}, s32[16]{0:T(128)}, u32[]{:S(2)}) copy-start(s32[16]{0:T(128)} %halves_ref.3) | copy-start | bytes 196
  1.1 5.3 %collective-permute-start.1 = (f32[64,1024]{1,0:T(8,128)S(1)}, f32[64,1024]{1,0:T(8,128)S(1)}, u32[]{:S(2)}, u32[]{:S(2)}) collective-permute-start(f32[64,1024]{1,0:T(8,128)S(1)} %get-tuple-element.7), channel_id=1, source_target_pairs={{1,0},{4,1},{5,4},{8,5},{9,8},{12,9},{13,12},{3,2},{6,3},{7,6},{10... | collective-permute-start | bytes 786440 | tf_op jit(solution)/shard_map/ppermute | solution.py:282
  2.4 4.2 %collective-permute-start = (f32[64,1024]{1,0:T(8,128)S(1)}, f32[64,1024]{1,0:T(8,128)S(1)}, u32[]{:S(2)}, u32[]{:S(2)}) collective-permute-start(f32[64,1024]{1,0:T(8,128)S(1)} %get-tuple-element.8), channel_id=1, source_target_pairs={{0,1},{1,4},{4,5},{5,8},{8,9},{9,12},{12,13},{2,3},{3,6},{6,7},{7,... | collective-permute-start | bytes 786440 | tf_op jit(solution)/shard_map/ppermute | solution.py:281
  6.8 13.6 %collective-permute-start.2 = (f32[256,128]{1,0:T(8,128)S(1)}, f32[256,128]{1,0:T(8,128)S(1)}, u32[]{:S(2)}, u32[]{:S(2)}) collective-permute-start(f32[256,128]{1,0:T(8,128)S(1)} %pad_maximum_fusion), channel_id=1, source_target_pairs={{0,2},{2,0},{1,3},{3,1},{4,6},{6,4},{5,7},{7,5},{8,10},{10,8},{9,1... | collective-permute-start | bytes 393224 | tf_op jit(solution)/shard_map/ppermute | solution.py:288
  11.3 17.3 %all-to-all-start = ((f32[16,8,192]{2,1,0:T(8,128)}), f32[16,8,192]{2,1,0:T(8,128)S(1)}, u32[]{:S(2)}, u32[]{:S(2)}) async-start(f32[16,8,192]{2,1,0:T(8,128)} %shard_map.55), calls=%async_computation | async-start | bytes 262144 | tf_op jit(solution)/shard_map/all_to_all | solution.py:276
  20.4 1.0 %copy-start = (f32[128,1024]{1,0:T(8,128)S(1)}, f32[128,1024]{1,0:T(8,128)}, u32[]{:S(2)}) copy-start(f32[128,1024]{1,0:T(8,128)} %base_ref.1) | copy-start | bytes 1572868
  21.5 0.7 %copy-start.1 = (s32[16]{0:T(128)S(1)}, s32[16]{0:T(128)}, u32[]{:S(2)}) copy-start(s32[16]{0:T(128)} %halves_ref.3) | copy-start | bytes 196

commit v3 on v2

--- a/solution.py
+++ b/solution.py
@@ -158,14 +158,12 @@
 
 
 def scan_kernel(
-    sides, halves_ref, got_ref, boxes_ref, out_ref, buffer, read_sems, write_sems,
-    prefix, window, code_s, weight_s, row_hot, col_hot, own_acc, far_acc, side_acc, corner_acc,
+    sides, halves_ref, got_ref, boxes_ref, out_ref, buffer, read_sems, write_sems, prefix, window, code_s, weight_s, *spaces
 ):
     sizes, block_rows, block_cols = buffer.shape
     blocks = block_cols // LANES
+    pairs = blocks // 2
     senders, _, slots = got_ref.shape
-    chunks = senders * slots // LANES
-    depth = row_hot.shape[1] // LANES
     own_rows = block_rows + HALO
     claim = lax.axis_index("claim")
 
@@ -180,7 +178,8 @@
         return 0
 
     lax.fori_loop(0, sizes, begin, 0)
-    for place in range(2 * sides + 2):
+    places = 2 * sides + 2
+    for place in range(places):
         code = got_ref[:, 2 * place, :].astype(jnp.int32)
         weight = got_ref[:, 2 * place + 1, :]
         split = senders // 2
@@ -188,53 +187,67 @@
             ref[place, 0:senders, :] = value[:, :LANES]
             ref[place, senders : senders + split, 0 : slots - LANES] = value[:split, LANES:]
             ref[place, senders : senders + split, slots - LANES : LANES] = value[split:, LANES:]
-    for acc in (own_acc, far_acc, side_acc, corner_acc):
-        acc[...] = jnp.zeros_like(acc)
-    target = {(0, False): own_acc, (1, False): far_acc, (0, True): side_acc, (1, True): corner_acc}
+    depth = spaces[0].shape[1] // LANES
+    chunks = code_s.shape[1] // depth
     one, none = jnp.ones((), BF16), jnp.zeros((), BF16)
 
-    def add_chunk(chunk, _):
-        for place in range(2 * sides + 2):
+    def iota16(size):
+        return lax.broadcasted_iota(jnp.int32, (size, LANES), 0).astype(F32).astype(BF16)
+
+    def add_chunk(chunk, fresh):
+        for place in range(places):
             vertical, side = divmod(place, sides + 1)
+            kind = 2 * vertical + (side > 0)
+            row_hot, col_hot, acc = spaces[3 * kind : 3 * kind + 3]
             rows = HALO if vertical else own_rows
-            cols = LANES if side else block_cols
-            code8 = code_s[place, pl.ds(pl.multiple_of(chunk * depth, depth), depth), :]
-            weight8 = weight_s[place, pl.ds(pl.multiple_of(chunk * depth, depth), depth), :]
-            row8 = lax.shift_right_logical(code8, 12) - ROW_BIAS
-            col8 = (code8 & (CODE - 1)) - COL_BIAS
-            high8 = weight8.astype(BF16).astype(F32)
-            low8 = weight8 - high8
-            row_iota = lax.broadcasted_iota(jnp.int32, (rows, LANES), 0).astype(F32).astype(BF16)
-            col_iota = lax.broadcasted_iota(jnp.int32, (LANES, LANES), 0).astype(F32).astype(BF16)
+            here = pl.ds(pl.multiple_of(chunk * depth, 8), depth)
+            code = code_s[place, here, :]
+            weight = weight_s[place, here, :]
+            row = lax.shift_right_logical(code, 12) - ROW_BIAS
+            col = (code & (CODE - 1)) - COL_BIAS
+            high = weight.astype(BF16).astype(F32)
+            parts = (high, weight - high)
+            width = LANES if side else 2 * LANES
+            if side:
+                inside = jnp.where(lax.shift_right_arithmetic(col, 7) == 0, col, -1)
+            else:
+                inside = col & (2 * LANES - 1)
+                pair = lax.shift_right_arithmetic(col, 8)
+            row_iota, col_iota = iota16(rows), iota16(width)
             for part in range(depth):
-                at = lanes_of(part)
-                hit = tall(pack16(row8[part : part + 1]), rows) == row_iota
-                row_hot[0:rows, at] = jnp.where(hit, tall(pack16(high8[part : part + 1]), rows), none)
-                row_hot[rows : 2 * rows, at] = jnp.where(hit, tall(pack16(low8[part : part + 1]), rows), none)
-                col = col8[part : part + 1]
-                for block in range(cols // LANES):
-                    inside = jnp.where(lax.shift_right_arithmetic(col, 7) == block, col & (LANES - 1), -1)
-                    col_hot[lanes_of(block), at] = jnp.where(
-                        tall(pack16(inside), LANES) == col_iota, one, none
-                    )
-            acc = target[vertical, side > 0]
-            acc[...] += lax.dot_general(
-                row_hot[0 : 2 * rows, :],
-                col_hot[0:cols, :],
-                (((1,), (1,)), ((), ())),
-                preferred_element_type=F32,
+                at, only = lanes_of(part), slice(part, part + 1)
+                row_hit = tall(pack16(row[only]), rows) == row_iota
+                col_hit = tall(pack16(inside[only]), width) == col_iota
+                if side:
+                    row_hot[:, at] = jnp.where(row_hit, one, none)
+                    for index, value in enumerate(parts):
+                        col_hot[lanes_of(index), at] = jnp.where(col_hit, tall(pack16(value[only]), LANES), none)
+                else:
+                    col_hot[:, at] = jnp.where(col_hit, one, none)
+                    for group in range(pairs):
+                        for index, value in enumerate(parts):
+                            mine = jnp.where(pair[only] == group, value[only], 0.0)
+                            start = (2 * group + index) * rows
+                            row_hot[start : start + rows, at] = jnp.where(row_hit, tall(pack16(mine), rows), none)
+            product = lax.dot_general(
+                row_hot[...], col_hot[...], (((1,), (1,)), ((), ())), preferred_element_type=F32
             )
-        return 0
-
-    lax.fori_loop(0, chunks // depth, add_chunk, 0)
+            acc[...] = product if fresh and side < 2 else acc[...] + product
+        return 0
+
+    add_chunk(0, True)
+    if chunks > 1:
+        lax.fori_loop(1, chunks, lambda chunk, _: add_chunk(chunk, False), 0)
+    own_acc, side_acc, far_acc, corner_acc = spaces[2::3]
     own_at = pl.multiple_of((1 - claim) * HALO, HALO)
     far_at = pl.multiple_of(claim * own_rows, HALO)
     for block in range(blocks):
-        here = lanes_of(block)
-        window[block, pl.ds(own_at, own_rows), :] = own_acc[:own_rows, here] + own_acc[own_rows:, here]
-        window[block, pl.ds(far_at, HALO), :] = far_acc[:HALO, here] + far_acc[HALO:, here]
-    window[blocks, pl.ds(own_at, own_rows), :] = side_acc[:own_rows] + side_acc[own_rows:]
-    window[blocks, pl.ds(far_at, HALO), :] = corner_acc[:HALO] + corner_acc[HALO:]
+        group, here = block // 2, lanes_of(block % 2)
+        for acc, rows, start in ((own_acc, own_rows, own_at), (far_acc, HALO, far_at)):
+            top = 2 * group * rows
+            window[block, pl.ds(start, rows), :] = acc[top : top + rows, here] + acc[top + rows : top + 2 * rows, here]
+    window[blocks, pl.ds(own_at, own_rows), :] = side_acc[:, :LANES] + side_acc[:, LANES:]
+    window[blocks, pl.ds(far_at, HALO), :] = corner_acc[:, :LANES] + corner_acc[:, LANES:]
     row_prefix(window, prefix)
 
     def one_size(step, _):
@@ -273,13 +286,13 @@
         in_specs=[whole, whole, scalars],
         out_shape=jax.ShapeDtypeStruct((devices, 4 * (sides + 1), slots), F32),
     )(claim_cell, claim_weight, claim_count)
-    got = lax.all_to_all(sent, ("row", "col", "claim"), split_axis=0, concat_axis=0, tiled=True)
 
     strips = rows * 2
     down = [(i, i + 1) for i in range(strips - 1)]
     up = [(i + 1, i) for i in range(strips - 1)]
     above = lax.ppermute(baseline[block_rows - HALO :], ("row", "claim"), down)
     below = lax.ppermute(baseline[:HALO], ("row", "claim"), up)
+    sent, above, below = lax.optimization_barrier((sent, above, below))
     pieces = (above, baseline, below)
     first = jnp.concatenate([piece[:, :HALO] for piece in pieces], axis=0)
     last = jnp.concatenate([piece[:, block_cols - HALO :] for piece in pieces], axis=0)
@@ -298,6 +311,7 @@
             ],
             axis=1,
         )
+    got = lax.all_to_all(sent, ("row", "col", "claim"), split_axis=0, concat_axis=0, tiled=True)
     sizes = half_widths.shape[0]
     blocks = block_cols // LANES
     places = 2 * (sides + 1)
@@ -315,8 +329,15 @@
         cost_estimate=pl.CostEstimate(flops=work, bytes_accessed=4 * sizes * block_rows * block_cols, transcendentals=0),
         compiler_params=pltpu.CompilerParams(vmem_limit_bytes=VMEM_LIMIT),
     )(half_widths, baseline, above, below, beside)
-    depth = 8 * LANES
-    own_rows = block_rows + HALO
+    depth = LANES * max(d for d in (8, 16, 24) if chunk_rows % d == 0)
+    spaces = []
+    for rows in (block_rows + HALO, HALO):
+        for tall_rows in (rows * blocks, rows):
+            spaces += [
+                pltpu.VMEM((tall_rows, depth), BF16),
+                pltpu.VMEM((2 * LANES, depth), BF16),
+                pltpu.VMEM((tall_rows, 2 * LANES), F32),
+            ]
     return pl.pallas_call(
         functools.partial(scan_kernel, sides),
         in_specs=[scalars, whole, pl.BlockSpec(memory_space=pltpu.HBM)],
@@ -329,12 +350,7 @@
             window,
             pltpu.VMEM((places, chunk_rows, LANES), jnp.int32),
             pltpu.VMEM((places, chunk_rows, LANES), F32),
-            pltpu.VMEM((2 * own_rows, depth), BF16),
-            pltpu.VMEM((block_cols, depth), BF16),
-            pltpu.VMEM((2 * own_rows, block_cols), F32),
-            pltpu.VMEM((2 * HALO, block_cols), F32),
-            pltpu.VMEM((2 * own_rows, LANES), F32),
-            pltpu.VMEM((2 * HALO, LANES), F32),
+            *spaces,
         ],
         out_shape=jax.ShapeDtypeStruct(field, F32),
         compiler_params=pltpu.CompilerParams(vmem_limit_bytes=VMEM_LIMIT),

time: 46.9 us -> 41.8 us (0.89)
  Pallas kernels: 25.8 us -> 22.3 us
  starting transfers between devices: 16.5 us -> 15.1 us
    pallas_call x1, Pallas kernels: 17.9 us -> 14.3 us  [shards(): pl.pallas_call(functools.partial(scan_kernel, sides), in_specs=[scalars,...]
    all_to_all x1, starting transfers between devices: 9.12 us -> 7.77 us  [shards(): lax.all_to_all(sent, ('row', 'col', 'claim'), split_axis=0, concat_axis=0...]
    slice x3 -> x2, local copies, waits for them, and re-layouts: 1.11 us -> 1.03 us  [shards(): piece[:, block_cols - HALO:]]
  transfers between devices with their start and end apart: 4 -> 4, of which waited for: 1 -> 0; matrix products, arithmetic and copies ran while one was open for 2% -> 2% of each run, Pallas kernels for 17% -> 19%
where the time goes in v3:
time: 41.8 us; the launch traced here: 41.4 us
  Pallas kernels  22.3 us (53%)
  starting transfers between devices  15.1 us (36%)
  local copies, waits for them, and re-layouts  3.8 us (9%)
    pallas_call x1, Pallas kernels, shards(): pl.pallas_call(functools.partial(scan_kernel, sides), in_specs=[scalars,...  14.3 us
    all_to_all x1, starting transfers between devices, shards(): lax.all_to_all(sent, ('row', 'col', 'claim'), split_axis=0, concat_axis=0...  7.77 us
    pallas_call x1, Pallas kernels, shards(): pl.pallas_call(base_kernel, in_specs=[scalars] + [whole] * 4, out_specs=p...  6.44 us
    ppermute x1, starting transfers between devices, shards(): above = lax.ppermute(baseline[block_rows - HALO:], ('row', 'claim'), down)  3.05 us
    ppermute x1, starting transfers between devices, shards(): lax.ppermute(jnp.concatenate([jnp.where(col == 0, last, 0.0), jnp.where(c...  3 us
    unnamed x6, local copies, waits for them, and re-layouts  1.7 us
    pallas_call x1, Pallas kernels, shards(): pl.pallas_call(functools.partial(pack_kernel, rows, cols, block_rows, blo...  1.5 us
    ppermute x1, starting transfers between devices, shards(): below = lax.ppermute(baseline[:HALO], ('row', 'claim'), up)  1.29 us
  transfers between devices with their start and end apart: 4, of which 0 were waited for; matrix products, arithmetic and copies ran while one was open for 2% of the time, Pallas kernels for 19%

profile of v3, /device:TPU:0, one launch (start us, length us, event | category | flops | bytes accessed | tf_op | source)
XLA Modules:
  0.0 41.4 jit_solution(11743980127607532526)
XLA Ops:
  0.0 0.0 copy-start.2
  0.0 1.1 %fusion.1 = (f32[64,1024]{1,0:T(8,128)S(1)}, f32[64,1024]{1,0:T(8,128)S(1)}) fusion(f32[128,1024]{1,0:T(8,128)} %base_ref.1), kind=kLoop, calls=%fused_computation.4 | loop fusion | bytes 1048576 | tf_op jit(solution)/shard_map/slice | solution.py:294
  1.1 1.3 %collective-permute-start.1 = (f32[64,1024]{1,0:T(8,128)S(1)}, f32[64,1024]{1,0:T(8,128)S(1)}, u32[]{:S(2)}, u32[]{:S(2)}) collective-permute-start(f32[64,1024]{1,0:T(8,128)S(1)} %get-tuple-element.13), channel_id=1, source_target_pairs={{1,0},{4,1},{5,4},{8,5},{9,8},{12,9},{13,12},{3,2},{6,3},{7,6},{10... | collective-permute-start | bytes 786440 | tf_op jit(solution)/shard_map/ppermute | solution.py:294
  2.4 3.0 %collective-permute-start = (f32[64,1024]{1,0:T(8,128)S(1)}, f32[64,1024]{1,0:T(8,128)S(1)}, u32[]{:S(2)}, u32[]{:S(2)}) collective-permute-start(f32[64,1024]{1,0:T(8,128)S(1)} %get-tuple-element.14), channel_id=1, source_target_pairs={{0,1},{1,4},{4,5},{5,8},{8,9},{9,12},{12,13},{2,3},{3,6},{6,7},{7,... | collective-permute-start | bytes 786440 | tf_op jit(solution)/shard_map/ppermute | solution.py:293
  5.4 1.5 %shard_map.55 = f32[16,8,192]{2,1,0:T(8,128)} custom-call(s32[1,8,192]{2,1,0:T(8,128)} %cell_ref.1, f32[1,8,192]{2,1,0:T(8,128)} %weight_ref.1, s32[1,8]{1,0:T(1,128)} %count_ref.1), custom_call_target="tpu_custom_call" | custom-call | tf_op jit(solution)/shard_map/pallas_call | solution.py:284
  6.9 1.0 %fusion = (f32[128,64]{1,0:T(8,128)S(1)}, f32[128,64]{1,0:T(8,128)S(1)}) fusion(f32[128,1024]{1,0:T(8,128)} %base_ref.1), kind=kLoop, calls=%fused_computation.3 | loop fusion | bytes 131072 | tf_op jit(solution)/shard_map/slice | solution.py:298
  7.9 0.0 collective-permute-done.1.below_ref
  7.9 0.0 collective-permute-done.above_ref
  7.9 0.1 fusion.2
  8.1 0.1 pad_maximum_fusion
  8.2 3.0 %collective-permute-start.2 = (f32[256,128]{1,0:T(8,128)S(1)}, f32[256,128]{1,0:T(8,128)S(1)}, u32[]{:S(2)}, u32[]{:S(2)}) collective-permute-start(f32[256,128]{1,0:T(8,128)S(1)} %pad_maximum_fusion), channel_id=1, source_target_pairs={{0,2},{2,0},{1,3},{3,1},{4,6},{6,4},{5,7},{7,5},{8,10},{10,8},{9,1... | collective-permute-start | bytes 393224 | tf_op jit(solution)/shard_map/ppermute | solution.py:301
  11.2 7.8 %all-to-all-start = ((f32[16,8,192]{2,1,0:T(8,128)}), f32[16,8,192]{2,1,0:T(8,128)S(1)}, u32[]{:S(2)}, u32[]{:S(2)}) async-start(f32[16,8,192]{2,1,0:T(8,128)} %shard_map.55), calls=%async_computation | async-start | bytes 262144 | tf_op jit(solution)/shard_map/all_to_all | solution.py:314
  18.9 0.0 collective-permute-done.2.beside_ref
  19.0 0.0 copy-start
  19.0 1.0 %copy-done = f32[128,1024]{1,0:T(8,128)S(1)} copy-done((f32[128,1024]{1,0:T(8,128)S(1)}, f32[128,1024]{1,0:T(8,128)}, u32[]{:S(2)}) %copy-start) | copy-done | bytes 524312
  20.0 0.0 copy-start.1
  20.0 0.7 %copy-done.1 = s32[16]{0:T(128)S(1)} copy-done((s32[16]{0:T(128)S(1)}, s32[16]{0:T(128)}, u32[]{:S(2)}) %copy-start.1) | copy-done | bytes 88
  20.7 6.4 %shard_map.56.boxes_ref = f32[16,128,1024]{2,1,0:T(8,128)} custom-call(s32[16]{0:T(128)S(1)} %copy-done.1, f32[128,1024]{1,0:T(8,128)S(1)} %copy-done, f32[64,1024]{1,0:T(8,128)S(1)} %collective-permute-done.above_ref, f32[64,1024]{1,0:T(8,128)S(1)} %collective-permute-done.1.below_ref, f32[256,128]{1,0:T(8,128)S(1)} %collective-permute-done.2.beside_ref), custom_call_target="tpu_custom_call" | custom-call | flops 2415919104 | bytes 8388608 | tf_op jit(solution)/shard_map/pallas_call | solution.py:323
  27.1 0.0 all-to-all-done.got_ref
  27.1 0.0 copy-done.2
  27.1 14.3 %shard_map.57 = f32[16,128,1024]{2,1,0:T(8,128)} custom-call(s32[16]{0:T(128)S(1)} %copy-done.2, f32[16,8,192]{2,1,0:T(8,128)S(1)} %all-to-all-done.got_ref, f32[16,128,1024]{2,1,0:T(8,128)} %shard_map.56.boxes_ref), custom_call_target="tpu_custom_call" | custom-call | tf_op jit(solution)/shard_map/pallas_call | solution.py:341
  (2 shorter events, 0.0 us)
Async XLA Ops:
  0.0 27.1 %copy-start.2 = (s32[16]{0:T(128)S(1)}, s32[16]{0:T(128)}, u32[]{:S(2)}) copy-start(s32[16]{0:T(128)} %halves_ref.3) | copy-start | bytes 196
  1.1 6.8 %collective-permute-start.1 = (f32[64,1024]{1,0:T(8,128)S(1)}, f32[64,1024]{1,0:T(8,128)S(1)}, u32[]{:S(2)}, u32[]{:S(2)}) collective-permute-start(f32[64,1024]{1,0:T(8,128)S(1)} %get-tuple-element.13), channel_id=1, source_target_pairs={{1,0},{4,1},{5,4},{8,5},{9,8},{12,9},{13,12},{3,2},{6,3},{7,6},{10... | collective-permute-start | bytes 786440 | tf_op jit(solution)/shard_map/ppermute | solution.py:294
  2.4 5.5 %collective-permute-start = (f32[64,1024]{1,0:T(8,128)S(1)}, f32[64,1024]{1,0:T(8,128)S(1)}, u32[]{:S(2)}, u32[]{:S(2)}) collective-permute-start(f32[64,1024]{1,0:T(8,128)S(1)} %get-tuple-element.14), channel_id=1, source_target_pairs={{0,1},{1,4},{4,5},{5,8},{8,9},{9,12},{12,13},{2,3},{3,6},{6,7},{7,... | collective-permute-start | bytes 786440 | tf_op jit(solution)/shard_map/ppermute | solution.py:293
  8.2 10.8 %collective-permute-start.2 = (f32[256,128]{1,0:T(8,128)S(1)}, f32[256,128]{1,0:T(8,128)S(1)}, u32[]{:S(2)}, u32[]{:S(2)}) collective-permute-start(f32[256,128]{1,0:T(8,128)S(1)} %pad_maximum_fusion), channel_id=1, source_target_pairs={{0,2},{2,0},{1,3},{3,1},{4,6},{6,4},{5,7},{7,5},{8,10},{10,8},{9,1... | collective-permute-start | bytes 393224 | tf_op jit(solution)/shard_map/ppermute | solution.py:301
  11.2 15.9 %all-to-all-start = ((f32[16,8,192]{2,1,0:T(8,128)}), f32[16,8,192]{2,1,0:T(8,128)S(1)}, u32[]{:S(2)}, u32[]{:S(2)}) async-start(f32[16,8,192]{2,1,0:T(8,128)} %shard_map.55), calls=%async_computation | async-start | bytes 262144 | tf_op jit(solution)/shard_map/all_to_all | solution.py:314
  19.0 1.0 %copy-start = (f32[128,1024]{1,0:T(8,128)S(1)}, f32[128,1024]{1,0:T(8,128)}, u32[]{:S(2)}) copy-start(f32[128,1024]{1,0:T(8,128)} %base_ref.1) | copy-start | bytes 1572868
  20.0 0.7 %copy-start.1 = (s32[16]{0:T(128)S(1)}, s32[16]{0:T(128)}, u32[]{:S(2)}) copy-start(s32[16]{0:T(128)} %halves_ref.3) | copy-start | bytes 196

commit v4 on v3

--- a/solution.py
+++ b/solution.py
@@ -13,7 +13,8 @@
 ROW_BIAS = 256
 COL_BIAS = 1024
 TINY = 1e-30
-VMEM_LIMIT = 52 * 1024 * 1024
+BIN_VMEM = 36 * 1024 * 1024
+SCAN_VMEM = 24 * 1024 * 1024
 F32 = jnp.float32
 BF16 = jnp.bfloat16
 
@@ -103,50 +104,18 @@
     return jnp.concatenate([band, band], axis=0)
 
 
-def column_boxes(prefix, half, block_rows, use):
-    band = band_of(half)
-    before = None
-    for block in range(prefix.shape[0]):
-        lower = prefix[block, pl.ds(HALO + 8 + half, block_rows), :]
-        upper = prefix[block, pl.ds(HALO + 7 - half, block_rows), :]
-        product = jnp.dot(
-            jnp.concatenate(halves(lower - upper), axis=1), band, preferred_element_type=F32
-        )
-        if block > 0:
-            use(block - 1, before + product[:, LANES:])
-        before = product[:, :LANES]
-
-
 def lanes_of(block):
     return slice(block * LANES, (block + 1) * LANES)
 
 
-def base_kernel(halves_ref, base_ref, above_ref, below_ref, beside_ref, out_ref, buffer, sems, window, prefix):
+def strips_kernel(sent_ref, base_ref, top_ref, bottom_ref, edges_ref):
     block_rows, block_cols = base_ref.shape
-    blocks = block_cols // LANES
-    for block in range(blocks):
-        window[block, 0:HALO, :] = above_ref[:, lanes_of(block)]
-        window[block, HALO : HALO + block_rows, :] = base_ref[:, lanes_of(block)]
-        window[block, HALO + block_rows :, :] = below_ref[:, lanes_of(block)]
-    window[blocks] = beside_ref[...]
-    row_prefix(window, prefix)
-    sizes = buffer.shape[0]
-
-    def one_size(step, _):
-        def use(block, boxes):
-            buffer[step, :, lanes_of(block)] = boxes
-
-        column_boxes(prefix, halves_ref[step], block_rows, use)
-        pltpu.make_async_copy(buffer.at[step], out_ref.at[step], sems.at[step]).start()
-        return 0
-
-    lax.fori_loop(0, sizes, one_size, 0, unroll=2)
-
-    def finish(step, _):
-        pltpu.make_async_copy(buffer.at[step], out_ref.at[step], sems.at[step]).wait()
-        return 0
-
-    lax.fori_loop(0, sizes, finish, 0)
+    top_ref[...] = base_ref[:HALO]
+    bottom_ref[...] = base_ref[block_rows - HALO :]
+    lane = lax.broadcasted_iota(jnp.int32, (block_rows, LANES), 1)
+    last = pltpu.roll(base_ref[:, block_cols - LANES :], HALO, axis=1)
+    first = pltpu.roll(base_ref[:, :LANES], HALO, axis=1)
+    edges_ref[...] = jnp.where(lane < HALO, last, first)
 
 
 def pack16(row):
@@ -157,27 +126,13 @@
     return jnp.concatenate([packed] * (size // 16), axis=0)
 
 
-def scan_kernel(
-    sides, halves_ref, got_ref, boxes_ref, out_ref, buffer, read_sems, write_sems, prefix, window, code_s, weight_s, *spaces
-):
-    sizes, block_rows, block_cols = buffer.shape
-    blocks = block_cols // LANES
+def bin_kernel(sides, got_ref, prefix, window, code_s, weight_s, *spaces):
+    blocks = window.shape[0] - 1
+    block_rows = window.shape[1] // 2
     pairs = blocks // 2
     senders, _, slots = got_ref.shape
     own_rows = block_rows + HALO
     claim = lax.axis_index("claim")
-
-    def read_of(step):
-        return pltpu.make_async_copy(boxes_ref.at[step], buffer.at[step], read_sems.at[step])
-
-    def write_of(step):
-        return pltpu.make_async_copy(buffer.at[step], out_ref.at[step], write_sems.at[step])
-
-    def begin(step, _):
-        read_of(step).start()
-        return 0
-
-    lax.fori_loop(0, sizes, begin, 0)
     places = 2 * sides + 2
     for place in range(places):
         code = got_ref[:, 2 * place, :].astype(jnp.int32)
@@ -250,25 +205,47 @@
     window[blocks, pl.ds(far_at, HALO), :] = corner_acc[:, :LANES] + corner_acc[:, LANES:]
     row_prefix(window, prefix)
 
+
+def scan_kernel(
+    group, halves_ref, counts_ref, base_ref, above_ref, below_ref, beside_ref, out_ref, buffer, sems, window, prefix
+):
+    sizes, block_rows, block_cols = buffer.shape
+    blocks = block_cols // LANES
+    for block in range(blocks):
+        window[block, 0:HALO, :] = above_ref[:, lanes_of(block)]
+        window[block, HALO : HALO + block_rows, :] = base_ref[:, lanes_of(block)]
+        window[block, HALO + block_rows :, :] = below_ref[:, lanes_of(block)]
+    window[blocks] = beside_ref[...]
+    row_prefix(window, prefix)
+
     def one_size(step, _):
         half = halves_ref[step]
         inverse = 1.0 / (2 * half + 1).astype(F32)
-        read_of(step).wait()
-
-        def use(block, counts):
-            here = lanes_of(block)
-            base = buffer[step, :, here]
-            gain = jnp.log(jnp.maximum(counts, TINY)) - jnp.log(base) - 1.0
-            buffer[step, :, here] = (counts * gain + base) * inverse
-
-        column_boxes(prefix, half, block_rows, use)
-        write_of(step).start()
+        band = band_of(half)
+        before = None
+        for first in range(0, blocks + 1, group):
+            some = range(first, min(first + group, blocks + 1))
+            strips = []
+            for block in some:
+                for field in (counts_ref, prefix):
+                    lower = field[block, pl.ds(HALO + 8 + half, block_rows), :]
+                    upper = field[block, pl.ds(HALO + 7 - half, block_rows), :]
+                    strips.append(jnp.concatenate(halves(lower - upper), axis=1))
+            product = jnp.dot(jnp.concatenate(strips, axis=0), band, preferred_element_type=F32)
+            for index, block in enumerate(some):
+                now = [product[(2 * index + f) * block_rows : (2 * index + f + 1) * block_rows] for f in (0, 1)]
+                if block > 0:
+                    counts, base = (old[:, :LANES] + new[:, LANES:] for old, new in zip(before, now))
+                    gain = jnp.log(jnp.maximum(counts, TINY)) - jnp.log(base) - 1.0
+                    buffer[step, :, lanes_of(block - 1)] = (counts * gain + base) * inverse
+                before = now
+        pltpu.make_async_copy(buffer.at[step], out_ref.at[step], sems.at[step]).start()
         return 0
 
     lax.fori_loop(0, sizes, one_size, 0, unroll=2)
 
     def finish(step, _):
-        write_of(step).wait()
+        pltpu.make_async_copy(buffer.at[step], out_ref.at[step], sems.at[step]).wait()
         return 0
 
     lax.fori_loop(0, sizes, finish, 0)
@@ -287,15 +264,22 @@
         out_shape=jax.ShapeDtypeStruct((devices, 4 * (sides + 1), slots), F32),
     )(claim_cell, claim_weight, claim_count)
 
+    got = lax.all_to_all(sent, ("row", "col", "claim"), split_axis=0, concat_axis=0, tiled=True)
+    top, bottom, edges = pl.pallas_call(
+        strips_kernel,
+        in_specs=[pl.BlockSpec(memory_space=pltpu.HBM), whole],
+        out_specs=[whole] * 3,
+        out_shape=[
+            jax.ShapeDtypeStruct((HALO, block_cols), F32),
+            jax.ShapeDtypeStruct((HALO, block_cols), F32),
+            jax.ShapeDtypeStruct((block_rows, LANES), F32),
+        ],
+    )(sent, baseline)
     strips = rows * 2
-    down = [(i, i + 1) for i in range(strips - 1)]
-    up = [(i + 1, i) for i in range(strips - 1)]
-    above = lax.ppermute(baseline[block_rows - HALO :], ("row", "claim"), down)
-    below = lax.ppermute(baseline[:HALO], ("row", "claim"), up)
-    sent, above, below = lax.optimization_barrier((sent, above, below))
-    pieces = (above, baseline, below)
-    first = jnp.concatenate([piece[:, :HALO] for piece in pieces], axis=0)
-    last = jnp.concatenate([piece[:, block_cols - HALO :] for piece in pieces], axis=0)
+    above = lax.ppermute(bottom, ("row", "claim"), [(i, i + 1) for i in range(strips - 1)])
+    below = lax.ppermute(top, ("row", "claim"), [(i + 1, i) for i in range(strips - 1)])
+    last = jnp.concatenate([above[:, block_cols - HALO :], edges[:, :HALO], below[:, block_cols - HALO :]], axis=0)
+    first = jnp.concatenate([above[:, :HALO], edges[:, HALO:], below[:, :HALO]], axis=0)
     if cols == 2:
         col = lax.axis_index("col")
         beside = lax.ppermute(
@@ -311,50 +295,48 @@
             ],
             axis=1,
         )
-    got = lax.all_to_all(sent, ("row", "col", "claim"), split_axis=0, concat_axis=0, tiled=True)
     sizes = half_widths.shape[0]
     blocks = block_cols // LANES
     places = 2 * (sides + 1)
     chunk_rows = devices * slots // LANES
     window = pltpu.VMEM((blocks + 1, 2 * block_rows, LANES), F32)
-    prefix = pltpu.VMEM((blocks + 1, 2 * block_rows + 8, LANES), F32)
-    field = (sizes, block_rows, block_cols)
-    work = 2 * sizes * block_rows * (blocks + 1) * (2 * LANES) ** 2
-    boxes = pl.pallas_call(
-        base_kernel,
-        in_specs=[scalars] + [whole] * 4,
-        out_specs=pl.BlockSpec(memory_space=pltpu.HBM),
-        out_shape=jax.ShapeDtypeStruct(field, F32),
-        scratch_shapes=[pltpu.VMEM(field, F32), pltpu.SemaphoreType.DMA((sizes,)), window, prefix],
-        cost_estimate=pl.CostEstimate(flops=work, bytes_accessed=4 * sizes * block_rows * block_cols, transcendentals=0),
-        compiler_params=pltpu.CompilerParams(vmem_limit_bytes=VMEM_LIMIT),
-    )(half_widths, baseline, above, below, beside)
+    prefix = (blocks + 1, 2 * block_rows + 8, LANES)
     depth = LANES * max(d for d in (8, 16, 24) if chunk_rows % d == 0)
     spaces = []
-    for rows in (block_rows + HALO, HALO):
-        for tall_rows in (rows * blocks, rows):
+    for rows_of in (block_rows + HALO, HALO):
+        for tall_rows in (rows_of * blocks, rows_of):
             spaces += [
                 pltpu.VMEM((tall_rows, depth), BF16),
                 pltpu.VMEM((2 * LANES, depth), BF16),
                 pltpu.VMEM((tall_rows, 2 * LANES), F32),
             ]
-    return pl.pallas_call(
-        functools.partial(scan_kernel, sides),
-        in_specs=[scalars, whole, pl.BlockSpec(memory_space=pltpu.HBM)],
-        out_specs=pl.BlockSpec(memory_space=pltpu.HBM),
+    counts = pl.pallas_call(
+        functools.partial(bin_kernel, sides),
+        in_specs=[whole],
+        out_specs=whole,
+        out_shape=jax.ShapeDtypeStruct(prefix, F32),
         scratch_shapes=[
-            pltpu.VMEM(field, F32),
-            pltpu.SemaphoreType.DMA((sizes,)),
-            pltpu.SemaphoreType.DMA((sizes,)),
-            prefix,
             window,
             pltpu.VMEM((places, chunk_rows, LANES), jnp.int32),
             pltpu.VMEM((places, chunk_rows, LANES), F32),
             *spaces,
         ],
+        compiler_params=pltpu.CompilerParams(vmem_limit_bytes=BIN_VMEM),
+    )(got)
+    field = (sizes, block_rows, block_cols)
+    return pl.pallas_call(
+        functools.partial(scan_kernel, 3),
+        in_specs=[scalars] + [whole] * 5,
+        out_specs=pl.BlockSpec(memory_space=pltpu.HBM),
+        scratch_shapes=[
+            pltpu.VMEM(field, F32),
+            pltpu.SemaphoreType.DMA((sizes,)),
+            window,
+            pltpu.VMEM(prefix, F32),
+        ],
         out_shape=jax.ShapeDtypeStruct(field, F32),
-        compiler_params=pltpu.CompilerParams(vmem_limit_bytes=VMEM_LIMIT),
-    )(half_widths, got, boxes)
+        compiler_params=pltpu.CompilerParams(vmem_limit_bytes=SCAN_VMEM),
+    )(half_widths, counts, baseline, above, below, beside)
 
 
 def solution(mesh):

time: 41.8 us -> 41.5 us (level)
  the two profiles are of different devices: /device:TPU:0 before, /device:TPU:1 now
where the time goes in v4:
time: 41.5 us; the launch traced here: 41.2 us
  Pallas kernels  19.6 us (47%)
  starting transfers between devices  13 us (31%)
  waiting for transfers between devices  5.56 us (13%)
  local copies, waits for them, and re-layouts  2.84 us (7%)
    pallas_call x1, Pallas kernels, shards(): pl.pallas_call(functools.partial(scan_kernel, 3), in_specs=[scalars] + [w...  10.8 us
    ppermute x1, waiting for transfers between devices, shards(): lax.ppermute(top, ('row', 'claim'), [(i + 1, i) for i in range(strips - 1)])  5.55 us
    pallas_call x1, Pallas kernels, shards(): pl.pallas_call(functools.partial(bin_kernel, sides), in_specs=[whole], ou...  5.43 us
    all_to_all x1, starting transfers between devices, shards(): lax.all_to_all(sent, ('row', 'col', 'claim'), split_axis=0, concat_axis=0...  4.93 us
    ppermute x1, starting transfers between devices, shards(): lax.ppermute(bottom, ('row', 'claim'), [(i, i + 1) for i in range(strips...  4.58 us
    ppermute x1, starting transfers between devices, shards(): lax.ppermute(top, ('row', 'claim'), [(i + 1, i) for i in range(strips - 1)])  2.01 us
    pallas_call x1, Pallas kernels, shards(): pl.pallas_call(strips_kernel, in_specs=[pl.BlockSpec(memory_space=pltpu.H...  1.86 us
    unnamed x4, local copies, waits for them, and re-layouts  1.69 us
  transfers between devices with their start and end apart: 4, of which 1 were waited for; matrix products, arithmetic and copies ran while one was open for 3% of the time, Pallas kernels for 13%

profile of v4, /device:TPU:1, one launch (start us, length us, event | category | flops | bytes accessed | tf_op | source)
XLA Modules:
  0.0 41.2 jit_solution(9721894995432480290)
XLA Ops:
  0.0 1.5 %shard_map.55.sent_ref = f32[16,8,192]{2,1,0:T(8,128)} custom-call(s32[1,8,192]{2,1,0:T(8,128)} %cell_ref.1, f32[1,8,192]{2,1,0:T(8,128)} %weight_ref.1, s32[1,8]{1,0:T(1,128)} %count_ref.1), custom_call_target="tpu_custom_call" | custom-call | tf_op jit(solution)/shard_map/pallas_call | solution.py:261
  1.5 1.9 %shard_map.57 = (f32[64,1024]{1,0:T(8,128)}, f32[64,1024]{1,0:T(8,128)}, f32[128,128]{1,0:T(8,128)}) custom-call(f32[16,8,192]{2,1,0:T(8,128)} %shard_map.55.sent_ref, f32[128,1024]{1,0:T(8,128)} %base_ref.3), custom_call_target="tpu_custom_call" | custom-call | tf_op jit(solution)/shard_map/pallas_call | solution.py:268
  3.3 4.6 %collective-permute-start = (f32[64,1024]{1,0:T(8,128)}, f32[64,1024]{1,0:T(8,128)S(1)}, u32[]{:S(2)}, u32[]{:S(2)}) collective-permute-start(f32[64,1024]{1,0:T(8,128)} %get-tuple-element.8), channel_id=1, source_target_pairs={{0,1},{1,4},{4,5},{5,8},{8,9},{9,12},{12,13},{2,3},{3,6},{6,7},{7,... | collective-permute-start | bytes 786440 | tf_op jit(solution)/shard_map/ppermute | solution.py:279
  7.9 4.9 %all-to-all-start = ((f32[16,8,192]{2,1,0:T(8,128)}), f32[16,8,192]{2,1,0:T(8,128)S(1)}, u32[]{:S(2)}, u32[]{:S(2)}) async-start(f32[16,8,192]{2,1,0:T(8,128)} %shard_map.55.sent_ref), calls=%async_computation | async-start | bytes 262144 | tf_op jit(solution)/shard_map/all_to_all | solution.py:267
  12.9 2.0 %collective-permute-start.1 = (f32[64,1024]{1,0:T(8,128)}, f32[64,1024]{1,0:T(8,128)S(1)}, u32[]{:S(2)}, u32[]{:S(2)}) collective-permute-start(f32[64,1024]{1,0:T(8,128)} %get-tuple-element.9), channel_id=1, source_target_pairs={{1,0},{4,1},{5,4},{8,5},{9,8},{12,9},{13,12},{3,2},{6,3},{7,6},{10... | collective-permute-start | bytes 786440 | tf_op jit(solution)/shard_map/ppermute | solution.py:280
  14.9 1.0 %fusion.2 = (f32[128,64]{1,0:T(8,128)S(1)}, f32[128,64]{1,0:T(8,128)S(1)}) fusion(f32[128,128]{1,0:T(8,128)} %get-tuple-element.10), kind=kLoop, calls=%fused_computation.5 | loop fusion | bytes 131072 | tf_op jit(solution)/shard_map/slice | solution.py:281
  15.9 0.0 collective-permute-done.above_ref
  15.9 0.1 fusion
  16.0 5.6 %collective-permute-done.1.below_ref = f32[64,1024]{1,0:T(8,128)S(1)} collective-permute-done((f32[64,1024]{1,0:T(8,128)}, f32[64,1024]{1,0:T(8,128)S(1)}, u32[]{:S(2)}, u32[]{:S(2)}) %collective-permute-start.1) | collective-permute-done | bytes 262176 | tf_op jit(solution)/shard_map/ppermute | solution.py:280
  21.5 0.1 fusion.1
  21.6 0.1 pad_maximum_fusion
  21.7 1.5 %collective-permute-start.2 = (f32[256,128]{1,0:T(8,128)S(1)}, f32[256,128]{1,0:T(8,128)S(1)}, u32[]{:S(2)}, u32[]{:S(2)}) collective-permute-start(f32[256,128]{1,0:T(8,128)S(1)} %pad_maximum_fusion), channel_id=1, source_target_pairs={{0,2},{2,0},{1,3},{3,1},{4,6},{6,4},{5,7},{7,5},{8,10},{10,8},{9,1... | collective-permute-start | bytes 393224 | tf_op jit(solution)/shard_map/ppermute | solution.py:285
  23.2 0.0 all-to-all-done.got_ref
  23.2 5.4 %shard_map.56.counts_ref = f32[9,264,128]{2,1,0:T(8,128)S(1)} custom-call(f32[16,8,192]{2,1,0:T(8,128)S(1)} %all-to-all-done.got_ref), custom_call_target="tpu_custom_call" | custom-call | tf_op jit(solution)/shard_map/pallas_call | solution.py:313
  28.7 0.0 collective-permute-done.2.beside_ref
  28.7 0.0 copy-start
  28.7 1.0 %copy-done = f32[128,1024]{1,0:T(8,128)S(1)} copy-done((f32[128,1024]{1,0:T(8,128)S(1)}, f32[128,1024]{1,0:T(8,128)}, u32[]{:S(2)}) %copy-start) | copy-done | bytes 524312
  29.7 0.0 copy-start.1
  29.7 0.7 %copy-done.1 = s32[16]{0:T(128)S(1)} copy-done((s32[16]{0:T(128)S(1)}, s32[16]{0:T(128)}, u32[]{:S(2)}) %copy-start.1) | copy-done | bytes 88
  30.4 10.8 %shard_map.58 = f32[16,128,1024]{2,1,0:T(8,128)} custom-call(s32[16]{0:T(128)S(1)} %copy-done.1, f32[9,264,128]{2,1,0:T(8,128)S(1)} %shard_map.56.counts_ref, f32[128,1024]{1,0:T(8,128)S(1)} %copy-done, f32[64,1024]{1,0:T(8,128)S(1)} %collective-permute-done.above_ref, f32[64,1024]{1,0:T(8,128)S(1)} %collective-permute-done.1.below_ref, ...), custom_call_target="tpu_custom_call" | custom-call | tf_op jit(solution)/shard_map/pallas_call | solution.py:327
  (1 shorter events, 0.0 us)
Async XLA Ops:
  3.3 12.5 %collective-permute-start = (f32[64,1024]{1,0:T(8,128)}, f32[64,1024]{1,0:T(8,128)S(1)}, u32[]{:S(2)}, u32[]{:S(2)}) collective-permute-start(f32[64,1024]{1,0:T(8,128)} %get-tuple-element.8), channel_id=1, source_target_pairs={{0,1},{1,4},{4,5},{5,8},{8,9},{9,12},{12,13},{2,3},{3,6},{6,7},{7,... | collective-permute-start | bytes 786440 | tf_op jit(solution)/shard_map/ppermute | solution.py:279
  7.9 15.3 %all-to-all-start = ((f32[16,8,192]{2,1,0:T(8,128)}), f32[16,8,192]{2,1,0:T(8,128)S(1)}, u32[]{:S(2)}, u32[]{:S(2)}) async-start(f32[16,8,192]{2,1,0:T(8,128)} %shard_map.55.sent_ref), calls=%async_computation | async-start | bytes 262144 | tf_op jit(solution)/shard_map/all_to_all | solution.py:267
  12.9 8.6 %collective-permute-start.1 = (f32[64,1024]{1,0:T(8,128)}, f32[64,1024]{1,0:T(8,128)S(1)}, u32[]{:S(2)}, u32[]{:S(2)}) collective-permute-start(f32[64,1024]{1,0:T(8,128)} %get-tuple-element.9), channel_id=1, source_target_pairs={{1,0},{4,1},{5,4},{8,5},{9,8},{12,9},{13,12},{3,2},{6,3},{7,6},{10... | collective-permute-start | bytes 786440 | tf_op jit(solution)/shard_map/ppermute | solution.py:280
  21.7 6.9 %collective-permute-start.2 = (f32[256,128]{1,0:T(8,128)S(1)}, f32[256,128]{1,0:T(8,128)S(1)}, u32[]{:S(2)}, u32[]{:S(2)}) collective-permute-start(f32[256,128]{1,0:T(8,128)S(1)} %pad_maximum_fusion), channel_id=1, source_target_pairs={{0,2},{2,0},{1,3},{3,1},{4,6},{6,4},{5,7},{7,5},{8,10},{10,8},{9,1... | collective-permute-start | bytes 393224 | tf_op jit(solution)/shard_map/ppermute | solution.py:285
  28.7 1.0 %copy-start = (f32[128,1024]{1,0:T(8,128)S(1)}, f32[128,1024]{1,0:T(8,128)}, u32[]{:S(2)}) copy-start(f32[128,1024]{1,0:T(8,128)} %base_ref.3) | copy-start | bytes 1572868
  29.7 0.7 %copy-start.1 = (s32[16]{0:T(128)S(1)}, s32[16]{0:T(128)}, u32[]{:S(2)}) copy-start(s32[16]{0:T(128)} %halves_ref.1) | copy-start | bytes 196

commit v5 on v4

--- a/solution.py
+++ b/solution.py
@@ -13,6 +13,7 @@
 ROW_BIAS = 256
 COL_BIAS = 1024
 TINY = 1e-30
+BASE_VMEM = 8 * 1024 * 1024
 BIN_VMEM = 36 * 1024 * 1024
 SCAN_VMEM = 24 * 1024 * 1024
 F32 = jnp.float32
@@ -108,14 +109,17 @@
     return slice(block * LANES, (block + 1) * LANES)
 
 
-def strips_kernel(sent_ref, base_ref, top_ref, bottom_ref, edges_ref):
+def base_kernel(halves_ref, base_ref, above_ref, below_ref, beside_ref, prefix, halves_out, window):
     block_rows, block_cols = base_ref.shape
-    top_ref[...] = base_ref[:HALO]
-    bottom_ref[...] = base_ref[block_rows - HALO :]
-    lane = lax.broadcasted_iota(jnp.int32, (block_rows, LANES), 1)
-    last = pltpu.roll(base_ref[:, block_cols - LANES :], HALO, axis=1)
-    first = pltpu.roll(base_ref[:, :LANES], HALO, axis=1)
-    edges_ref[...] = jnp.where(lane < HALO, last, first)
+    blocks = block_cols // LANES
+    for step in range(halves_ref.shape[0]):
+        halves_out[step] = halves_ref[step]
+    for block in range(blocks):
+        window[block, 0:HALO, :] = above_ref[:, lanes_of(block)]
+        window[block, HALO : HALO + block_rows, :] = base_ref[:, lanes_of(block)]
+        window[block, HALO + block_rows :, :] = below_ref[:, lanes_of(block)]
+    window[blocks] = beside_ref[...]
+    row_prefix(window, prefix)
 
 
 def pack16(row):
@@ -206,17 +210,9 @@
     row_prefix(window, prefix)
 
 
-def scan_kernel(
-    group, halves_ref, counts_ref, base_ref, above_ref, below_ref, beside_ref, out_ref, buffer, sems, window, prefix
-):
+def scan_kernel(group, halves_ref, counts_ref, prefix_ref, out_ref, buffer, sems):
     sizes, block_rows, block_cols = buffer.shape
     blocks = block_cols // LANES
-    for block in range(blocks):
-        window[block, 0:HALO, :] = above_ref[:, lanes_of(block)]
-        window[block, HALO : HALO + block_rows, :] = base_ref[:, lanes_of(block)]
-        window[block, HALO + block_rows :, :] = below_ref[:, lanes_of(block)]
-    window[blocks] = beside_ref[...]
-    row_prefix(window, prefix)
 
     def one_size(step, _):
         half = halves_ref[step]
@@ -227,7 +223,7 @@
             some = range(first, min(first + group, blocks + 1))
             strips = []
             for block in some:
-                for field in (counts_ref, prefix):
+                for field in (counts_ref, prefix_ref):
                     lower = field[block, pl.ds(HALO + 8 + half, block_rows), :]
                     upper = field[block, pl.ds(HALO + 7 - half, block_rows), :]
                     strips.append(jnp.concatenate(halves(lower - upper), axis=1))
@@ -264,22 +260,14 @@
         out_shape=jax.ShapeDtypeStruct((devices, 4 * (sides + 1), slots), F32),
     )(claim_cell, claim_weight, claim_count)
 
+    strips = rows * 2
+    above = lax.ppermute(baseline[block_rows - HALO :], ("row", "claim"), [(i, i + 1) for i in range(strips - 1)])
+    below = lax.ppermute(baseline[:HALO], ("row", "claim"), [(i + 1, i) for i in range(strips - 1)])
+    sent, _, _ = lax.optimization_barrier((sent, above, below))
     got = lax.all_to_all(sent, ("row", "col", "claim"), split_axis=0, concat_axis=0, tiled=True)
-    top, bottom, edges = pl.pallas_call(
-        strips_kernel,
-        in_specs=[pl.BlockSpec(memory_space=pltpu.HBM), whole],
-        out_specs=[whole] * 3,
-        out_shape=[
-            jax.ShapeDtypeStruct((HALO, block_cols), F32),
-            jax.ShapeDtypeStruct((HALO, block_cols), F32),
-            jax.ShapeDtypeStruct((block_rows, LANES), F32),
-        ],
-    )(sent, baseline)
-    strips = rows * 2
-    above = lax.ppermute(bottom, ("row", "claim"), [(i, i + 1) for i in range(strips - 1)])
-    below = lax.ppermute(top, ("row", "claim"), [(i + 1, i) for i in range(strips - 1)])
-    last = jnp.concatenate([above[:, block_cols - HALO :], edges[:, :HALO], below[:, block_cols - HALO :]], axis=0)
-    first = jnp.concatenate([above[:, :HALO], edges[:, HALO:], below[:, :HALO]], axis=0)
+    pieces = (above, baseline, below)
+    first = jnp.concatenate([piece[:, :HALO] for piece in pieces], axis=0)
+    last = jnp.concatenate([piece[:, block_cols - HALO :] for piece in pieces], axis=0)
     if cols == 2:
         col = lax.axis_index("col")
         beside = lax.ppermute(
@@ -310,6 +298,15 @@
                 pltpu.VMEM((2 * LANES, depth), BF16),
                 pltpu.VMEM((tall_rows, 2 * LANES), F32),
             ]
+    base, half_widths = pl.pallas_call(
+        base_kernel,
+        in_specs=[scalars] + [whole] * 4,
+        out_specs=[whole, scalars],
+        out_shape=[jax.ShapeDtypeStruct(prefix, F32), jax.ShapeDtypeStruct(half_widths.shape, jnp.int32)],
+        scratch_shapes=[window],
+        cost_estimate=pl.CostEstimate(flops=0, bytes_accessed=8 * 1024 * 1024, transcendentals=0),
+        compiler_params=pltpu.CompilerParams(vmem_limit_bytes=BASE_VMEM),
+    )(half_widths, baseline, above, below, beside)
     counts = pl.pallas_call(
         functools.partial(bin_kernel, sides),
         in_specs=[whole],
@@ -326,17 +323,12 @@
     field = (sizes, block_rows, block_cols)
     return pl.pallas_call(
         functools.partial(scan_kernel, 3),
-        in_specs=[scalars] + [whole] * 5,
+        in_specs=[scalars, whole, whole],
         out_specs=pl.BlockSpec(memory_space=pltpu.HBM),
-        scratch_shapes=[
-            pltpu.VMEM(field, F32),
-            pltpu.SemaphoreType.DMA((sizes,)),
-            window,
-            pltpu.VMEM(prefix, F32),
-        ],
+        scratch_shapes=[pltpu.VMEM(field, F32), pltpu.SemaphoreType.DMA((sizes,))],
         out_shape=jax.ShapeDtypeStruct(field, F32),
         compiler_params=pltpu.CompilerParams(vmem_limit_bytes=SCAN_VMEM),
-    )(half_widths, counts, baseline, above, below, beside)
+    )(half_widths, counts, base)
 
 
 def solution(mesh):

time: 41.5 us -> 42.8 us (1.031)
  the two profiles are of different devices: /device:TPU:1 before, /device:TPU:0 now
where the time goes in v5:
time: 42.8 us; the launch traced here: 42.5 us
  Pallas kernels  18.7 us (44%)
  starting transfers between devices  17.3 us (40%)
  waiting for transfers between devices  4.88 us (11%)
  local copies, waits for them, and re-layouts  1.36 us (3%)
    all_to_all x1, starting transfers between devices, shards(): lax.all_to_all(sent, ('row', 'col', 'claim'), split_axis=0, concat_axis=0...  11 us
    pallas_call x1, Pallas kernels, shards(): pl.pallas_call(functools.partial(scan_kernel, 3), in_specs=[scalars, whol...  10.3 us
    pallas_call x1, Pallas kernels, shards(): pl.pallas_call(functools.partial(bin_kernel, sides), in_specs=[whole], ou...  5.44 us
    ppermute x1, waiting for transfers between devices, shards(): lax.ppermute(jnp.concatenate([jnp.where(col == 0, last, 0.0), jnp.where(c...  4.87 us
    ppermute x1, starting transfers between devices, shards(): lax.ppermute(baseline[block_rows - HALO:], ('row', 'claim'), [(i, i + 1)...  3.05 us
    ppermute x1, starting transfers between devices, shards(): lax.ppermute(jnp.concatenate([jnp.where(col == 0, last, 0.0), jnp.where(c...  1.99 us
    pallas_call x1, Pallas kernels, shards(): pl.pallas_call(functools.partial(pack_kernel, rows, cols, block_rows, blo...  1.5 us
    pallas_call x1, Pallas kernels, shards(): pl.pallas_call(base_kernel, in_specs=[scalars] + [whole] * 4, out_specs=[...  1.46 us
  transfers between devices with their start and end apart: 4, of which 1 were waited for; matrix products, arithmetic and copies ran while one was open for 1% of the time, Pallas kernels for 7%

profile of v5, /device:TPU:0, one launch (start us, length us, event | category | flops | bytes accessed | tf_op | source)
XLA Modules:
  0.0 42.5 jit_solution(5183171916280015127)
XLA Ops:
  0.0 0.0 copy-start
  0.0 0.0 copy-start.1
  0.0 1.1 %fusion.1 = (f32[64,1024]{1,0:T(8,128)S(1)}, f32[64,1024]{1,0:T(8,128)S(1)}) fusion(f32[128,1024]{1,0:T(8,128)} %base_ref.1), kind=kLoop, calls=%fused_computation.4 | loop fusion | bytes 1048576 | tf_op jit(solution)/shard_map/slice | solution.py:265
  1.1 1.3 %collective-permute-start.1 = (f32[64,1024]{1,0:T(8,128)S(1)}, f32[64,1024]{1,0:T(8,128)S(1)}, u32[]{:S(2)}, u32[]{:S(2)}) collective-permute-start(f32[64,1024]{1,0:T(8,128)S(1)} %get-tuple-element.13), channel_id=1, source_target_pairs={{1,0},{4,1},{5,4},{8,5},{9,8},{12,9},{13,12},{3,2},{6,3},{7,6},{10... | collective-permute-start | bytes 786440 | tf_op jit(solution)/shard_map/ppermute | solution.py:265
  2.4 3.0 %collective-permute-start = (f32[64,1024]{1,0:T(8,128)S(1)}, f32[64,1024]{1,0:T(8,128)S(1)}, u32[]{:S(2)}, u32[]{:S(2)}) collective-permute-start(f32[64,1024]{1,0:T(8,128)S(1)} %get-tuple-element.14), channel_id=1, source_target_pairs={{0,1},{1,4},{4,5},{5,8},{8,9},{9,12},{12,13},{2,3},{3,6},{6,7},{7,... | collective-permute-start | bytes 786440 | tf_op jit(solution)/shard_map/ppermute | solution.py:264
  5.5 1.5 %shard_map.56 = f32[16,8,192]{2,1,0:T(8,128)} custom-call(s32[1,8,192]{2,1,0:T(8,128)} %cell_ref.1, f32[1,8,192]{2,1,0:T(8,128)} %weight_ref.1, s32[1,8]{1,0:T(1,128)} %count_ref.1), custom_call_target="tpu_custom_call" | custom-call | tf_op jit(solution)/shard_map/pallas_call | solution.py:257
  7.0 0.0 copy-done
  7.0 0.1 fusion
  7.1 0.0 collective-permute-done.1.below_ref
  7.1 0.0 collective-permute-done.above_ref
  7.1 11.0 %all-to-all-start = ((f32[16,8,192]{2,1,0:T(8,128)}), f32[16,8,192]{2,1,0:T(8,128)S(1)}, u32[]{:S(2)}, u32[]{:S(2)}) async-start(f32[16,8,192]{2,1,0:T(8,128)} %shard_map.56), calls=%async_computation | async-start | bytes 262144 | tf_op jit(solution)/shard_map/all_to_all | solution.py:267
  18.1 0.1 fusion.3
  18.2 0.1 fusion.2
  18.3 0.1 pad_maximum_fusion
  18.4 2.0 %collective-permute-start.2 = (f32[256,128]{1,0:T(8,128)S(1)}, f32[256,128]{1,0:T(8,128)S(1)}, u32[]{:S(2)}, u32[]{:S(2)}) collective-permute-start(f32[256,128]{1,0:T(8,128)S(1)} %pad_maximum_fusion), channel_id=1, source_target_pairs={{0,2},{2,0},{1,3},{3,1},{4,6},{6,4},{5,7},{7,5},{8,10},{10,8},{9,1... | collective-permute-start | bytes 393224 | tf_op jit(solution)/shard_map/ppermute | solution.py:273
  20.4 4.9 %collective-permute-done.2.beside_ref = f32[256,128]{1,0:T(8,128)S(1)} collective-permute-done((f32[256,128]{1,0:T(8,128)S(1)}, f32[256,128]{1,0:T(8,128)S(1)}, u32[]{:S(2)}, u32[]{:S(2)}) %collective-permute-start.2) | collective-permute-done | bytes 131104 | tf_op jit(solution)/shard_map/ppermute | solution.py:273
  25.3 0.0 copy-done.1
  25.3 1.5 %shard_map.55 = (f32[9,264,128]{2,1,0:T(8,128)S(1)}, s32[16]{0:T(128)S(1)}) custom-call(s32[16]{0:T(128)S(1)} %copy-done.1, f32[128,1024]{1,0:T(8,128)S(1)} %copy-done, f32[64,1024]{1,0:T(8,128)S(1)} %collective-permute-done.above_ref, f32[64,1024]{1,0:T(8,128)S(1)} %collective-permute-done.1.below_ref, f32[256,128]{1,0:T(8,128)S(1)} %collective-permute-done.2.beside_ref), custom_call_target="tpu_custom_call" | custom-call | bytes 8388608 | tf_op jit(solution)/shard_map/pallas_call | solution.py:301
  26.7 0.0 all-to-all-done.got_ref
  26.8 5.4 %shard_map.57.counts_ref = f32[9,264,128]{2,1,0:T(8,128)S(1)} custom-call(f32[16,8,192]{2,1,0:T(8,128)S(1)} %all-to-all-done.got_ref), custom_call_target="tpu_custom_call" | custom-call | tf_op jit(solution)/shard_map/pallas_call | solution.py:310
  32.2 10.3 %shard_map.58 = f32[16,128,1024]{2,1,0:T(8,128)} custom-call(s32[16]{0:T(128)S(1)} %get-tuple-element.8.halves_ref, f32[9,264,128]{2,1,0:T(8,128)S(1)} %shard_map.57.counts_ref, f32[9,264,128]{2,1,0:T(8,128)S(1)} %get-tuple-element.10.prefix_ref), custom_call_target="tpu_custom_call" | custom-call | tf_op jit(solution)/shard_map/pallas_call | solution.py:324
  (1 shorter events, 0.0 us)
Async XLA Ops:
  0.0 7.0 %copy-start = (f32[128,1024]{1,0:T(8,128)S(1)}, f32[128,1024]{1,0:T(8,128)}, u32[]{:S(2)}) copy-start(f32[128,1024]{1,0:T(8,128)} %base_ref.1) | copy-start | bytes 1572868
  0.0 25.3 %copy-start.1 = (s32[16]{0:T(128)S(1)}, s32[16]{0:T(128)}, u32[]{:S(2)}) copy-start(s32[16]{0:T(128)} %halves_ref.1) | copy-start | bytes 196
  1.1 5.9 %collective-permute-start.1 = (f32[64,1024]{1,0:T(8,128)S(1)}, f32[64,1024]{1,0:T(8,128)S(1)}, u32[]{:S(2)}, u32[]{:S(2)}) collective-permute-start(f32[64,1024]{1,0:T(8,128)S(1)} %get-tuple-element.13), channel_id=1, source_target_pairs={{1,0},{4,1},{5,4},{8,5},{9,8},{12,9},{13,12},{3,2},{6,3},{7,6},{10... | collective-permute-start | bytes 786440 | tf_op jit(solution)/shard_map/ppermute | solution.py:265
  2.4 4.7 %collective-permute-start = (f32[64,1024]{1,0:T(8,128)S(1)}, f32[64,1024]{1,0:T(8,128)S(1)}, u32[]{:S(2)}, u32[]{:S(2)}) collective-permute-start(f32[64,1024]{1,0:T(8,128)S(1)} %get-tuple-element.14), channel_id=1, source_target_pairs={{0,1},{1,4},{4,5},{5,8},{8,9},{9,12},{12,13},{2,3},{3,6},{6,7},{7,... | collective-permute-start | bytes 786440 | tf_op jit(solution)/shard_map/ppermute | solution.py:264
  7.1 19.6 %all-to-all-start = ((f32[16,8,192]{2,1,0:T(8,128)}), f32[16,8,192]{2,1,0:T(8,128)S(1)}, u32[]{:S(2)}, u32[]{:S(2)}) async-start(f32[16,8,192]{2,1,0:T(8,128)} %shard_map.56), calls=%async_computation | async-start | bytes 262144 | tf_op jit(solution)/shard_map/all_to_all | solution.py:267
  18.4 6.9 %collective-permute-start.2 = (f32[256,128]{1,0:T(8,128)S(1)}, f32[256,128]{1,0:T(8,128)S(1)}, u32[]{:S(2)}, u32[]{:S(2)}) collective-permute-start(f32[256,128]{1,0:T(8,128)S(1)} %pad_maximum_fusion), channel_id=1, source_target_pairs={{0,2},{2,0},{1,3},{3,1},{4,6},{6,4},{5,7},{7,5},{8,10},{10,8},{9,1... | collective-permute-start | bytes 393224 | tf_op jit(solution)/shard_map/ppermute | solution.py:273

commit v6 on v5

--- a/solution.py
+++ b/solution.py
@@ -109,7 +109,7 @@
     return slice(block * LANES, (block + 1) * LANES)
 
 
-def base_kernel(halves_ref, base_ref, above_ref, below_ref, beside_ref, prefix, halves_out, window):
+def base_kernel(halves_ref, base_ref, above_ref, below_ref, upper_ref, beside_ref, lower_ref, prefix, halves_out, window):
     block_rows, block_cols = base_ref.shape
     blocks = block_cols // LANES
     for step in range(halves_ref.shape[0]):
@@ -118,7 +118,9 @@
         window[block, 0:HALO, :] = above_ref[:, lanes_of(block)]
         window[block, HALO : HALO + block_rows, :] = base_ref[:, lanes_of(block)]
         window[block, HALO + block_rows :, :] = below_ref[:, lanes_of(block)]
-    window[blocks] = beside_ref[...]
+    window[blocks, 0:HALO, :] = upper_ref[...]
+    window[blocks, HALO : HALO + block_rows, :] = beside_ref[...]
+    window[blocks, HALO + block_rows :, :] = lower_ref[...]
     row_prefix(window, prefix)
 
 
@@ -260,29 +262,42 @@
         out_shape=jax.ShapeDtypeStruct((devices, 4 * (sides + 1), slots), F32),
     )(claim_cell, claim_weight, claim_count)
 
+    got = lax.all_to_all(sent, ("row", "col", "claim"), split_axis=0, concat_axis=0, tiled=True)
+    _, block = lax.optimization_barrier((sent, baseline))
     strips = rows * 2
-    above = lax.ppermute(baseline[block_rows - HALO :], ("row", "claim"), [(i, i + 1) for i in range(strips - 1)])
-    below = lax.ppermute(baseline[:HALO], ("row", "claim"), [(i + 1, i) for i in range(strips - 1)])
-    sent, _, _ = lax.optimization_barrier((sent, above, below))
-    got = lax.all_to_all(sent, ("row", "col", "claim"), split_axis=0, concat_axis=0, tiled=True)
-    pieces = (above, baseline, below)
-    first = jnp.concatenate([piece[:, :HALO] for piece in pieces], axis=0)
-    last = jnp.concatenate([piece[:, block_cols - HALO :] for piece in pieces], axis=0)
+    down = [(i, i + 1) for i in range(strips - 1)]
+    up = [(i + 1, i) for i in range(strips - 1)]
+    above = lax.ppermute(block[block_rows - HALO :], ("row", "claim"), down)
+    below = lax.ppermute(block[:HALO], ("row", "claim"), up)
+    first, last = block[:, :HALO], block[:, block_cols - HALO :]
     if cols == 2:
         col = lax.axis_index("col")
-        beside = lax.ppermute(
-            jnp.concatenate([jnp.where(col == 0, last, 0.0), jnp.where(col == 1, first, 0.0)], axis=1),
-            "col",
-            [(0, 1), (1, 0)],
+        edge = jnp.concatenate([jnp.where(col == 0, last, 0.0), jnp.where(col == 1, first, 0.0)], axis=1)
+
+        def place(strip, column):
+            return (strip // 2 * cols + column) * 2 + strip % 2
+
+        def across(pairs):
+            return [(place(i, c), place(j, 1 - c)) for i, j in pairs for c in (0, 1)]
+
+        axes = ("row", "col", "claim")
+        beside = (
+            lax.ppermute(edge[block_rows - HALO :], axes, across(down)),
+            lax.ppermute(edge, "col", [(0, 1), (1, 0)]),
+            lax.ppermute(edge[:HALO], axes, across(up)),
         )
     else:
-        beside = jnp.concatenate(
+        pieces = (above, block, below)
+        first = jnp.concatenate([piece[:, :HALO] for piece in pieces], axis=0)
+        last = jnp.concatenate([piece[:, block_cols - HALO :] for piece in pieces], axis=0)
+        sides_of = jnp.concatenate(
             [
                 lax.ppermute(last, "col", [(i, i + 1) for i in range(cols - 1)]),
                 lax.ppermute(first, "col", [(i + 1, i) for i in range(cols - 1)]),
             ],
             axis=1,
         )
+        beside = (sides_of[:HALO], sides_of[HALO : HALO + block_rows], sides_of[HALO + block_rows :])
     sizes = half_widths.shape[0]
     blocks = block_cols // LANES
     places = 2 * (sides + 1)
@@ -300,13 +315,13 @@
             ]
     base, half_widths = pl.pallas_call(
         base_kernel,
-        in_specs=[scalars] + [whole] * 4,
+        in_specs=[scalars] + [whole] * 6,
         out_specs=[whole, scalars],
         out_shape=[jax.ShapeDtypeStruct(prefix, F32), jax.ShapeDtypeStruct(half_widths.shape, jnp.int32)],
         scratch_shapes=[window],
-        cost_estimate=pl.CostEstimate(flops=0, bytes_accessed=8 * 1024 * 1024, transcendentals=0),
+        cost_estimate=pl.CostEstimate(flops=0, bytes_accessed=4 * 1024 * 1024, transcendentals=0),
         compiler_params=pltpu.CompilerParams(vmem_limit_bytes=BASE_VMEM),
-    )(half_widths, baseline, above, below, beside)
+    )(half_widths, baseline, above, below, *beside)
     counts = pl.pallas_call(
         functools.partial(bin_kernel, sides),
         in_specs=[whole],
@@ -318,6 +333,7 @@
             pltpu.VMEM((places, chunk_rows, LANES), F32),
             *spaces,
         ],
+        cost_estimate=pl.CostEstimate(flops=0, bytes_accessed=20 * 1024 * 1024, transcendentals=0),
         compiler_params=pltpu.CompilerParams(vmem_limit_bytes=BIN_VMEM),
     )(got)
     field = (sizes, block_rows, block_cols)

time: 42.8 us -> 41.4 us (0.967)
  the two profiles are of different devices: /device:TPU:0 before, /device:TPU:1 now
where the time goes in v6:
time: 41.4 us; the launch traced here: 41.1 us
  starting transfers between devices  20.8 us (50%)
  Pallas kernels  18.8 us (45%)
  local copies, waits for them, and re-layouts  1.07 us (3%)
    pallas_call x1, Pallas kernels, shards(): pl.pallas_call(functools.partial(scan_kernel, 3), in_specs=[scalars, whol...  10.3 us
    all_to_all x1, starting transfers between devices, shards(): lax.all_to_all(sent, ('row', 'col', 'claim'), split_axis=0, concat_axis=0...  7.32 us
    pallas_call x1, Pallas kernels, shards(): pl.pallas_call(functools.partial(bin_kernel, sides), in_specs=[whole], ou...  5.44 us
    ppermute x1, starting transfers between devices, shards(): lax.ppermute(edge[block_rows - HALO:], axes, across(down))  4.54 us
    ppermute x1, starting transfers between devices, shards(): above = lax.ppermute(block[block_rows - HALO:], ('row', 'claim'), down)  3.55 us
    ppermute x1, starting transfers between devices, shards(): below = lax.ppermute(block[:HALO], ('row', 'claim'), up)  2.01 us
    ppermute x1, starting transfers between devices, shards(): lax.ppermute(edge[:HALO], axes, across(up))  1.92 us
    pallas_call x1, Pallas kernels, shards(): pl.pallas_call(base_kernel, in_specs=[scalars] + [whole] * 6, out_specs=[...  1.59 us
  transfers between devices with their start and end apart: 6, of which 0 were waited for; matrix products, arithmetic and copies ran while one was open for 3% of the time, Pallas kernels for 13%

profile of v6, /device:TPU:1, one launch (start us, length us, event | category | flops | bytes accessed | tf_op | source)
XLA Modules:
  0.0 41.1 jit_solution(15320442986513879416)
XLA Ops:
  0.0 0.0 copy-start
  0.0 1.5 %shard_map.55 = f32[16,8,192]{2,1,0:T(8,128)} custom-call(s32[1,8,192]{2,1,0:T(8,128)} %cell_ref.1, f32[1,8,192]{2,1,0:T(8,128)} %weight_ref.1, s32[1,8]{1,0:T(1,128)} %count_ref.1), custom_call_target="tpu_custom_call" | custom-call | tf_op jit(solution)/shard_map/pallas_call | solution.py:259
  1.5 7.3 %all-to-all-start = ((f32[16,8,192]{2,1,0:T(8,128)}), f32[16,8,192]{2,1,0:T(8,128)S(1)}, u32[]{:S(2)}, u32[]{:S(2)}) async-start(f32[16,8,192]{2,1,0:T(8,128)} %shard_map.55), calls=%async_computation | async-start | bytes 262144 | tf_op jit(solution)/shard_map/all_to_all | solution.py:265
  8.8 1.1 %fusion.2 = (f32[64,1024]{1,0:T(8,128)S(1)}, f32[64,1024]{1,0:T(8,128)S(1)}) fusion(f32[128,1024]{1,0:T(8,128)} %base_ref.1), kind=kLoop, calls=%fused_computation.9 | loop fusion | bytes 1048576 | tf_op jit(solution)/shard_map/slice | solution.py:271
  9.9 0.0 copy-start.1
  9.9 2.0 %collective-permute-start.1 = (f32[64,1024]{1,0:T(8,128)S(1)}, f32[64,1024]{1,0:T(8,128)S(1)}, u32[]{:S(2)}, u32[]{:S(2)}) collective-permute-start(f32[64,1024]{1,0:T(8,128)S(1)} %get-tuple-element.13), channel_id=1, source_target_pairs={{1,0},{4,1},{5,4},{8,5},{9,8},{12,9},{13,12},{3,2},{6,3},{7,6},{10... | collective-permute-start | bytes 786440 | tf_op jit(solution)/shard_map/ppermute | solution.py:271
  11.9 3.6 %collective-permute-start = (f32[64,1024]{1,0:T(8,128)S(1)}, f32[64,1024]{1,0:T(8,128)S(1)}, u32[]{:S(2)}, u32[]{:S(2)}) collective-permute-start(f32[64,1024]{1,0:T(8,128)S(1)} %get-tuple-element.14), channel_id=1, source_target_pairs={{0,1},{1,4},{4,5},{5,8},{8,9},{9,12},{12,13},{2,3},{3,6},{6,7},{7,... | collective-permute-start | bytes 786440 | tf_op jit(solution)/shard_map/ppermute | solution.py:270
  15.5 0.0 copy-done
  15.5 0.1 slice_select_fusion
  15.6 0.1 pad_maximum_fusion
  15.7 1.5 %collective-permute-start.3 = (f32[128,128]{1,0:T(8,128)S(1)}, f32[128,128]{1,0:T(8,128)S(1)}, u32[]{:S(2)}, u32[]{:S(2)}) collective-permute-start(f32[128,128]{1,0:T(8,128)S(1)} %pad_maximum_fusion), channel_id=1, source_target_pairs={{0,2},{2,0},{1,3},{3,1},{4,6},{6,4},{5,7},{7,5},{8,10},{10,8},{9,1... | collective-permute-start | bytes 196616 | tf_op jit(solution)/shard_map/ppermute | solution.py:286
  17.1 0.1 fusion.1
  17.2 1.9 %collective-permute-start.4 = (f32[64,128]{1,0:T(8,128)S(1)}, f32[64,128]{1,0:T(8,128)S(1)}, u32[]{:S(2)}, u32[]{:S(2)}) collective-permute-start(f32[64,128]{1,0:T(8,128)S(1)} %get-tuple-element.15), channel_id=1, source_target_pairs={{1,2},{3,0},{4,3},{6,1},{5,6},{7,4},{8,7},{10,5},{9,10},{11,8},{12... | collective-permute-start | bytes 98312 | tf_op jit(solution)/shard_map/ppermute | solution.py:287
  19.1 4.5 %collective-permute-start.2 = (f32[64,128]{1,0:T(8,128)S(1)}, f32[64,128]{1,0:T(8,128)S(1)}, u32[]{:S(2)}, u32[]{:S(2)}) collective-permute-start(f32[64,128]{1,0:T(8,128)S(1)} %get-tuple-element.16), channel_id=1, source_target_pairs={{0,3},{2,1},{1,6},{3,4},{4,7},{6,5},{5,10},{7,8},{8,11},{10,9},{9,... | collective-permute-start | bytes 98312 | tf_op jit(solution)/shard_map/ppermute | solution.py:285
  23.7 0.0 all-to-all-done.got_ref
  23.7 5.4 %shard_map.57.counts_ref = f32[9,264,128]{2,1,0:T(8,128)S(1)} custom-call(f32[16,8,192]{2,1,0:T(8,128)S(1)} %all-to-all-done.got_ref), custom_call_target="tpu_custom_call" | custom-call | bytes 20971520 | tf_op jit(solution)/shard_map/pallas_call | solution.py:325
  29.2 0.0 collective-permute-done.4.lower_ref
  29.2 0.0 collective-permute-done.2.upper_ref
  29.2 0.0 collective-permute-done.3.beside_ref
  29.2 0.0 collective-permute-done.1.below_ref
  29.2 0.0 collective-permute-done.above_ref
  29.2 0.0 copy-done.1
  29.2 1.6 %shard_map.56 = (f32[9,264,128]{2,1,0:T(8,128)S(1)}, s32[16]{0:T(128)S(1)}) custom-call(s32[16]{0:T(128)S(1)} %copy-done.1, f32[128,1024]{1,0:T(8,128)S(1)} %copy-done, f32[64,1024]{1,0:T(8,128)S(1)} %collective-permute-done.above_ref, f32[64,1024]{1,0:T(8,128)S(1)} %collective-permute-done.1.below_ref, f32[64,128]{1,0:T(8,128)S(1)} %collective-permute-done.2.upper_ref, ...), custom_call_target="tpu_custom_call" | custom-call | bytes 4194304 | tf_op jit(solution)/shard_map/pallas_call | solution.py:316
  30.8 10.3 %shard_map.58 = f32[16,128,1024]{2,1,0:T(8,128)} custom-call(s32[16]{0:T(128)S(1)} %get-tuple-element.9.halves_ref, f32[9,264,128]{2,1,0:T(8,128)S(1)} %shard_map.57.counts_ref, f32[9,264,128]{2,1,0:T(8,128)S(1)} %get-tuple-element.10.prefix_ref), custom_call_target="tpu_custom_call" | custom-call | tf_op jit(solution)/shard_map/pallas_call | solution.py:340
Async XLA Ops:
  0.0 15.5 %copy-start = (f32[128,1024]{1,0:T(8,128)S(1)}, f32[128,1024]{1,0:T(8,128)}, u32[]{:S(2)}) copy-start(f32[128,1024]{1,0:T(8,128)} %base_ref.1) | copy-start | bytes 1572868
  1.5 22.2 %all-to-all-start = ((f32[16,8,192]{2,1,0:T(8,128)}), f32[16,8,192]{2,1,0:T(8,128)S(1)}, u32[]{:S(2)}, u32[]{:S(2)}) async-start(f32[16,8,192]{2,1,0:T(8,128)} %shard_map.55), calls=%async_computation | async-start | bytes 262144 | tf_op jit(solution)/shard_map/all_to_all | solution.py:265
  9.9 19.3 %copy-start.1 = (s32[16]{0:T(128)S(1)}, s32[16]{0:T(128)}, u32[]{:S(2)}) copy-start(s32[16]{0:T(128)} %halves_ref.1) | copy-start | bytes 196
  9.9 19.3 %collective-permute-start.1 = (f32[64,1024]{1,0:T(8,128)S(1)}, f32[64,1024]{1,0:T(8,128)S(1)}, u32[]{:S(2)}, u32[]{:S(2)}) collective-permute-start(f32[64,1024]{1,0:T(8,128)S(1)} %get-tuple-element.13), channel_id=1, source_target_pairs={{1,0},{4,1},{5,4},{8,5},{9,8},{12,9},{13,12},{3,2},{6,3},{7,6},{10... | collective-permute-start | bytes 786440 | tf_op jit(solution)/shard_map/ppermute | solution.py:271
  11.9 17.3 %collective-permute-start = (f32[64,1024]{1,0:T(8,128)S(1)}, f32[64,1024]{1,0:T(8,128)S(1)}, u32[]{:S(2)}, u32[]{:S(2)}) collective-permute-start(f32[64,1024]{1,0:T(8,128)S(1)} %get-tuple-element.14), channel_id=1, source_target_pairs={{0,1},{1,4},{4,5},{5,8},{8,9},{9,12},{12,13},{2,3},{3,6},{6,7},{7,... | collective-permute-start | bytes 786440 | tf_op jit(solution)/shard_map/ppermute | solution.py:270
  15.7 13.5 %collective-permute-start.3 = (f32[128,128]{1,0:T(8,128)S(1)}, f32[128,128]{1,0:T(8,128)S(1)}, u32[]{:S(2)}, u32[]{:S(2)}) collective-permute-start(f32[128,128]{1,0:T(8,128)S(1)} %pad_maximum_fusion), channel_id=1, source_target_pairs={{0,2},{2,0},{1,3},{3,1},{4,6},{6,4},{5,7},{7,5},{8,10},{10,8},{9,1... | collective-permute-start | bytes 196616 | tf_op jit(solution)/shard_map/ppermute | solution.py:286
  17.2 11.9 %collective-permute-start.4 = (f32[64,128]{1,0:T(8,128)S(1)}, f32[64,128]{1,0:T(8,128)S(1)}, u32[]{:S(2)}, u32[]{:S(2)}) collective-permute-start(f32[64,128]{1,0:T(8,128)S(1)} %get-tuple-element.15), channel_id=1, source_target_pairs={{1,2},{3,0},{4,3},{6,1},{5,6},{7,4},{8,7},{10,5},{9,10},{11,8},{12... | collective-permute-start | bytes 98312 | tf_op jit(solution)/shard_map/ppermute | solution.py:287
  19.1 10.0 %collective-permute-start.2 = (f32[64,128]{1,0:T(8,128)S(1)}, f32[64,128]{1,0:T(8,128)S(1)}, u32[]{:S(2)}, u32[]{:S(2)}) collective-permute-start(f32[64,128]{1,0:T(8,128)S(1)} %get-tuple-element.16), channel_id=1, source_target_pairs={{0,3},{2,1},{1,6},{3,4},{4,7},{6,5},{5,10},{7,8},{8,11},{10,9},{9,... | collective-permute-start | bytes 98312 | tf_op jit(solution)/shard_map/ppermute | solution.py:285

commit v7 on v6

--- a/solution.py
+++ b/solution.py
@@ -109,18 +109,25 @@
     return slice(block * LANES, (block + 1) * LANES)
 
 
-def base_kernel(halves_ref, base_ref, above_ref, below_ref, upper_ref, beside_ref, lower_ref, prefix, halves_out, window):
+def base_kernel(
+    halves_ref, base_ref, inner_ref, outer_ref, beside_ref, inner_side_ref, outer_side_ref, prefix, halves_out, window
+):
     block_rows, block_cols = base_ref.shape
     blocks = block_cols // LANES
     for step in range(halves_ref.shape[0]):
         halves_out[step] = halves_ref[step]
+    claim = lax.axis_index("claim")
+    far_side = HALO + block_rows
+    inner_at = pl.multiple_of((1 - claim) * far_side, HALO)
+    outer_at = pl.multiple_of(claim * far_side, HALO)
     for block in range(blocks):
-        window[block, 0:HALO, :] = above_ref[:, lanes_of(block)]
-        window[block, HALO : HALO + block_rows, :] = base_ref[:, lanes_of(block)]
-        window[block, HALO + block_rows :, :] = below_ref[:, lanes_of(block)]
-    window[blocks, 0:HALO, :] = upper_ref[...]
-    window[blocks, HALO : HALO + block_rows, :] = beside_ref[...]
-    window[blocks, HALO + block_rows :, :] = lower_ref[...]
+        here = lanes_of(block)
+        window[block, HALO:far_side, :] = base_ref[:, here]
+        window[block, pl.ds(inner_at, HALO), :] = inner_ref[:, here]
+        window[block, pl.ds(outer_at, HALO), :] = outer_ref[:, here]
+    window[blocks, HALO:far_side, :] = beside_ref[...]
+    window[blocks, pl.ds(inner_at, HALO), :] = inner_side_ref[...]
+    window[blocks, pl.ds(outer_at, HALO), :] = outer_side_ref[...]
     row_prefix(window, prefix)
 
 
@@ -264,40 +271,45 @@
 
     got = lax.all_to_all(sent, ("row", "col", "claim"), split_axis=0, concat_axis=0, tiled=True)
     _, block = lax.optimization_barrier((sent, baseline))
-    strips = rows * 2
-    down = [(i, i + 1) for i in range(strips - 1)]
-    up = [(i + 1, i) for i in range(strips - 1)]
-    above = lax.ppermute(block[block_rows - HALO :], ("row", "claim"), down)
-    below = lax.ppermute(block[:HALO], ("row", "claim"), up)
+    claim = lax.axis_index("claim")
+    seams = [(2 * i + 1, 2 * i + 2) for i in range(rows - 1)]
+    seams += [(j, i) for i, j in seams]
+
+    def swapped(cells, within, across, axes):
+        top, bottom = cells[:HALO], cells[block_rows - HALO :]
+        return (
+            lax.ppermute(jnp.where(claim == 0, bottom, top), axes[0], within),
+            lax.ppermute(jnp.where(claim == 0, top, bottom), axes[1], across),
+        )
+
+    inner, outer = swapped(block, [(0, 1), (1, 0)], seams, ("claim", ("row", "claim")))
     first, last = block[:, :HALO], block[:, block_cols - HALO :]
     if cols == 2:
         col = lax.axis_index("col")
         edge = jnp.concatenate([jnp.where(col == 0, last, 0.0), jnp.where(col == 1, first, 0.0)], axis=1)
+        beside = lax.ppermute(edge, "col", [(0, 1), (1, 0)])
 
         def place(strip, column):
             return (strip // 2 * cols + column) * 2 + strip % 2
 
-        def across(pairs):
-            return [(place(i, c), place(j, 1 - c)) for i, j in pairs for c in (0, 1)]
-
-        axes = ("row", "col", "claim")
-        beside = (
-            lax.ppermute(edge[block_rows - HALO :], axes, across(down)),
-            lax.ppermute(edge, "col", [(0, 1), (1, 0)]),
-            lax.ppermute(edge[:HALO], axes, across(up)),
+        inner_side, outer_side = swapped(
+            edge,
+            [(2 * c + k, 2 * (1 - c) + 1 - k) for c in (0, 1) for k in (0, 1)],
+            [(place(i, c), place(j, 1 - c)) for i, j in seams for c in (0, 1)],
+            (("col", "claim"), ("row", "col", "claim")),
         )
     else:
-        pieces = (above, block, below)
-        first = jnp.concatenate([piece[:, :HALO] for piece in pieces], axis=0)
-        last = jnp.concatenate([piece[:, block_cols - HALO :] for piece in pieces], axis=0)
-        sides_of = jnp.concatenate(
-            [
-                lax.ppermute(last, "col", [(i, i + 1) for i in range(cols - 1)]),
-                lax.ppermute(first, "col", [(i + 1, i) for i in range(cols - 1)]),
-            ],
-            axis=1,
-        )
-        beside = (sides_of[:HALO], sides_of[HALO : HALO + block_rows], sides_of[HALO + block_rows :])
+
+        def sides_of(cells):
+            return jnp.concatenate(
+                [
+                    lax.ppermute(cells[:, block_cols - HALO :], "col", [(i, i + 1) for i in range(cols - 1)]),
+                    lax.ppermute(cells[:, :HALO], "col", [(i + 1, i) for i in range(cols - 1)]),
+                ],
+                axis=1,
+            )
+
+        beside, inner_side, outer_side = sides_of(block), sides_of(inner), sides_of(outer)
     sizes = half_widths.shape[0]
     blocks = block_cols // LANES
     places = 2 * (sides + 1)
@@ -321,7 +333,7 @@
         scratch_shapes=[window],
         cost_estimate=pl.CostEstimate(flops=0, bytes_accessed=4 * 1024 * 1024, transcendentals=0),
         compiler_params=pltpu.CompilerParams(vmem_limit_bytes=BASE_VMEM),
-    )(half_widths, baseline, above, below, *beside)
+    )(half_widths, baseline, inner, outer, beside, inner_side, outer_side)
     counts = pl.pallas_call(
         functools.partial(bin_kernel, sides),
         in_specs=[whole],

time: 41.4 us -> 38 us (0.918)
  the two profiles are of different devices: /device:TPU:1 before, /device:TPU:0 now
where the time goes in v7:
time: 38 us; the launch traced here: 37.7 us
  Pallas kernels  18.7 us (49%)
  starting transfers between devices  17.5 us (46%)
  other arithmetic  1.33 us (4%)
    pallas_call x1, Pallas kernels, shards(): pl.pallas_call(functools.partial(scan_kernel, 3), in_specs=[scalars, whol...  10.3 us
    all_to_all x1, starting transfers between devices, shards(): lax.all_to_all(sent, ('row', 'col', 'claim'), split_axis=0, concat_axis=0...  7.36 us
    ppermute x2, starting transfers between devices, swapped(): lax.ppermute(jnp.where(claim == 0, bottom, top), axes[0], within)  7.29 us
    pallas_call x1, Pallas kernels, shards(): pl.pallas_call(functools.partial(bin_kernel, sides), in_specs=[whole], ou...  5.44 us
    ppermute x1, starting transfers between devices, shards(): beside = lax.ppermute(edge, 'col', [(0, 1), (1, 0)])  1.53 us
    pallas_call x1, Pallas kernels, shards(): pl.pallas_call(functools.partial(pack_kernel, rows, cols, block_rows, blo...  1.5 us
    pallas_call x1, Pallas kernels, shards(): pl.pallas_call(base_kernel, in_specs=[scalars] + [whole] * 6, out_specs=[...  1.49 us
    ppermute x2, starting transfers between devices, swapped(): lax.ppermute(jnp.where(claim == 0, top, bottom), axes[1], across)  1.34 us
  transfers between devices with their start and end apart: 6, of which 0 were waited for; matrix products, arithmetic and copies ran while one was open for 4% of the time, Pallas kernels for 14%

profile of v7, /device:TPU:0, one launch (start us, length us, event | category | flops | bytes accessed | tf_op | source)
XLA Modules:
  0.0 37.7 jit_solution(976735600068619191)
XLA Ops:
  0.0 0.0 copy-start
  0.0 1.5 %shard_map.55 = f32[16,8,192]{2,1,0:T(8,128)} custom-call(s32[1,8,192]{2,1,0:T(8,128)} %cell_ref.1, f32[1,8,192]{2,1,0:T(8,128)} %weight_ref.1, s32[1,8]{1,0:T(1,128)} %count_ref.1), custom_call_target="tpu_custom_call" | custom-call | tf_op jit(solution)/shard_map/pallas_call | solution.py:266
  1.5 7.4 %all-to-all-start = ((f32[16,8,192]{2,1,0:T(8,128)}), f32[16,8,192]{2,1,0:T(8,128)S(1)}, u32[]{:S(2)}, u32[]{:S(2)}) async-start(f32[16,8,192]{2,1,0:T(8,128)} %shard_map.55), calls=%async_computation | async-start | bytes 262144 | tf_op jit(solution)/shard_map/all_to_all | solution.py:272
  8.9 1.1 %slice_select_fusion = (f32[64,1024]{1,0:T(8,128)S(1)}, f32[64,1024]{1,0:T(8,128)S(1)}) fusion(f32[128,1024]{1,0:T(8,128)} %base_ref.1, pred[]{:T(512)S(6)} %eq.12), kind=kLoop, calls=%fused_computation | loop fusion | flops 131072 | bytes 1048577 | tf_op jit(solution)/shard_map/jit(_where)/select_n | solution.py:282
  9.9 0.0 copy-start.1
  10.0 0.7 %collective-permute-start.1 = (f32[64,1024]{1,0:T(8,128)S(1)}, f32[64,1024]{1,0:T(8,128)S(1)}, u32[]{:S(2)}, u32[]{:S(2)}) collective-permute-start(f32[64,1024]{1,0:T(8,128)S(1)} %get-tuple-element.13), channel_id=1, source_target_pairs={{1,4},{5,8},{9,12},{4,1},{8,5},{12,9},{3,6},{7,10},{11,14},{6,3},{... | collective-permute-start | bytes 786440 | tf_op jit(solution)/shard_map/ppermute | solution.py:282
  10.6 3.3 %collective-permute-start = (f32[64,1024]{1,0:T(8,128)S(1)}, f32[64,1024]{1,0:T(8,128)S(1)}, u32[]{:S(2)}, u32[]{:S(2)}) collective-permute-start(f32[64,1024]{1,0:T(8,128)S(1)} %get-tuple-element.14), channel_id=1, source_target_pairs={{0,1},{1,0},{2,3},{3,2},{4,5},{5,4},{6,7},{7,6},{8,9},{9,8},{10,11... | collective-permute-start | bytes 786440 | tf_op jit(solution)/shard_map/ppermute | solution.py:281
  14.0 0.0 copy-done
  14.0 0.1 slice_select_fusion.3
  14.1 0.1 pad_maximum_fusion
  14.2 1.5 %collective-permute-start.2 = (f32[128,128]{1,0:T(8,128)S(1)}, f32[128,128]{1,0:T(8,128)S(1)}, u32[]{:S(2)}, u32[]{:S(2)}) collective-permute-start(f32[128,128]{1,0:T(8,128)S(1)} %pad_maximum_fusion), channel_id=1, source_target_pairs={{0,2},{2,0},{1,3},{3,1},{4,6},{6,4},{5,7},{7,5},{8,10},{10,8},{9,1... | collective-permute-start | bytes 196616 | tf_op jit(solution)/shard_map/ppermute | solution.py:290
  15.7 0.1 broadcast_select_fusion
  15.8 0.7 %collective-permute-start.4 = (f32[64,128]{1,0:T(8,128)S(1)}, f32[64,128]{1,0:T(8,128)S(1)}, u32[]{:S(2)}, u32[]{:S(2)}) collective-permute-start(f32[64,128]{1,0:T(8,128)S(1)} %get-tuple-element.15), channel_id=1, source_target_pairs={{1,6},{3,4},{5,10},{7,8},{9,14},{11,12},{4,3},{6,1},{8,7},{10,5},{... | collective-permute-start | bytes 98312 | tf_op jit(solution)/shard_map/ppermute | solution.py:282
  16.5 4.0 %collective-permute-start.3 = (f32[64,128]{1,0:T(8,128)S(1)}, f32[64,128]{1,0:T(8,128)S(1)}, u32[]{:S(2)}, u32[]{:S(2)}) collective-permute-start(f32[64,128]{1,0:T(8,128)S(1)} %get-tuple-element.16), channel_id=1, source_target_pairs={{0,3},{1,2},{2,1},{3,0},{4,7},{5,6},{6,5},{7,4},{8,11},{9,10},{10,... | collective-permute-start | bytes 98312 | tf_op jit(solution)/shard_map/ppermute | solution.py:281
  20.4 0.0 all-to-all-done.got_ref
  20.4 5.4 %shard_map.57.counts_ref = f32[9,264,128]{2,1,0:T(8,128)S(1)} custom-call(f32[16,8,192]{2,1,0:T(8,128)S(1)} %all-to-all-done.got_ref), custom_call_target="tpu_custom_call" | custom-call | bytes 20971520 | tf_op jit(solution)/shard_map/pallas_call | solution.py:337
  25.9 0.0 collective-permute-done.4.outer_side_ref
  25.9 0.0 collective-permute-done.3.inner_side_ref
  25.9 0.0 collective-permute-done.2.beside_ref
  25.9 0.0 collective-permute-done.1.outer_ref
  25.9 0.0 collective-permute-done.inner_ref
  25.9 0.0 copy-done.1
  25.9 1.5 %shard_map.56 = (f32[9,264,128]{2,1,0:T(8,128)S(1)}, s32[16]{0:T(128)S(1)}) custom-call(s32[16]{0:T(128)S(1)} %copy-done.1, f32[128,1024]{1,0:T(8,128)S(1)} %copy-done, f32[64,1024]{1,0:T(8,128)S(1)} %collective-permute-done.inner_ref, f32[64,1024]{1,0:T(8,128)S(1)} %collective-permute-done.1.outer_ref, f32[128,128]{1,0:T(8,128)S(1)} %collective-permute-done.2.beside_ref, ...), custom_call_target="tpu_custom_call" | custom-call | bytes 4194304 | tf_op jit(solution)/shard_map/pallas_call | solution.py:328
  27.4 10.3 %shard_map.58 = f32[16,128,1024]{2,1,0:T(8,128)} custom-call(s32[16]{0:T(128)S(1)} %get-tuple-element.9.halves_ref, f32[9,264,128]{2,1,0:T(8,128)S(1)} %shard_map.57.counts_ref, f32[9,264,128]{2,1,0:T(8,128)S(1)} %get-tuple-element.10.prefix_ref), custom_call_target="tpu_custom_call" | custom-call | tf_op jit(solution)/shard_map/pallas_call | solution.py:352
Async XLA Ops:
  0.0 14.0 %copy-start = (f32[128,1024]{1,0:T(8,128)S(1)}, f32[128,1024]{1,0:T(8,128)}, u32[]{:S(2)}) copy-start(f32[128,1024]{1,0:T(8,128)} %base_ref.1) | copy-start | bytes 1572868
  1.5 18.9 %all-to-all-start = ((f32[16,8,192]{2,1,0:T(8,128)}), f32[16,8,192]{2,1,0:T(8,128)S(1)}, u32[]{:S(2)}, u32[]{:S(2)}) async-start(f32[16,8,192]{2,1,0:T(8,128)} %shard_map.55), calls=%async_computation | async-start | bytes 262144 | tf_op jit(solution)/shard_map/all_to_all | solution.py:272
  9.9 16.0 %copy-start.1 = (s32[16]{0:T(128)S(1)}, s32[16]{0:T(128)}, u32[]{:S(2)}) copy-start(s32[16]{0:T(128)} %halves_ref.1) | copy-start | bytes 196
  10.0 15.9 %collective-permute-start.1 = (f32[64,1024]{1,0:T(8,128)S(1)}, f32[64,1024]{1,0:T(8,128)S(1)}, u32[]{:S(2)}, u32[]{:S(2)}) collective-permute-start(f32[64,1024]{1,0:T(8,128)S(1)} %get-tuple-element.13), channel_id=1, source_target_pairs={{1,4},{5,8},{9,12},{4,1},{8,5},{12,9},{3,6},{7,10},{11,14},{6,3},{... | collective-permute-start | bytes 786440 | tf_op jit(solution)/shard_map/ppermute | solution.py:282
  10.6 15.3 %collective-permute-start = (f32[64,1024]{1,0:T(8,128)S(1)}, f32[64,1024]{1,0:T(8,128)S(1)}, u32[]{:S(2)}, u32[]{:S(2)}) collective-permute-start(f32[64,1024]{1,0:T(8,128)S(1)} %get-tuple-element.14), channel_id=1, source_target_pairs={{0,1},{1,0},{2,3},{3,2},{4,5},{5,4},{6,7},{7,6},{8,9},{9,8},{10,11... | collective-permute-start | bytes 786440 | tf_op jit(solution)/shard_map/ppermute | solution.py:281
  14.2 11.7 %collective-permute-start.2 = (f32[128,128]{1,0:T(8,128)S(1)}, f32[128,128]{1,0:T(8,128)S(1)}, u32[]{:S(2)}, u32[]{:S(2)}) collective-permute-start(f32[128,128]{1,0:T(8,128)S(1)} %pad_maximum_fusion), channel_id=1, source_target_pairs={{0,2},{2,0},{1,3},{3,1},{4,6},{6,4},{5,7},{7,5},{8,10},{10,8},{9,1... | collective-permute-start | bytes 196616 | tf_op jit(solution)/shard_map/ppermute | solution.py:290
  15.8 10.1 %collective-permute-start.4 = (f32[64,128]{1,0:T(8,128)S(1)}, f32[64,128]{1,0:T(8,128)S(1)}, u32[]{:S(2)}, u32[]{:S(2)}) collective-permute-start(f32[64,128]{1,0:T(8,128)S(1)} %get-tuple-element.15), channel_id=1, source_target_pairs={{1,6},{3,4},{5,10},{7,8},{9,14},{11,12},{4,3},{6,1},{8,7},{10,5},{... | collective-permute-start | bytes 98312 | tf_op jit(solution)/shard_map/ppermute | solution.py:282
  16.5 9.4 %collective-permute-start.3 = (f32[64,128]{1,0:T(8,128)S(1)}, f32[64,128]{1,0:T(8,128)S(1)}, u32[]{:S(2)}, u32[]{:S(2)}) collective-permute-start(f32[64,128]{1,0:T(8,128)S(1)} %get-tuple-element.16), channel_id=1, source_target_pairs={{0,3},{1,2},{2,1},{3,0},{4,7},{5,6},{6,5},{7,4},{8,11},{9,10},{10,... | collective-permute-start | bytes 98312 | tf_op jit(solution)/shard_map/ppermute | solution.py:281

commit v8 on v5

--- a/solution.py
+++ b/solution.py
@@ -109,16 +109,23 @@
     return slice(block * LANES, (block + 1) * LANES)
 
 
-def base_kernel(halves_ref, base_ref, above_ref, below_ref, beside_ref, prefix, halves_out, window):
+def base_kernel(halves_ref, base_ref, inner_ref, outer_ref, beside_ref, prefix, halves_out, window):
     block_rows, block_cols = base_ref.shape
     blocks = block_cols // LANES
     for step in range(halves_ref.shape[0]):
         halves_out[step] = halves_ref[step]
+    claim = lax.axis_index("claim")
+    far_side = HALO + block_rows
+    inner_at = pl.multiple_of((1 - claim) * far_side, HALO)
+    outer_at = pl.multiple_of(claim * far_side, HALO)
     for block in range(blocks):
-        window[block, 0:HALO, :] = above_ref[:, lanes_of(block)]
-        window[block, HALO : HALO + block_rows, :] = base_ref[:, lanes_of(block)]
-        window[block, HALO + block_rows :, :] = below_ref[:, lanes_of(block)]
-    window[blocks] = beside_ref[...]
+        here = lanes_of(block)
+        window[block, HALO:far_side, :] = base_ref[:, here]
+        window[block, pl.ds(inner_at, HALO), :] = inner_ref[:, here]
+        window[block, pl.ds(outer_at, HALO), :] = outer_ref[:, here]
+    window[blocks, HALO:far_side, :] = beside_ref[:block_rows]
+    window[blocks, pl.ds(inner_at, HALO), :] = beside_ref[block_rows : block_rows + HALO]
+    window[blocks, pl.ds(outer_at, HALO), :] = beside_ref[block_rows + HALO :]
     row_prefix(window, prefix)
 
 
@@ -260,21 +267,22 @@
         out_shape=jax.ShapeDtypeStruct((devices, 4 * (sides + 1), slots), F32),
     )(claim_cell, claim_weight, claim_count)
 
-    strips = rows * 2
-    above = lax.ppermute(baseline[block_rows - HALO :], ("row", "claim"), [(i, i + 1) for i in range(strips - 1)])
-    below = lax.ppermute(baseline[:HALO], ("row", "claim"), [(i + 1, i) for i in range(strips - 1)])
-    sent, _, _ = lax.optimization_barrier((sent, above, below))
     got = lax.all_to_all(sent, ("row", "col", "claim"), split_axis=0, concat_axis=0, tiled=True)
-    pieces = (above, baseline, below)
+    _, block = lax.optimization_barrier((sent, baseline))
+    claim = lax.axis_index("claim")
+    seams = [(2 * i + 1, 2 * i + 2) for i in range(rows - 1)]
+    seams += [(j, i) for i, j in seams]
+
+    top, bottom = block[:HALO], block[block_rows - HALO :]
+    inner = lax.ppermute(jnp.where(claim == 0, bottom, top), "claim", [(0, 1), (1, 0)])
+    outer = lax.ppermute(jnp.where(claim == 0, top, bottom), ("row", "claim"), seams)
+    pieces = (block, inner, outer)
     first = jnp.concatenate([piece[:, :HALO] for piece in pieces], axis=0)
     last = jnp.concatenate([piece[:, block_cols - HALO :] for piece in pieces], axis=0)
     if cols == 2:
         col = lax.axis_index("col")
-        beside = lax.ppermute(
-            jnp.concatenate([jnp.where(col == 0, last, 0.0), jnp.where(col == 1, first, 0.0)], axis=1),
-            "col",
-            [(0, 1), (1, 0)],
-        )
+        edge = jnp.concatenate([jnp.where(col == 0, last, 0.0), jnp.where(col == 1, first, 0.0)], axis=1)
+        beside = lax.ppermute(edge, "col", [(0, 1), (1, 0)])
     else:
         beside = jnp.concatenate(
             [
@@ -304,9 +312,9 @@
         out_specs=[whole, scalars],
         out_shape=[jax.ShapeDtypeStruct(prefix, F32), jax.ShapeDtypeStruct(half_widths.shape, jnp.int32)],
         scratch_shapes=[window],
-        cost_estimate=pl.CostEstimate(flops=0, bytes_accessed=8 * 1024 * 1024, transcendentals=0),
+        cost_estimate=pl.CostEstimate(flops=0, bytes_accessed=4 * 1024 * 1024, transcendentals=0),
         compiler_params=pltpu.CompilerParams(vmem_limit_bytes=BASE_VMEM),
-    )(half_widths, baseline, above, below, beside)
+    )(half_widths, baseline, inner, outer, beside)
     counts = pl.pallas_call(
         functools.partial(bin_kernel, sides),
         in_specs=[whole],
@@ -318,6 +326,7 @@
             pltpu.VMEM((places, chunk_rows, LANES), F32),
             *spaces,
         ],
+        cost_estimate=pl.CostEstimate(flops=0, bytes_accessed=20 * 1024 * 1024, transcendentals=0),
         compiler_params=pltpu.CompilerParams(vmem_limit_bytes=BIN_VMEM),
     )(got)
     field = (sizes, block_rows, block_cols)

time: 42.8 us -> 37.6 us (0.88)
  starting transfers between devices: 17.3 us -> 11.9 us
  local copies, waits for them, and re-layouts: 1.36 us -> 0.24 us
  other arithmetic: 0.13 us -> 1.19 us
    all_to_all x1, waiting for transfers between devices: 0.01 us -> 4.2 us  [shards(): lax.all_to_all(sent, ('row', 'col', 'claim'), split_axis=0, concat_axis=0...]
    ppermute x3, waiting for transfers between devices: 4.88 us -> 1.03 us  [the longest x1 1.02 us: shards(): lax.ppermute(jnp.where(claim == 0, bottom, top), 'claim', [(0, 1), (1, 0)])]
    ppermute x3, starting transfers between devices: 6.33 us -> 3.01 us  [the longest x1 1.93 us: shards(): beside = lax.ppermute(edge, 'col', [(0, 1), (1, 0)])]
    all_to_all x1, starting transfers between devices: 11 us -> 8.88 us  [shards(): lax.all_to_all(sent, ('row', 'col', 'claim'), split_axis=0, concat_axis=0...]
    slice x1 -> x0, local copies, waits for them, and re-layouts: 1.12 us -> none  [shards(): baseline[:HALO]]
    select_n x0 -> x1, other arithmetic: none -> 1.07 us  [shards(): jnp.where(claim == 0, top, bottom)]
  transfers between devices with their start and end apart: 4 -> 4, of which waited for: 1 -> 2; matrix products, arithmetic and copies ran while one was open for 1% -> 1% of each run, Pallas kernels for 7% -> 15%
where the time goes in v8:
time: 37.6 us; the launch traced here: 37.3 us
  Pallas kernels  18.7 us (50%)
  starting transfers between devices  11.9 us (32%)
  waiting for transfers between devices  5.23 us (14%)
  other arithmetic  1.19 us (3%)
    pallas_call x1, Pallas kernels, shards(): pl.pallas_call(functools.partial(scan_kernel, 3), in_specs=[scalars, whol...  10.3 us
    all_to_all x1, starting transfers between devices, shards(): lax.all_to_all(sent, ('row', 'col', 'claim'), split_axis=0, concat_axis=0...  8.88 us
    pallas_call x1, Pallas kernels, shards(): pl.pallas_call(functools.partial(bin_kernel, sides), in_specs=[whole], ou...  5.43 us
    all_to_all x1, waiting for transfers between devices, shards(): lax.all_to_all(sent, ('row', 'col', 'claim'), split_axis=0, concat_axis=0...  4.2 us
    ppermute x1, starting transfers between devices, shards(): beside = lax.ppermute(edge, 'col', [(0, 1), (1, 0)])  1.93 us
    pallas_call x1, Pallas kernels, shards(): pl.pallas_call(functools.partial(pack_kernel, rows, cols, block_rows, blo...  1.5 us
    pallas_call x1, Pallas kernels, shards(): pl.pallas_call(base_kernel, in_specs=[scalars] + [whole] * 4, out_specs=[...  1.49 us
    select_n x1, other arithmetic, shards(): jnp.where(claim == 0, top, bottom)  1.07 us
  transfers between devices with their start and end apart: 4, of which 2 were waited for; matrix products, arithmetic and copies ran while one was open for 1% of the time, Pallas kernels for 15%

profile of v8, /device:TPU:0, one launch (start us, length us, event | category | flops | bytes accessed | tf_op | source)
XLA Modules:
  0.0 37.3 jit_solution(5154176311693077333)
XLA Ops:
  0.0 0.0 copy-start
  0.0 1.5 %shard_map.55 = f32[16,8,192]{2,1,0:T(8,128)} custom-call(s32[1,8,192]{2,1,0:T(8,128)} %cell_ref.1, f32[1,8,192]{2,1,0:T(8,128)} %weight_ref.1, s32[1,8]{1,0:T(1,128)} %count_ref.1), custom_call_target="tpu_custom_call" | custom-call | tf_op jit(solution)/shard_map/pallas_call | solution.py:264
  1.5 1.1 %slice_select_fusion = (f32[64,1024]{1,0:T(8,128)S(1)}, f32[64,1024]{1,0:T(8,128)S(1)}) fusion(f32[128,1024]{1,0:T(8,128)} %base_ref.1, pred[]{:T(512)S(6)} %eq.10), kind=kLoop, calls=%fused_computation | loop fusion | flops 131072 | bytes 1048577 | tf_op jit(solution)/shard_map/jit(_where)/select_n | solution.py:278
  2.6 0.7 %collective-permute-start.1 = (f32[64,1024]{1,0:T(8,128)S(1)}, f32[64,1024]{1,0:T(8,128)S(1)}, u32[]{:S(2)}, u32[]{:S(2)}) collective-permute-start(f32[64,1024]{1,0:T(8,128)S(1)} %get-tuple-element.13), channel_id=1, source_target_pairs={{1,4},{5,8},{9,12},{4,1},{8,5},{12,9},{3,6},{7,10},{11,14},{6,3},{... | collective-permute-start | bytes 786440 | tf_op jit(solution)/shard_map/ppermute | solution.py:278
  3.3 8.9 %all-to-all-start = ((f32[16,8,192]{2,1,0:T(8,128)}), f32[16,8,192]{2,1,0:T(8,128)S(1)}, u32[]{:S(2)}, u32[]{:S(2)}) async-start(f32[16,8,192]{2,1,0:T(8,128)} %shard_map.55), calls=%async_computation | async-start | bytes 262144 | tf_op jit(solution)/shard_map/all_to_all | solution.py:270
  12.2 0.4 %collective-permute-start = (f32[64,1024]{1,0:T(8,128)S(1)}, f32[64,1024]{1,0:T(8,128)S(1)}, u32[]{:S(2)}, u32[]{:S(2)}) collective-permute-start(f32[64,1024]{1,0:T(8,128)S(1)} %get-tuple-element.14), channel_id=1, source_target_pairs={{0,1},{1,0},{2,3},{3,2},{4,5},{5,4},{6,7},{7,6},{8,9},{9,8},{10,11... | collective-permute-start | bytes 786440 | tf_op jit(solution)/shard_map/ppermute | solution.py:277
  12.6 0.0 copy-done
  12.6 0.1 fusion
  12.6 0.0 collective-permute-done.1.outer_ref
  12.7 0.1 fusion.2
  12.7 0.0 copy-start.1
  12.7 1.0 %collective-permute-done.inner_ref = f32[64,1024]{1,0:T(8,128)S(1)} collective-permute-done((f32[64,1024]{1,0:T(8,128)S(1)}, f32[64,1024]{1,0:T(8,128)S(1)}, u32[]{:S(2)}, u32[]{:S(2)}) %collective-permute-start) | collective-permute-done | bytes 262176 | tf_op jit(solution)/shard_map/ppermute | solution.py:277
  13.8 0.1 fusion.1
  13.9 0.1 pad_maximum_fusion
  14.0 1.9 %collective-permute-start.2 = (f32[256,128]{1,0:T(8,128)S(1)}, f32[256,128]{1,0:T(8,128)S(1)}, u32[]{:S(2)}, u32[]{:S(2)}) collective-permute-start(f32[256,128]{1,0:T(8,128)S(1)} %pad_maximum_fusion), channel_id=1, source_target_pairs={{0,2},{2,0},{1,3},{3,1},{4,6},{6,4},{5,7},{7,5},{8,10},{10,8},{9,1... | collective-permute-start | bytes 393224 | tf_op jit(solution)/shard_map/ppermute | solution.py:285
  15.9 4.2 %all-to-all-done.got_ref = f32[16,8,192]{2,1,0:T(8,128)S(1)} async-done(((f32[16,8,192]{2,1,0:T(8,128)}), f32[16,8,192]{2,1,0:T(8,128)S(1)}, u32[]{:S(2)}, u32[]{:S(2)}) %all-to-all-start) | async-done | bytes 98336 | tf_op jit(solution)/shard_map/all_to_all | solution.py:270
  20.1 5.4 %shard_map.57.counts_ref = f32[9,264,128]{2,1,0:T(8,128)S(1)} custom-call(f32[16,8,192]{2,1,0:T(8,128)S(1)} %all-to-all-done.got_ref), custom_call_target="tpu_custom_call" | custom-call | bytes 20971520 | tf_op jit(solution)/shard_map/pallas_call | solution.py:318
  25.5 0.0 collective-permute-done.2.beside_ref
  25.5 0.0 copy-done.1
  25.6 1.5 %shard_map.56 = (f32[9,264,128]{2,1,0:T(8,128)S(1)}, s32[16]{0:T(128)S(1)}) custom-call(s32[16]{0:T(128)S(1)} %copy-done.1, f32[128,1024]{1,0:T(8,128)S(1)} %copy-done, f32[64,1024]{1,0:T(8,128)S(1)} %collective-permute-done.inner_ref, f32[64,1024]{1,0:T(8,128)S(1)} %collective-permute-done.1.outer_ref, f32[256,128]{1,0:T(8,128)S(1)} %collective-permute-done.2.beside_ref), custom_call_target="tpu_custom_call" | custom-call | bytes 4194304 | tf_op jit(solution)/shard_map/pallas_call | solution.py:309
  27.1 10.3 %shard_map.58 = f32[16,128,1024]{2,1,0:T(8,128)} custom-call(s32[16]{0:T(128)S(1)} %get-tuple-element.9.halves_ref, f32[9,264,128]{2,1,0:T(8,128)S(1)} %shard_map.57.counts_ref, f32[9,264,128]{2,1,0:T(8,128)S(1)} %get-tuple-element.10.prefix_ref), custom_call_target="tpu_custom_call" | custom-call | tf_op jit(solution)/shard_map/pallas_call | solution.py:333
  (1 shorter events, 0.0 us)
Async XLA Ops:
  0.0 12.6 %copy-start = (f32[128,1024]{1,0:T(8,128)S(1)}, f32[128,1024]{1,0:T(8,128)}, u32[]{:S(2)}) copy-start(f32[128,1024]{1,0:T(8,128)} %base_ref.1) | copy-start | bytes 1572868
  2.6 10.1 %collective-permute-start.1 = (f32[64,1024]{1,0:T(8,128)S(1)}, f32[64,1024]{1,0:T(8,128)S(1)}, u32[]{:S(2)}, u32[]{:S(2)}) collective-permute-start(f32[64,1024]{1,0:T(8,128)S(1)} %get-tuple-element.13), channel_id=1, source_target_pairs={{1,4},{5,8},{9,12},{4,1},{8,5},{12,9},{3,6},{7,10},{11,14},{6,3},{... | collective-permute-start | bytes 786440 | tf_op jit(solution)/shard_map/ppermute | solution.py:278
  3.3 16.8 %all-to-all-start = ((f32[16,8,192]{2,1,0:T(8,128)}), f32[16,8,192]{2,1,0:T(8,128)S(1)}, u32[]{:S(2)}, u32[]{:S(2)}) async-start(f32[16,8,192]{2,1,0:T(8,128)} %shard_map.55), calls=%async_computation | async-start | bytes 262144 | tf_op jit(solution)/shard_map/all_to_all | solution.py:270
  12.2 1.6 %collective-permute-start = (f32[64,1024]{1,0:T(8,128)S(1)}, f32[64,1024]{1,0:T(8,128)S(1)}, u32[]{:S(2)}, u32[]{:S(2)}) collective-permute-start(f32[64,1024]{1,0:T(8,128)S(1)} %get-tuple-element.14), channel_id=1, source_target_pairs={{0,1},{1,0},{2,3},{3,2},{4,5},{5,4},{6,7},{7,6},{8,9},{9,8},{10,11... | collective-permute-start | bytes 786440 | tf_op jit(solution)/shard_map/ppermute | solution.py:277
  12.7 12.8 %copy-start.1 = (s32[16]{0:T(128)S(1)}, s32[16]{0:T(128)}, u32[]{:S(2)}) copy-start(s32[16]{0:T(128)} %halves_ref.1) | copy-start | bytes 196
  14.0 11.6 %collective-permute-start.2 = (f32[256,128]{1,0:T(8,128)S(1)}, f32[256,128]{1,0:T(8,128)S(1)}, u32[]{:S(2)}, u32[]{:S(2)}) collective-permute-start(f32[256,128]{1,0:T(8,128)S(1)} %pad_maximum_fusion), channel_id=1, source_target_pairs={{0,2},{2,0},{1,3},{3,1},{4,6},{6,4},{5,7},{7,5},{8,10},{10,8},{9,1... | collective-permute-start | bytes 393224 | tf_op jit(solution)/shard_map/ppermute | solution.py:285

commit v9 on v8

--- a/solution.py
+++ b/solution.py
@@ -76,24 +76,27 @@
     return high, (value - high.astype(F32)).astype(BF16)
 
 
-def row_prefix(window, prefix):
-    side, rows, _ = window.shape
-    side -= 1
+def prefix_of(cells, prefix, block):
+    sub = lax.broadcasted_iota(jnp.int32, (cells.shape[0] // 8, 8, LANES), 1)
+    cells = cells.reshape(-1, 8, LANES)
+    for hop in (1, 2, 4):
+        cells = cells + jnp.where(sub >= hop, pltpu.roll(cells, hop, axis=1), 0.0)
+    carry = jnp.zeros((8, LANES), F32)
+    prefix[block, 0:8, :] = carry
+    for tile in range(cells.shape[0]):
+        total = cells[tile] + carry
+        prefix[block, 8 * tile + 8 : 8 * tile + 16, :] = total
+        carry = jnp.broadcast_to(total[7:8], (8, LANES))
+
+
+def row_prefix(window, prefix, ends):
+    blocks, rows, _ = prefix.shape[0] - 1, window.shape[1], LANES
     lane = lax.broadcasted_iota(jnp.int32, (rows, LANES), 1)
-    sub = lax.broadcasted_iota(jnp.int32, (rows // 8, 8, LANES), 1)
-    before = window[side]
-    for block in range(side + 1):
-        after = window[side] if block == side else pltpu.roll(window[block], HALO, axis=1)
-        cells = jnp.where(lane < HALO, before, after).reshape(-1, 8, LANES)
+    before = ends
+    for block in range(blocks + 1):
+        after = ends if block == blocks else pltpu.roll(window[block], HALO, axis=1)
+        prefix_of(jnp.where(lane < HALO, before, after), prefix, block)
         before = after
-        for hop in (1, 2, 4):
-            cells = cells + jnp.where(sub >= hop, pltpu.roll(cells, hop, axis=1), 0.0)
-        carry = jnp.zeros((8, LANES), F32)
-        prefix[block, 0:8, :] = carry
-        for tile in range(rows // 8):
-            total = cells[tile] + carry
-            prefix[block, 8 * tile + 8 : 8 * tile + 16, :] = total
-            carry = jnp.broadcast_to(total[7:8], (8, LANES))
 
 
 def band_of(half):
@@ -109,24 +112,22 @@
     return slice(block * LANES, (block + 1) * LANES)
 
 
-def base_kernel(halves_ref, base_ref, inner_ref, outer_ref, beside_ref, prefix, halves_out, window):
+def halo_rows(claim, block_rows):
+    far_side = HALO + block_rows
+    return pl.multiple_of((1 - claim) * far_side, HALO), pl.multiple_of(claim * far_side, HALO)
+
+
+def base_kernel(halves_ref, base_ref, inner_ref, outer_ref, prefix, halves_out, window):
     block_rows, block_cols = base_ref.shape
-    blocks = block_cols // LANES
     for step in range(halves_ref.shape[0]):
         halves_out[step] = halves_ref[step]
-    claim = lax.axis_index("claim")
-    far_side = HALO + block_rows
-    inner_at = pl.multiple_of((1 - claim) * far_side, HALO)
-    outer_at = pl.multiple_of(claim * far_side, HALO)
-    for block in range(blocks):
+    inner_at, outer_at = halo_rows(lax.axis_index("claim"), block_rows)
+    for block in range(block_cols // LANES):
         here = lanes_of(block)
-        window[block, HALO:far_side, :] = base_ref[:, here]
+        window[block, HALO : HALO + block_rows, :] = base_ref[:, here]
         window[block, pl.ds(inner_at, HALO), :] = inner_ref[:, here]
         window[block, pl.ds(outer_at, HALO), :] = outer_ref[:, here]
-    window[blocks, HALO:far_side, :] = beside_ref[:block_rows]
-    window[blocks, pl.ds(inner_at, HALO), :] = beside_ref[block_rows : block_rows + HALO]
-    window[blocks, pl.ds(outer_at, HALO), :] = beside_ref[block_rows + HALO :]
-    row_prefix(window, prefix)
+    row_prefix(window, prefix, jnp.zeros((window.shape[1], LANES), F32))
 
 
 def pack16(row):
@@ -214,12 +215,20 @@
             window[block, pl.ds(start, rows), :] = acc[top : top + rows, here] + acc[top + rows : top + 2 * rows, here]
     window[blocks, pl.ds(own_at, own_rows), :] = side_acc[:, :LANES] + side_acc[:, LANES:]
     window[blocks, pl.ds(far_at, HALO), :] = corner_acc[:, :LANES] + corner_acc[:, LANES:]
-    row_prefix(window, prefix)
-
-
-def scan_kernel(group, halves_ref, counts_ref, prefix_ref, out_ref, buffer, sems):
+    row_prefix(window, prefix, window[blocks])
+
+
+def scan_kernel(group, halves_ref, counts_ref, prefix_ref, beside_ref, out_ref, buffer, sems, rows_s, ends):
     sizes, block_rows, block_cols = buffer.shape
     blocks = block_cols // LANES
+    inner_at, outer_at = halo_rows(lax.axis_index("claim"), block_rows)
+    rows_s[HALO : HALO + block_rows, :] = beside_ref[:block_rows]
+    rows_s[pl.ds(inner_at, HALO), :] = beside_ref[block_rows : block_rows + HALO]
+    rows_s[pl.ds(outer_at, HALO), :] = beside_ref[block_rows + HALO :]
+    prefix_of(rows_s[...], ends, 0)
+    lane = lax.broadcasted_iota(jnp.int32, ends.shape[1:], 1)
+    ends[1] = jnp.where(lane < HALO, prefix_ref[blocks], ends[0])
+    ends[0] = jnp.where(lane < HALO, ends[0], prefix_ref[0])
 
     def one_size(step, _):
         half = halves_ref[step]
@@ -230,9 +239,11 @@
             some = range(first, min(first + group, blocks + 1))
             strips = []
             for block in some:
-                for field in (counts_ref, prefix_ref):
-                    lower = field[block, pl.ds(HALO + 8 + half, block_rows), :]
-                    upper = field[block, pl.ds(HALO + 7 - half, block_rows), :]
+                at_end = block in (0, blocks)
+                base_at = (ends, block // blocks) if at_end else (prefix_ref, block)
+                for field, index in ((counts_ref, block), base_at):
+                    lower = field[index, pl.ds(HALO + 8 + half, block_rows), :]
+                    upper = field[index, pl.ds(HALO + 7 - half, block_rows), :]
                     strips.append(jnp.concatenate(halves(lower - upper), axis=1))
             product = jnp.dot(jnp.concatenate(strips, axis=0), band, preferred_element_type=F32)
             for index, block in enumerate(some):
@@ -308,13 +319,14 @@
             ]
     base, half_widths = pl.pallas_call(
         base_kernel,
-        in_specs=[scalars] + [whole] * 4,
+        in_specs=[scalars] + [whole] * 3,
         out_specs=[whole, scalars],
         out_shape=[jax.ShapeDtypeStruct(prefix, F32), jax.ShapeDtypeStruct(half_widths.shape, jnp.int32)],
         scratch_shapes=[window],
         cost_estimate=pl.CostEstimate(flops=0, bytes_accessed=4 * 1024 * 1024, transcendentals=0),
         compiler_params=pltpu.CompilerParams(vmem_limit_bytes=BASE_VMEM),
-    )(half_widths, baseline, inner, outer, beside)
+    )(half_widths, baseline, inner, outer)
+    got, base, half_widths = lax.optimization_barrier((got, base, half_widths))
     counts = pl.pallas_call(
         functools.partial(bin_kernel, sides),
         in_specs=[whole],
@@ -332,12 +344,17 @@
     field = (sizes, block_rows, block_cols)
     return pl.pallas_call(
         functools.partial(scan_kernel, 3),
-        in_specs=[scalars, whole, whole],
+        in_specs=[scalars, whole, whole, whole],
         out_specs=pl.BlockSpec(memory_space=pltpu.HBM),
-        scratch_shapes=[pltpu.VMEM(field, F32), pltpu.SemaphoreType.DMA((sizes,))],
+        scratch_shapes=[
+            pltpu.VMEM(field, F32),
+            pltpu.SemaphoreType.DMA((sizes,)),
+            pltpu.VMEM((2 * block_rows, LANES), F32),
+            pltpu.VMEM((2, 2 * block_rows + 8, LANES), F32),
+        ],
         out_shape=jax.ShapeDtypeStruct(field, F32),
         compiler_params=pltpu.CompilerParams(vmem_limit_bytes=SCAN_VMEM),
-    )(half_widths, counts, base)
+    )(half_widths, counts, base, beside)
 
 
 def solution(mesh):

time: 37.6 us -> 36.3 us (0.965)
  waiting for transfers between devices: 5.23 us -> 3.74 us
    all_to_all x1, waiting for transfers between devices: 4.2 us -> 2.71 us  [shards(): lax.all_to_all(sent, ('row', 'col', 'claim'), split_axis=0, concat_axis=0...]
  transfers between devices with their start and end apart: 4 -> 4, of which waited for: 2 -> 2; matrix products, arithmetic and copies ran while one was open for 1% -> 1% of each run, Pallas kernels for 15% -> 19%
where the time goes in v9:
time: 36.3 us; the launch traced here: 35.9 us
  Pallas kernels  18.8 us (52%)
  starting transfers between devices  11.9 us (33%)
  waiting for transfers between devices  3.74 us (10%)
  other arithmetic  1.2 us (3%)
    pallas_call x1, Pallas kernels, shards(): pl.pallas_call(functools.partial(scan_kernel, 3), in_specs=[scalars, whol...  10.4 us
    all_to_all x1, starting transfers between devices, shards(): lax.all_to_all(sent, ('row', 'col', 'claim'), split_axis=0, concat_axis=0...  8.88 us
    pallas_call x1, Pallas kernels, shards(): pl.pallas_call(functools.partial(bin_kernel, sides), in_specs=[whole], ou...  5.45 us
    all_to_all x1, waiting for transfers between devices, shards(): lax.all_to_all(sent, ('row', 'col', 'claim'), split_axis=0, concat_axis=0...  2.71 us
    ppermute x1, starting transfers between devices, shards(): beside = lax.ppermute(edge, 'col', [(0, 1), (1, 0)])  1.93 us
    pallas_call x1, Pallas kernels, shards(): pl.pallas_call(functools.partial(pack_kernel, rows, cols, block_rows, blo...  1.5 us
    pallas_call x1, Pallas kernels, shards(): pl.pallas_call(base_kernel, in_specs=[scalars] + [whole] * 3, out_specs=[...  1.48 us
    select_n x1, other arithmetic, shards(): jnp.where(claim == 0, top, bottom)  1.08 us
  transfers between devices with their start and end apart: 4, of which 2 were waited for; matrix products, arithmetic and copies ran while one was open for 1% of the time, Pallas kernels for 19%

profile of v9, /device:TPU:0, one launch (start us, length us, event | category | flops | bytes accessed | tf_op | source)
XLA Modules:
  0.0 35.9 jit_solution(9425902606973023301)
XLA Ops:
  0.0 0.0 copy-start
  0.0 1.5 %shard_map.55 = f32[16,8,192]{2,1,0:T(8,128)} custom-call(s32[1,8,192]{2,1,0:T(8,128)} %cell_ref.1, f32[1,8,192]{2,1,0:T(8,128)} %weight_ref.1, s32[1,8]{1,0:T(1,128)} %count_ref.1), custom_call_target="tpu_custom_call" | custom-call | tf_op jit(solution)/shard_map/pallas_call | solution.py:275
  1.5 0.0 copy-start.1
  1.5 1.1 %slice_select_fusion = (f32[64,1024]{1,0:T(8,128)S(1)}, f32[64,1024]{1,0:T(8,128)S(1)}) fusion(f32[128,1024]{1,0:T(8,128)} %base_ref.1, pred[]{:T(512)S(6)} %eq.10), kind=kLoop, calls=%fused_computation | loop fusion | flops 131072 | bytes 1048577 | tf_op jit(solution)/shard_map/jit(_where)/select_n | solution.py:289
  2.6 0.7 %collective-permute-start.1 = (f32[64,1024]{1,0:T(8,128)S(1)}, f32[64,1024]{1,0:T(8,128)S(1)}, u32[]{:S(2)}, u32[]{:S(2)}) collective-permute-start(f32[64,1024]{1,0:T(8,128)S(1)} %get-tuple-element.19), channel_id=1, source_target_pairs={{1,4},{5,8},{9,12},{4,1},{8,5},{12,9},{3,6},{7,10},{11,14},{6,3},{... | collective-permute-start | bytes 786440 | tf_op jit(solution)/shard_map/ppermute | solution.py:289
  3.3 8.9 %all-to-all-start = ((f32[16,8,192]{2,1,0:T(8,128)}), f32[16,8,192]{2,1,0:T(8,128)S(1)}, u32[]{:S(2)}, u32[]{:S(2)}) async-start(f32[16,8,192]{2,1,0:T(8,128)} %shard_map.55), calls=%async_computation | async-start | bytes 262144 | tf_op jit(solution)/shard_map/all_to_all | solution.py:281
  12.2 0.4 %collective-permute-start = (f32[64,1024]{1,0:T(8,128)S(1)}, f32[64,1024]{1,0:T(8,128)S(1)}, u32[]{:S(2)}, u32[]{:S(2)}) collective-permute-start(f32[64,1024]{1,0:T(8,128)S(1)} %get-tuple-element.20), channel_id=1, source_target_pairs={{0,1},{1,0},{2,3},{3,2},{4,5},{5,4},{6,7},{7,6},{8,9},{9,8},{10,11... | collective-permute-start | bytes 786440 | tf_op jit(solution)/shard_map/ppermute | solution.py:288
  12.6 0.0 copy-done
  12.6 0.1 fusion
  12.7 0.0 collective-permute-done.1.outer_ref
  12.7 0.1 fusion.2
  12.7 1.0 %collective-permute-done.inner_ref = f32[64,1024]{1,0:T(8,128)S(1)} collective-permute-done((f32[64,1024]{1,0:T(8,128)S(1)}, f32[64,1024]{1,0:T(8,128)S(1)}, u32[]{:S(2)}, u32[]{:S(2)}) %collective-permute-start) | collective-permute-done | bytes 262176 | tf_op jit(solution)/shard_map/ppermute | solution.py:288
  13.8 0.1 fusion.1
  13.9 0.1 pad_maximum_fusion
  14.0 1.9 %collective-permute-start.2 = (f32[256,128]{1,0:T(8,128)S(1)}, f32[256,128]{1,0:T(8,128)S(1)}, u32[]{:S(2)}, u32[]{:S(2)}) collective-permute-start(f32[256,128]{1,0:T(8,128)S(1)} %pad_maximum_fusion), channel_id=1, source_target_pairs={{0,2},{2,0},{1,3},{3,1},{4,6},{6,4},{5,7},{7,5},{8,10},{10,8},{9,1... | collective-permute-start | bytes 393224 | tf_op jit(solution)/shard_map/ppermute | solution.py:296
  15.9 0.0 copy-done.1
  15.9 1.5 %shard_map.56 = (f32[9,264,128]{2,1,0:T(8,128)S(1)}, s32[16]{0:T(128)S(1)}) custom-call(s32[16]{0:T(128)S(1)} %copy-done.1, f32[128,1024]{1,0:T(8,128)S(1)} %copy-done, f32[64,1024]{1,0:T(8,128)S(1)} %collective-permute-done.inner_ref, f32[64,1024]{1,0:T(8,128)S(1)} %collective-permute-done.1.outer_ref), custom_call_target="tpu_custom_call" | custom-call | bytes 4194304 | tf_op jit(solution)/shard_map/pallas_call | solution.py:320
  17.4 2.7 %all-to-all-done.got_ref = f32[16,8,192]{2,1,0:T(8,128)S(1)} async-done(((f32[16,8,192]{2,1,0:T(8,128)}), f32[16,8,192]{2,1,0:T(8,128)S(1)}, u32[]{:S(2)}, u32[]{:S(2)}) %all-to-all-start) | async-done | bytes 98336 | tf_op jit(solution)/shard_map/all_to_all | solution.py:281
  20.1 5.4 %shard_map.57.counts_ref = f32[9,264,128]{2,1,0:T(8,128)S(1)} custom-call(f32[16,8,192]{2,1,0:T(8,128)S(1)} %all-to-all-done.got_ref), custom_call_target="tpu_custom_call" | custom-call | bytes 20971520 | tf_op jit(solution)/shard_map/pallas_call | solution.py:330
  25.6 0.0 collective-permute-done.2.beside_ref
  25.6 10.4 %shard_map.58 = f32[16,128,1024]{2,1,0:T(8,128)} custom-call(s32[16]{0:T(128)S(1)} %get-tuple-element.14.halves_ref, f32[9,264,128]{2,1,0:T(8,128)S(1)} %shard_map.57.counts_ref, f32[9,264,128]{2,1,0:T(8,128)S(1)} %get-tuple-element.16.prefix_ref, f32[256,128]{1,0:T(8,128)S(1)} %collective-permute-done.2.beside_ref), custom_call_target="tpu_custom_call" | custom-call | tf_op jit(solution)/shard_map/pallas_call | solution.py:345
  (1 shorter events, 0.0 us)
Async XLA Ops:
  0.0 12.6 %copy-start = (f32[128,1024]{1,0:T(8,128)S(1)}, f32[128,1024]{1,0:T(8,128)}, u32[]{:S(2)}) copy-start(f32[128,1024]{1,0:T(8,128)} %base_ref.1) | copy-start | bytes 1572868
  1.5 14.4 %copy-start.1 = (s32[16]{0:T(128)S(1)}, s32[16]{0:T(128)}, u32[]{:S(2)}) copy-start(s32[16]{0:T(128)} %halves_ref.1) | copy-start | bytes 196
  2.6 10.1 %collective-permute-start.1 = (f32[64,1024]{1,0:T(8,128)S(1)}, f32[64,1024]{1,0:T(8,128)S(1)}, u32[]{:S(2)}, u32[]{:S(2)}) collective-permute-start(f32[64,1024]{1,0:T(8,128)S(1)} %get-tuple-element.19), channel_id=1, source_target_pairs={{1,4},{5,8},{9,12},{4,1},{8,5},{12,9},{3,6},{7,10},{11,14},{6,3},{... | collective-permute-start | bytes 786440 | tf_op jit(solution)/shard_map/ppermute | solution.py:289
  3.3 16.8 %all-to-all-start = ((f32[16,8,192]{2,1,0:T(8,128)}), f32[16,8,192]{2,1,0:T(8,128)S(1)}, u32[]{:S(2)}, u32[]{:S(2)}) async-start(f32[16,8,192]{2,1,0:T(8,128)} %shard_map.55), calls=%async_computation | async-start | bytes 262144 | tf_op jit(solution)/shard_map/all_to_all | solution.py:281
  12.2 1.6 %collective-permute-start = (f32[64,1024]{1,0:T(8,128)S(1)}, f32[64,1024]{1,0:T(8,128)S(1)}, u32[]{:S(2)}, u32[]{:S(2)}) collective-permute-start(f32[64,1024]{1,0:T(8,128)S(1)} %get-tuple-element.20), channel_id=1, source_target_pairs={{0,1},{1,0},{2,3},{3,2},{4,5},{5,4},{6,7},{7,6},{8,9},{9,8},{10,11... | collective-permute-start | bytes 786440 | tf_op jit(solution)/shard_map/ppermute | solution.py:288
  14.0 11.6 %collective-permute-start.2 = (f32[256,128]{1,0:T(8,128)S(1)}, f32[256,128]{1,0:T(8,128)S(1)}, u32[]{:S(2)}, u32[]{:S(2)}) collective-permute-start(f32[256,128]{1,0:T(8,128)S(1)} %pad_maximum_fusion), channel_id=1, source_target_pairs={{0,2},{2,0},{1,3},{3,1},{4,6},{6,4},{5,7},{7,5},{8,10},{10,8},{9,1... | collective-permute-start | bytes 393224 | tf_op jit(solution)/shard_map/ppermute | solution.py:296

commit v10 on v9

--- a/solution.py
+++ b/solution.py
@@ -40,7 +40,16 @@
     return found
 
 
-def pack_kernel(rows, cols, block_rows, block_cols, cell_ref, weight_ref, count_ref, out_ref):
+def pack_kernel(rows, cols, block_rows, block_cols, cell_ref, weight_ref, count_ref, base_ref, out_ref, outer_ref, inner_ref, sems):
+    claim_here = lax.axis_index("claim")
+    last_rows = block_rows - HALO
+    starts = ((1 - claim_here) * last_rows, claim_here * last_rows)
+    copies = [
+        pltpu.make_async_copy(base_ref.at[pl.ds(pl.multiple_of(start, 8), HALO)], ref, sems.at[index])
+        for index, (start, ref) in enumerate(zip(starts, (inner_ref, outer_ref)))
+    ]
+    for copy in copies:
+        copy.start()
     cell = cell_ref[0]
     tiles, slots = cell.shape
     slot = lax.broadcasted_iota(jnp.int32, (1, slots), 1)
@@ -69,6 +78,8 @@
                     out_ref[index, 2 * place : 2 * place + 1, :] = code
                     out_ref[index, 2 * place + 1 : 2 * place + 2, :] = weights[tile] if there else zero
                 index += 1
+    for copy in copies:
+        copy.wait()
 
 
 def halves(value):
@@ -272,21 +283,22 @@
     devices = rows * cols * 2
     whole = pl.BlockSpec(memory_space=pltpu.VMEM)
     scalars = pl.BlockSpec(memory_space=pltpu.SMEM)
-    sent = pl.pallas_call(
+    remote = pl.BlockSpec(memory_space=pltpu.HBM)
+    strip = jax.ShapeDtypeStruct((HALO, block_cols), F32)
+    sent, outer, inner = pl.pallas_call(
         functools.partial(pack_kernel, rows, cols, block_rows, block_cols),
-        in_specs=[whole, whole, scalars],
-        out_shape=jax.ShapeDtypeStruct((devices, 4 * (sides + 1), slots), F32),
-    )(claim_cell, claim_weight, claim_count)
-
+        in_specs=[whole, whole, scalars, remote],
+        out_specs=[whole, remote, remote],
+        out_shape=[jax.ShapeDtypeStruct((devices, 4 * (sides + 1), slots), F32), strip, strip],
+        scratch_shapes=[pltpu.SemaphoreType.DMA((2,))],
+    )(claim_cell, claim_weight, claim_count, baseline)
     got = lax.all_to_all(sent, ("row", "col", "claim"), split_axis=0, concat_axis=0, tiled=True)
     _, block = lax.optimization_barrier((sent, baseline))
-    claim = lax.axis_index("claim")
     seams = [(2 * i + 1, 2 * i + 2) for i in range(rows - 1)]
     seams += [(j, i) for i, j in seams]
 
-    top, bottom = block[:HALO], block[block_rows - HALO :]
-    inner = lax.ppermute(jnp.where(claim == 0, bottom, top), "claim", [(0, 1), (1, 0)])
-    outer = lax.ppermute(jnp.where(claim == 0, top, bottom), ("row", "claim"), seams)
+    outer = lax.ppermute(outer, ("row", "claim"), seams)
+    inner = lax.ppermute(inner, "claim", [(0, 1), (1, 0)])
     pieces = (block, inner, outer)
     first = jnp.concatenate([piece[:, :HALO] for piece in pieces], axis=0)
     last = jnp.concatenate([piece[:, block_cols - HALO :] for piece in pieces], axis=0)

time: 36.3 us -> 53.7 us (1.48)
  the two profiles are of different devices: /device:TPU:0 before, /device:TPU:1 now
where the time goes in v10:
time: 53.7 us; the launch traced here: 53.4 us
  Pallas kernels  35.8 us (67%)
  starting transfers between devices  12.5 us (23%)
  waiting for transfers between devices  3.79 us (7%)
  local copies, waits for them, and re-layouts  1.11 us (2%)
    pallas_call x1, Pallas kernels, shards(): pl.pallas_call(functools.partial(pack_kernel, rows, cols, block_rows, blo...  18.5 us
    pallas_call x1, Pallas kernels, shards(): pl.pallas_call(functools.partial(scan_kernel, 3), in_specs=[scalars, whol...  10.4 us
    all_to_all x1, starting transfers between devices, shards(): lax.all_to_all(sent, ('row', 'col', 'claim'), split_axis=0, concat_axis=0...  7.38 us
    pallas_call x1, Pallas kernels, shards(): pl.pallas_call(functools.partial(bin_kernel, sides), in_specs=[whole], ou...  5.45 us
    ppermute x1, waiting for transfers between devices, shards(): outer = lax.ppermute(outer, ('row', 'claim'), seams)  3.78 us
    ppermute x1, starting transfers between devices, shards(): outer = lax.ppermute(outer, ('row', 'claim'), seams)  3.53 us
    ppermute x1, starting transfers between devices, shards(): beside = lax.ppermute(edge, 'col', [(0, 1), (1, 0)])  1.48 us
    pallas_call x1, Pallas kernels, shards(): pl.pallas_call(base_kernel, in_specs=[scalars] + [whole] * 3, out_specs=[...  1.48 us
  transfers between devices with their start and end apart: 4, of which 1 were waited for; matrix products, arithmetic and copies ran while one was open for 2% of the time, Pallas kernels for 13%

profile of v10, /device:TPU:1, one launch (start us, length us, event | category | flops | bytes accessed | tf_op | source)
XLA Modules:
  0.0 53.4 jit_solution(15897133930486470541)
XLA Ops:
  0.0 0.0 copy-start
  0.0 0.0 copy-start.1
  0.0 18.5 %shard_map.55 = (f32[16,8,192]{2,1,0:T(8,128)}, f32[64,1024]{1,0:T(8,128)}, f32[64,1024]{1,0:T(8,128)}) custom-call(s32[1,8,192]{2,1,0:T(8,128)} %cell_ref.1, f32[1,8,192]{2,1,0:T(8,128)} %weight_ref.1, s32[1,8]{1,0:T(1,128)} %count_ref.1, f32[128,1024]{1,0:T(8,128)} %base_ref.3), custom_call_target="tpu_custom_call" | custom-call | tf_op jit(solution)/shard_map/pallas_call | solution.py:288
  18.5 0.1 collective-permute-start
  18.6 7.4 %all-to-all-start = ((f32[16,8,192]{2,1,0:T(8,128)}), f32[16,8,192]{2,1,0:T(8,128)S(1)}, u32[]{:S(2)}, u32[]{:S(2)}) async-start(f32[16,8,192]{2,1,0:T(8,128)} %get-tuple-element.14), calls=%async_computation | async-start | bytes 262144 | tf_op jit(solution)/shard_map/all_to_all | solution.py:295
  26.0 3.5 %collective-permute-start.1 = (f32[64,1024]{1,0:T(8,128)}, f32[64,1024]{1,0:T(8,128)S(1)}, u32[]{:S(2)}, u32[]{:S(2)}) collective-permute-start(f32[64,1024]{1,0:T(8,128)} %get-tuple-element.16), channel_id=1, source_target_pairs={{1,4},{5,8},{9,12},{4,1},{8,5},{12,9},{3,6},{7,10},{11,14},{6,3},{... | collective-permute-start | bytes 786440 | tf_op jit(solution)/shard_map/ppermute | solution.py:300
  29.5 1.0 %fusion = (f32[128,64]{1,0:T(8,128)S(1)}, f32[128,64]{1,0:T(8,128)S(1)}) fusion(f32[128,1024]{1,0:T(8,128)} %base_ref.3), kind=kLoop, calls=%fused_computation.3 | loop fusion | bytes 131072 | tf_op jit(solution)/shard_map/slice | solution.py:304
  30.5 0.0 collective-permute-done.inner_ref
  30.5 0.1 fusion.1
  30.6 3.8 %collective-permute-done.1.outer_ref = f32[64,1024]{1,0:T(8,128)S(1)} collective-permute-done((f32[64,1024]{1,0:T(8,128)}, f32[64,1024]{1,0:T(8,128)S(1)}, u32[]{:S(2)}, u32[]{:S(2)}) %collective-permute-start.1) | collective-permute-done | bytes 262176 | tf_op jit(solution)/shard_map/ppermute | solution.py:300
  34.3 0.1 fusion.2
  34.4 0.1 pad_maximum_fusion
  34.6 1.5 %collective-permute-start.2 = (f32[256,128]{1,0:T(8,128)S(1)}, f32[256,128]{1,0:T(8,128)S(1)}, u32[]{:S(2)}, u32[]{:S(2)}) collective-permute-start(f32[256,128]{1,0:T(8,128)S(1)} %pad_maximum_fusion), channel_id=1, source_target_pairs={{0,2},{2,0},{1,3},{3,1},{4,6},{6,4},{5,7},{7,5},{8,10},{10,8},{9,1... | collective-permute-start | bytes 393224 | tf_op jit(solution)/shard_map/ppermute | solution.py:308
  36.0 0.0 copy-done
  36.0 0.0 copy-done.1
  36.0 1.5 %shard_map.56 = (f32[9,264,128]{2,1,0:T(8,128)S(1)}, s32[16]{0:T(128)S(1)}) custom-call(s32[16]{0:T(128)S(1)} %copy-done.1, f32[128,1024]{1,0:T(8,128)S(1)} %copy-done, f32[64,1024]{1,0:T(8,128)S(1)} %collective-permute-done.inner_ref, f32[64,1024]{1,0:T(8,128)S(1)} %collective-permute-done.1.outer_ref), custom_call_target="tpu_custom_call" | custom-call | bytes 4194304 | tf_op jit(solution)/shard_map/pallas_call | solution.py:332
  37.5 0.0 all-to-all-done.got_ref
  37.5 5.4 %shard_map.57.counts_ref = f32[9,264,128]{2,1,0:T(8,128)S(1)} custom-call(f32[16,8,192]{2,1,0:T(8,128)S(1)} %all-to-all-done.got_ref), custom_call_target="tpu_custom_call" | custom-call | bytes 20971520 | tf_op jit(solution)/shard_map/pallas_call | solution.py:342
  43.0 0.0 collective-permute-done.2.beside_ref
  43.0 10.4 %shard_map.58 = f32[16,128,1024]{2,1,0:T(8,128)} custom-call(s32[16]{0:T(128)S(1)} %get-tuple-element.19.halves_ref, f32[9,264,128]{2,1,0:T(8,128)S(1)} %shard_map.57.counts_ref, f32[9,264,128]{2,1,0:T(8,128)S(1)} %get-tuple-element.21.prefix_ref, f32[256,128]{1,0:T(8,128)S(1)} %collective-permute-done.2.beside_ref), custom_call_target="tpu_custom_call" | custom-call | tf_op jit(solution)/shard_map/pallas_call | solution.py:357
  (1 shorter events, 0.0 us)
Async XLA Ops:
  0.0 36.0 %copy-start = (f32[128,1024]{1,0:T(8,128)S(1)}, f32[128,1024]{1,0:T(8,128)}, u32[]{:S(2)}) copy-start(f32[128,1024]{1,0:T(8,128)} %base_ref.3) | copy-start | bytes 1572868
  0.0 36.0 %copy-start.1 = (s32[16]{0:T(128)S(1)}, s32[16]{0:T(128)}, u32[]{:S(2)}) copy-start(s32[16]{0:T(128)} %halves_ref.1) | copy-start | bytes 196
  18.5 12.0 %collective-permute-start = (f32[64,1024]{1,0:T(8,128)}, f32[64,1024]{1,0:T(8,128)S(1)}, u32[]{:S(2)}, u32[]{:S(2)}) collective-permute-start(f32[64,1024]{1,0:T(8,128)} %get-tuple-element.15), channel_id=1, source_target_pairs={{0,1},{1,0},{2,3},{3,2},{4,5},{5,4},{6,7},{7,6},{8,9},{9,8},{10,11... | collective-permute-start | bytes 786440 | tf_op jit(solution)/shard_map/ppermute | solution.py:301
  18.6 18.9 %all-to-all-start = ((f32[16,8,192]{2,1,0:T(8,128)}), f32[16,8,192]{2,1,0:T(8,128)S(1)}, u32[]{:S(2)}, u32[]{:S(2)}) async-start(f32[16,8,192]{2,1,0:T(8,128)} %get-tuple-element.14), calls=%async_computation | async-start | bytes 262144 | tf_op jit(solution)/shard_map/all_to_all | solution.py:295
  26.0 8.4 %collective-permute-start.1 = (f32[64,1024]{1,0:T(8,128)}, f32[64,1024]{1,0:T(8,128)S(1)}, u32[]{:S(2)}, u32[]{:S(2)}) collective-permute-start(f32[64,1024]{1,0:T(8,128)} %get-tuple-element.16), channel_id=1, source_target_pairs={{1,4},{5,8},{9,12},{4,1},{8,5},{12,9},{3,6},{7,10},{11,14},{6,3},{... | collective-permute-start | bytes 786440 | tf_op jit(solution)/shard_map/ppermute | solution.py:300
  34.6 8.4 %collective-permute-start.2 = (f32[256,128]{1,0:T(8,128)S(1)}, f32[256,128]{1,0:T(8,128)S(1)}, u32[]{:S(2)}, u32[]{:S(2)}) collective-permute-start(f32[256,128]{1,0:T(8,128)S(1)} %pad_maximum_fusion), channel_id=1, source_target_pairs={{0,2},{2,0},{1,3},{3,1},{4,6},{6,4},{5,7},{7,5},{8,10},{10,8},{9,1... | collective-permute-start | bytes 393224 | tf_op jit(solution)/shard_map/ppermute | solution.py:308

commit v11 on v9

--- a/solution.py
+++ b/solution.py
@@ -256,7 +256,7 @@
         pltpu.make_async_copy(buffer.at[step], out_ref.at[step], sems.at[step]).start()
         return 0
 
-    lax.fori_loop(0, sizes, one_size, 0, unroll=2)
+    lax.fori_loop(0, sizes, one_size, 0, unroll=4)
 
     def finish(step, _):
         pltpu.make_async_copy(buffer.at[step], out_ref.at[step], sems.at[step]).wait()
@@ -343,7 +343,7 @@
     )(got)
     field = (sizes, block_rows, block_cols)
     return pl.pallas_call(
-        functools.partial(scan_kernel, 3),
+        functools.partial(scan_kernel, 1),
         in_specs=[scalars, whole, whole, whole],
         out_specs=pl.BlockSpec(memory_space=pltpu.HBM),
         scratch_shapes=[

time: 36.3 us -> 35.4 us (0.975)
  Pallas kernels: 18.8 us -> 18 us
    pallas_call x1, Pallas kernels: 10.4 us -> 9.59 us  [shards(): pl.pallas_call(functools.partial(scan_kernel, 1), in_specs=[scalars, whol...]
  transfers between devices with their start and end apart: 4 -> 4, of which waited for: 2 -> 2; matrix products, arithmetic and copies ran while one was open for 1% -> 1% of each run, Pallas kernels for 19% -> 20%
where the time goes in v11:
time: 35.4 us; the launch traced here: 35.2 us
  Pallas kernels  18 us (51%)
  starting transfers between devices  11.9 us (34%)
  waiting for transfers between devices  3.74 us (11%)
  other arithmetic  1.2 us (3%)
    pallas_call x1, Pallas kernels, shards(): pl.pallas_call(functools.partial(scan_kernel, 1), in_specs=[scalars, whol...  9.59 us
    all_to_all x1, starting transfers between devices, shards(): lax.all_to_all(sent, ('row', 'col', 'claim'), split_axis=0, concat_axis=0...  8.88 us
    pallas_call x1, Pallas kernels, shards(): pl.pallas_call(functools.partial(bin_kernel, sides), in_specs=[whole], ou...  5.45 us
    all_to_all x1, waiting for transfers between devices, shards(): lax.all_to_all(sent, ('row', 'col', 'claim'), split_axis=0, concat_axis=0...  2.71 us
    ppermute x1, starting transfers between devices, shards(): beside = lax.ppermute(edge, 'col', [(0, 1), (1, 0)])  1.93 us
    pallas_call x1, Pallas kernels, shards(): pl.pallas_call(functools.partial(pack_kernel, rows, cols, block_rows, blo...  1.5 us
    pallas_call x1, Pallas kernels, shards(): pl.pallas_call(base_kernel, in_specs=[scalars] + [whole] * 3, out_specs=[...  1.48 us
    select_n x1, other arithmetic, shards(): jnp.where(claim == 0, top, bottom)  1.08 us
  transfers between devices with their start and end apart: 4, of which 2 were waited for; matrix products, arithmetic and copies ran while one was open for 1% of the time, Pallas kernels for 20%

profile of v11, /device:TPU:0, one launch (start us, length us, event | category | flops | bytes accessed | tf_op | source)
XLA Modules:
  0.0 35.2 jit_solution(15185334181836892853)
XLA Ops:
  0.0 0.0 copy-start
  0.0 1.5 %shard_map.55 = f32[16,8,192]{2,1,0:T(8,128)} custom-call(s32[1,8,192]{2,1,0:T(8,128)} %cell_ref.1, f32[1,8,192]{2,1,0:T(8,128)} %weight_ref.1, s32[1,8]{1,0:T(1,128)} %count_ref.1), custom_call_target="tpu_custom_call" | custom-call | tf_op jit(solution)/shard_map/pallas_call | solution.py:275
  1.5 0.0 copy-start.1
  1.5 1.1 %slice_select_fusion = (f32[64,1024]{1,0:T(8,128)S(1)}, f32[64,1024]{1,0:T(8,128)S(1)}) fusion(f32[128,1024]{1,0:T(8,128)} %base_ref.1, pred[]{:T(512)S(6)} %eq.10), kind=kLoop, calls=%fused_computation | loop fusion | flops 131072 | bytes 1048577 | tf_op jit(solution)/shard_map/jit(_where)/select_n | solution.py:289
  2.6 0.7 %collective-permute-start.1 = (f32[64,1024]{1,0:T(8,128)S(1)}, f32[64,1024]{1,0:T(8,128)S(1)}, u32[]{:S(2)}, u32[]{:S(2)}) collective-permute-start(f32[64,1024]{1,0:T(8,128)S(1)} %get-tuple-element.19), channel_id=1, source_target_pairs={{1,4},{5,8},{9,12},{4,1},{8,5},{12,9},{3,6},{7,10},{11,14},{6,3},{... | collective-permute-start | bytes 786440 | tf_op jit(solution)/shard_map/ppermute | solution.py:289
  3.3 8.9 %all-to-all-start = ((f32[16,8,192]{2,1,0:T(8,128)}), f32[16,8,192]{2,1,0:T(8,128)S(1)}, u32[]{:S(2)}, u32[]{:S(2)}) async-start(f32[16,8,192]{2,1,0:T(8,128)} %shard_map.55), calls=%async_computation | async-start | bytes 262144 | tf_op jit(solution)/shard_map/all_to_all | solution.py:281
  12.2 0.4 %collective-permute-start = (f32[64,1024]{1,0:T(8,128)S(1)}, f32[64,1024]{1,0:T(8,128)S(1)}, u32[]{:S(2)}, u32[]{:S(2)}) collective-permute-start(f32[64,1024]{1,0:T(8,128)S(1)} %get-tuple-element.20), channel_id=1, source_target_pairs={{0,1},{1,0},{2,3},{3,2},{4,5},{5,4},{6,7},{7,6},{8,9},{9,8},{10,11... | collective-permute-start | bytes 786440 | tf_op jit(solution)/shard_map/ppermute | solution.py:288
  12.6 0.0 copy-done
  12.6 0.1 fusion
  12.7 0.0 collective-permute-done.1.outer_ref
  12.7 0.1 fusion.2
  12.7 1.0 %collective-permute-done.inner_ref = f32[64,1024]{1,0:T(8,128)S(1)} collective-permute-done((f32[64,1024]{1,0:T(8,128)S(1)}, f32[64,1024]{1,0:T(8,128)S(1)}, u32[]{:S(2)}, u32[]{:S(2)}) %collective-permute-start) | collective-permute-done | bytes 262176 | tf_op jit(solution)/shard_map/ppermute | solution.py:288
  13.8 0.1 fusion.1
  13.9 0.1 pad_maximum_fusion
  14.0 1.9 %collective-permute-start.2 = (f32[256,128]{1,0:T(8,128)S(1)}, f32[256,128]{1,0:T(8,128)S(1)}, u32[]{:S(2)}, u32[]{:S(2)}) collective-permute-start(f32[256,128]{1,0:T(8,128)S(1)} %pad_maximum_fusion), channel_id=1, source_target_pairs={{0,2},{2,0},{1,3},{3,1},{4,6},{6,4},{5,7},{7,5},{8,10},{10,8},{9,1... | collective-permute-start | bytes 393224 | tf_op jit(solution)/shard_map/ppermute | solution.py:296
  15.9 0.0 copy-done.1
  15.9 1.5 %shard_map.56 = (f32[9,264,128]{2,1,0:T(8,128)S(1)}, s32[16]{0:T(128)S(1)}) custom-call(s32[16]{0:T(128)S(1)} %copy-done.1, f32[128,1024]{1,0:T(8,128)S(1)} %copy-done, f32[64,1024]{1,0:T(8,128)S(1)} %collective-permute-done.inner_ref, f32[64,1024]{1,0:T(8,128)S(1)} %collective-permute-done.1.outer_ref), custom_call_target="tpu_custom_call" | custom-call | bytes 4194304 | tf_op jit(solution)/shard_map/pallas_call | solution.py:320
  17.4 2.7 %all-to-all-done.got_ref = f32[16,8,192]{2,1,0:T(8,128)S(1)} async-done(((f32[16,8,192]{2,1,0:T(8,128)}), f32[16,8,192]{2,1,0:T(8,128)S(1)}, u32[]{:S(2)}, u32[]{:S(2)}) %all-to-all-start) | async-done | bytes 98336 | tf_op jit(solution)/shard_map/all_to_all | solution.py:281
  20.1 5.4 %shard_map.57.counts_ref = f32[9,264,128]{2,1,0:T(8,128)S(1)} custom-call(f32[16,8,192]{2,1,0:T(8,128)S(1)} %all-to-all-done.got_ref), custom_call_target="tpu_custom_call" | custom-call | bytes 20971520 | tf_op jit(solution)/shard_map/pallas_call | solution.py:330
  25.6 0.0 collective-permute-done.2.beside_ref
  25.6 9.6 %shard_map.58 = f32[16,128,1024]{2,1,0:T(8,128)} custom-call(s32[16]{0:T(128)S(1)} %get-tuple-element.14.halves_ref, f32[9,264,128]{2,1,0:T(8,128)S(1)} %shard_map.57.counts_ref, f32[9,264,128]{2,1,0:T(8,128)S(1)} %get-tuple-element.16.prefix_ref, f32[256,128]{1,0:T(8,128)S(1)} %collective-permute-done.2.beside_ref), custom_call_target="tpu_custom_call" | custom-call | tf_op jit(solution)/shard_map/pallas_call | solution.py:345
  (1 shorter events, 0.0 us)
Async XLA Ops:
  0.0 12.6 %copy-start = (f32[128,1024]{1,0:T(8,128)S(1)}, f32[128,1024]{1,0:T(8,128)}, u32[]{:S(2)}) copy-start(f32[128,1024]{1,0:T(8,128)} %base_ref.1) | copy-start | bytes 1572868
  1.5 14.4 %copy-start.1 = (s32[16]{0:T(128)S(1)}, s32[16]{0:T(128)}, u32[]{:S(2)}) copy-start(s32[16]{0:T(128)} %halves_ref.1) | copy-start | bytes 196
  2.6 10.1 %collective-permute-start.1 = (f32[64,1024]{1,0:T(8,128)S(1)}, f32[64,1024]{1,0:T(8,128)S(1)}, u32[]{:S(2)}, u32[]{:S(2)}) collective-permute-start(f32[64,1024]{1,0:T(8,128)S(1)} %get-tuple-element.19), channel_id=1, source_target_pairs={{1,4},{5,8},{9,12},{4,1},{8,5},{12,9},{3,6},{7,10},{11,14},{6,3},{... | collective-permute-start | bytes 786440 | tf_op jit(solution)/shard_map/ppermute | solution.py:289
  3.3 16.8 %all-to-all-start = ((f32[16,8,192]{2,1,0:T(8,128)}), f32[16,8,192]{2,1,0:T(8,128)S(1)}, u32[]{:S(2)}, u32[]{:S(2)}) async-start(f32[16,8,192]{2,1,0:T(8,128)} %shard_map.55), calls=%async_computation | async-start | bytes 262144 | tf_op jit(solution)/shard_map/all_to_all | solution.py:281
  12.2 1.6 %collective-permute-start = (f32[64,1024]{1,0:T(8,128)S(1)}, f32[64,1024]{1,0:T(8,128)S(1)}, u32[]{:S(2)}, u32[]{:S(2)}) collective-permute-start(f32[64,1024]{1,0:T(8,128)S(1)} %get-tuple-element.20), channel_id=1, source_target_pairs={{0,1},{1,0},{2,3},{3,2},{4,5},{5,4},{6,7},{7,6},{8,9},{9,8},{10,11... | collective-permute-start | bytes 786440 | tf_op jit(solution)/shard_map/ppermute | solution.py:288
  14.0 11.6 %collective-permute-start.2 = (f32[256,128]{1,0:T(8,128)S(1)}, f32[256,128]{1,0:T(8,128)S(1)}, u32[]{:S(2)}, u32[]{:S(2)}) collective-permute-start(f32[256,128]{1,0:T(8,128)S(1)} %pad_maximum_fusion), channel_id=1, source_target_pairs={{0,2},{2,0},{1,3},{3,1},{4,6},{6,4},{5,7},{7,5},{8,10},{10,8},{9,1... | collective-permute-start | bytes 393224 | tf_op jit(solution)/shard_map/ppermute | solution.py:296

commit v12 on v11

--- a/solution.py
+++ b/solution.py
@@ -256,7 +256,7 @@
         pltpu.make_async_copy(buffer.at[step], out_ref.at[step], sems.at[step]).start()
         return 0
 
-    lax.fori_loop(0, sizes, one_size, 0, unroll=4)
+    lax.fori_loop(0, sizes, one_size, 0, unroll=8)
 
     def finish(step, _):
         pltpu.make_async_copy(buffer.at[step], out_ref.at[step], sems.at[step]).wait()

time: 35.4 us -> 35.2 us (level)
  no operation moved by 1% of the time
where the time goes in v12:
time: 35.2 us; the launch traced here: 35 us
  Pallas kernels  17.8 us (51%)
  starting transfers between devices  11.9 us (34%)
  waiting for transfers between devices  3.74 us (11%)
  other arithmetic  1.2 us (3%)
    pallas_call x1, Pallas kernels, shards(): pl.pallas_call(functools.partial(scan_kernel, 1), in_specs=[scalars, whol...  9.38 us
    all_to_all x1, starting transfers between devices, shards(): lax.all_to_all(sent, ('row', 'col', 'claim'), split_axis=0, concat_axis=0...  8.88 us
    pallas_call x1, Pallas kernels, shards(): pl.pallas_call(functools.partial(bin_kernel, sides), in_specs=[whole], ou...  5.45 us
    all_to_all x1, waiting for transfers between devices, shards(): lax.all_to_all(sent, ('row', 'col', 'claim'), split_axis=0, concat_axis=0...  2.71 us
    ppermute x1, starting transfers between devices, shards(): beside = lax.ppermute(edge, 'col', [(0, 1), (1, 0)])  1.93 us
    pallas_call x1, Pallas kernels, shards(): pl.pallas_call(functools.partial(pack_kernel, rows, cols, block_rows, blo...  1.5 us
    pallas_call x1, Pallas kernels, shards(): pl.pallas_call(base_kernel, in_specs=[scalars] + [whole] * 3, out_specs=[...  1.48 us
    select_n x1, other arithmetic, shards(): jnp.where(claim == 0, top, bottom)  1.08 us
  transfers between devices with their start and end apart: 4, of which 2 were waited for; matrix products, arithmetic and copies ran while one was open for 1% of the time, Pallas kernels for 20%

profile of v12, /device:TPU:0, one launch (start us, length us, event | category | flops | bytes accessed | tf_op | source)
XLA Modules:
  0.0 35.0 jit_solution(5337319315352682418)
XLA Ops:
  0.0 0.0 copy-start
  0.0 1.5 %shard_map.55 = f32[16,8,192]{2,1,0:T(8,128)} custom-call(s32[1,8,192]{2,1,0:T(8,128)} %cell_ref.1, f32[1,8,192]{2,1,0:T(8,128)} %weight_ref.1, s32[1,8]{1,0:T(1,128)} %count_ref.1), custom_call_target="tpu_custom_call" | custom-call | tf_op jit(solution)/shard_map/pallas_call | solution.py:275
  1.5 0.0 copy-start.1
  1.5 1.1 %slice_select_fusion = (f32[64,1024]{1,0:T(8,128)S(1)}, f32[64,1024]{1,0:T(8,128)S(1)}) fusion(f32[128,1024]{1,0:T(8,128)} %base_ref.1, pred[]{:T(512)S(6)} %eq.10), kind=kLoop, calls=%fused_computation | loop fusion | flops 131072 | bytes 1048577 | tf_op jit(solution)/shard_map/jit(_where)/select_n | solution.py:289
  2.6 0.7 %collective-permute-start.1 = (f32[64,1024]{1,0:T(8,128)S(1)}, f32[64,1024]{1,0:T(8,128)S(1)}, u32[]{:S(2)}, u32[]{:S(2)}) collective-permute-start(f32[64,1024]{1,0:T(8,128)S(1)} %get-tuple-element.19), channel_id=1, source_target_pairs={{1,4},{5,8},{9,12},{4,1},{8,5},{12,9},{3,6},{7,10},{11,14},{6,3},{... | collective-permute-start | bytes 786440 | tf_op jit(solution)/shard_map/ppermute | solution.py:289
  3.3 8.9 %all-to-all-start = ((f32[16,8,192]{2,1,0:T(8,128)}), f32[16,8,192]{2,1,0:T(8,128)S(1)}, u32[]{:S(2)}, u32[]{:S(2)}) async-start(f32[16,8,192]{2,1,0:T(8,128)} %shard_map.55), calls=%async_computation | async-start | bytes 262144 | tf_op jit(solution)/shard_map/all_to_all | solution.py:281
  12.2 0.4 %collective-permute-start = (f32[64,1024]{1,0:T(8,128)S(1)}, f32[64,1024]{1,0:T(8,128)S(1)}, u32[]{:S(2)}, u32[]{:S(2)}) collective-permute-start(f32[64,1024]{1,0:T(8,128)S(1)} %get-tuple-element.20), channel_id=1, source_target_pairs={{0,1},{1,0},{2,3},{3,2},{4,5},{5,4},{6,7},{7,6},{8,9},{9,8},{10,11... | collective-permute-start | bytes 786440 | tf_op jit(solution)/shard_map/ppermute | solution.py:288
  12.6 0.0 copy-done
  12.6 0.1 fusion
  12.7 0.0 collective-permute-done.1.outer_ref
  12.7 0.1 fusion.2
  12.7 1.0 %collective-permute-done.inner_ref = f32[64,1024]{1,0:T(8,128)S(1)} collective-permute-done((f32[64,1024]{1,0:T(8,128)S(1)}, f32[64,1024]{1,0:T(8,128)S(1)}, u32[]{:S(2)}, u32[]{:S(2)}) %collective-permute-start) | collective-permute-done | bytes 262176 | tf_op jit(solution)/shard_map/ppermute | solution.py:288
  13.8 0.1 fusion.1
  13.9 0.1 pad_maximum_fusion
  14.0 1.9 %collective-permute-start.2 = (f32[256,128]{1,0:T(8,128)S(1)}, f32[256,128]{1,0:T(8,128)S(1)}, u32[]{:S(2)}, u32[]{:S(2)}) collective-permute-start(f32[256,128]{1,0:T(8,128)S(1)} %pad_maximum_fusion), channel_id=1, source_target_pairs={{0,2},{2,0},{1,3},{3,1},{4,6},{6,4},{5,7},{7,5},{8,10},{10,8},{9,1... | collective-permute-start | bytes 393224 | tf_op jit(solution)/shard_map/ppermute | solution.py:296
  15.9 0.0 copy-done.1
  15.9 1.5 %shard_map.56 = (f32[9,264,128]{2,1,0:T(8,128)S(1)}, s32[16]{0:T(128)S(1)}) custom-call(s32[16]{0:T(128)S(1)} %copy-done.1, f32[128,1024]{1,0:T(8,128)S(1)} %copy-done, f32[64,1024]{1,0:T(8,128)S(1)} %collective-permute-done.inner_ref, f32[64,1024]{1,0:T(8,128)S(1)} %collective-permute-done.1.outer_ref), custom_call_target="tpu_custom_call" | custom-call | bytes 4194304 | tf_op jit(solution)/shard_map/pallas_call | solution.py:320
  17.4 2.7 %all-to-all-done.got_ref = f32[16,8,192]{2,1,0:T(8,128)S(1)} async-done(((f32[16,8,192]{2,1,0:T(8,128)}), f32[16,8,192]{2,1,0:T(8,128)S(1)}, u32[]{:S(2)}, u32[]{:S(2)}) %all-to-all-start) | async-done | bytes 98336 | tf_op jit(solution)/shard_map/all_to_all | solution.py:281
  20.1 5.4 %shard_map.57.counts_ref = f32[9,264,128]{2,1,0:T(8,128)S(1)} custom-call(f32[16,8,192]{2,1,0:T(8,128)S(1)} %all-to-all-done.got_ref), custom_call_target="tpu_custom_call" | custom-call | bytes 20971520 | tf_op jit(solution)/shard_map/pallas_call | solution.py:330
  25.6 0.0 collective-permute-done.2.beside_ref
  25.6 9.4 %shard_map.58 = f32[16,128,1024]{2,1,0:T(8,128)} custom-call(s32[16]{0:T(128)S(1)} %get-tuple-element.14.halves_ref, f32[9,264,128]{2,1,0:T(8,128)S(1)} %shard_map.57.counts_ref, f32[9,264,128]{2,1,0:T(8,128)S(1)} %get-tuple-element.16.prefix_ref, f32[256,128]{1,0:T(8,128)S(1)} %collective-permute-done.2.beside_ref), custom_call_target="tpu_custom_call" | custom-call | tf_op jit(solution)/shard_map/pallas_call | solution.py:345
  (1 shorter events, 0.0 us)
Async XLA Ops:
  0.0 12.6 %copy-start = (f32[128,1024]{1,0:T(8,128)S(1)}, f32[128,1024]{1,0:T(8,128)}, u32[]{:S(2)}) copy-start(f32[128,1024]{1,0:T(8,128)} %base_ref.1) | copy-start | bytes 1572868
  1.5 14.4 %copy-start.1 = (s32[16]{0:T(128)S(1)}, s32[16]{0:T(128)}, u32[]{:S(2)}) copy-start(s32[16]{0:T(128)} %halves_ref.1) | copy-start | bytes 196
  2.6 10.1 %collective-permute-start.1 = (f32[64,1024]{1,0:T(8,128)S(1)}, f32[64,1024]{1,0:T(8,128)S(1)}, u32[]{:S(2)}, u32[]{:S(2)}) collective-permute-start(f32[64,1024]{1,0:T(8,128)S(1)} %get-tuple-element.19), channel_id=1, source_target_pairs={{1,4},{5,8},{9,12},{4,1},{8,5},{12,9},{3,6},{7,10},{11,14},{6,3},{... | collective-permute-start | bytes 786440 | tf_op jit(solution)/shard_map/ppermute | solution.py:289
  3.3 16.8 %all-to-all-start = ((f32[16,8,192]{2,1,0:T(8,128)}), f32[16,8,192]{2,1,0:T(8,128)S(1)}, u32[]{:S(2)}, u32[]{:S(2)}) async-start(f32[16,8,192]{2,1,0:T(8,128)} %shard_map.55), calls=%async_computation | async-start | bytes 262144 | tf_op jit(solution)/shard_map/all_to_all | solution.py:281
  12.2 1.6 %collective-permute-start = (f32[64,1024]{1,0:T(8,128)S(1)}, f32[64,1024]{1,0:T(8,128)S(1)}, u32[]{:S(2)}, u32[]{:S(2)}) collective-permute-start(f32[64,1024]{1,0:T(8,128)S(1)} %get-tuple-element.20), channel_id=1, source_target_pairs={{0,1},{1,0},{2,3},{3,2},{4,5},{5,4},{6,7},{7,6},{8,9},{9,8},{10,11... | collective-permute-start | bytes 786440 | tf_op jit(solution)/shard_map/ppermute | solution.py:288
  14.0 11.6 %collective-permute-start.2 = (f32[256,128]{1,0:T(8,128)S(1)}, f32[256,128]{1,0:T(8,128)S(1)}, u32[]{:S(2)}, u32[]{:S(2)}) collective-permute-start(f32[256,128]{1,0:T(8,128)S(1)} %pad_maximum_fusion), channel_id=1, source_target_pairs={{0,2},{2,0},{1,3},{3,1},{4,6},{6,4},{5,7},{7,5},{8,10},{10,8},{9,1... | collective-permute-start | bytes 393224 | tf_op jit(solution)/shard_map/ppermute | solution.py:296
